TPU v7x, 256 devices: a whole 4x4x8 slice. The times are simulated.
256 devices in a mesh: head: 16 (over z, core), seq: 16 (over x, y).
Axes of the slice: x: 4, y: 4, z: 8, core: 2. Of those that a mesh axis runs over, the one named last changes fastest.
Arguments:
- queries: bfloat16 [8192, 2048], P(('seq', 'head')), may hold values from -6 to 6
- key_vectors: bfloat16 [8192, 2048], P(('seq', 'head')), may hold values from -6 to 6
- value_vectors: bfloat16 [8192, 2048], P(('seq', 'head')), may hold values from -6 to 6
- out_grad: bfloat16 [8192, 2048], P(('seq', 'head')), may hold values from -6 to 6
- key_tiles: int32 [16, 64, 38], replicated, may hold values from 0 to 63, as said below
- tile_count: int32 [16, 64], replicated, may hold values from 4 to 38, as said below
Outputs:
- attended: bfloat16 [8192, 2048], P(('seq', 'head'))
- grad_queries: bfloat16 [8192, 2048], P(('seq', 'head'))
- grad_keys: bfloat16 [8192, 2048], P(('seq', 'head'))
- grad_values: bfloat16 [8192, 2048], P(('seq', 'head'))
Inputs may be any that keep to these rules, and one draw needn't show every extreme that they name: key_tiles[h, i, 0] is i; the 38 entries of one list are distinct; only the first tile_count[h, i] entries are active. `tile_count`: each list covers 5 to 60 percent of the clip's tiles; the value 38 is taken in every draw.
All inputs are finite; a program needn't handle non-finite values.
Results may differ from a plain program's by a relative error of at most 0.029.
Values may be sent and summed in bfloat16 or wider, within the bound.
No kernel may reach another device: no remote copies, remote signals or barrier semaphores. Data moves between devices by JAX's collectives and lax.ppermute only.
A program may use at most 128 MiB of HBM per device.

v0:
```python
import math

import jax
import jax.numpy as jnp
from jax import lax
from jax.sharding import PartitionSpec as P

DH = 128
TILE = 128
GROUP = 8


masked_score = -1e30
lane_count = 4


def tile_graph(key_tiles, tile_count):
    head_total, block_total, slot_total = key_tiles.shape
    live = (jnp.arange(slot_total, dtype=jnp.int32)[None, None, :] < tile_count[:, :, None]).astype(
        jnp.int32
    )
    head_ids = jnp.broadcast_to(
        jnp.arange(head_total, dtype=jnp.int32)[:, None, None], key_tiles.shape
    )
    row_ids = jnp.broadcast_to(
        jnp.arange(block_total, dtype=jnp.int32)[None, :, None], key_tiles.shape
    )
    empty = jnp.zeros((head_total, block_total, block_total), jnp.int32)
    return empty.at[head_ids, row_ids, key_tiles].max(live)


def to_tiles(row_data, head_local, tile_rows):
    row_total, column_total = row_data.shape
    head_width = column_total // head_local
    shaped = row_data.reshape(row_total // tile_rows, tile_rows, head_local, head_width)
    return shaped.transpose(2, 0, 1, 3).reshape(-1, tile_rows, head_width)


def from_tiles(tile_data, head_local):
    tile_total, tile_rows, head_width = tile_data.shape
    shaped = tile_data.reshape(head_local, tile_total // head_local, tile_rows, head_width)
    return shaped.transpose(1, 2, 0, 3).reshape(-1, head_local * head_width)


def column_lists(adjacency):
    row_total, col_total = adjacency.shape
    ranking = jnp.argsort(
        (1 - adjacency) * col_total + jnp.arange(col_total, dtype=jnp.int32)[None, :], axis=1
    )
    group_total = -(-col_total // GROUP)
    return (ranking, jnp.sum(adjacency, axis=1), group_total)


def pair_plan(live_count, group_total):
    row_total = live_count.shape[0]
    pair_total = row_total * group_total
    item_of = jnp.repeat(jnp.arange(row_total, dtype=jnp.int32), group_total)
    group_of = jnp.tile(jnp.arange(group_total, dtype=jnp.int32), row_total)
    pair_used = group_of * GROUP < live_count[item_of]
    ranking = jnp.argsort(
        jnp.where(pair_used, 0, pair_total) + jnp.arange(pair_total, dtype=jnp.int32)
    )
    item_of = item_of[ranking]
    group_of = group_of[ranking]
    pair_used = pair_used[ranking]
    turn_total = (jnp.sum(pair_used.astype(jnp.int32)) + lane_count - 1) // lane_count
    return (item_of, group_of, pair_used, turn_total)


def batch_at(pair_table, ranking, live_count, turn_at):
    item_of, group_of, pair_used, turn_total = pair_table
    first_pair = turn_at * lane_count
    item_ids = lax.dynamic_slice_in_dim(item_of, first_pair, lane_count)
    group_ids = lax.dynamic_slice_in_dim(group_of, first_pair, lane_count)
    used_now = lax.dynamic_slice_in_dim(pair_used, first_pair, lane_count)
    offsets = group_ids[:, None] * GROUP + jnp.arange(GROUP, dtype=jnp.int32)[None, :]
    columns = jnp.take_along_axis(ranking[item_ids], offsets, axis=1)
    slot_live = used_now[:, None] & (offsets < live_count[item_ids][:, None])
    return (item_ids, columns, slot_live)


def query_passes(work_query, work_grad, work_head, work_block, tile_mask, key_all, value_all):
    row_total, tile_rows, head_width = work_query.shape
    block_total = tile_mask.shape[1]
    inv_root = 1.0 / math.sqrt(head_width)
    ranking, live_count, group_total = column_lists(tile_mask[work_head, work_block])
    pair_table = pair_plan(live_count, group_total)
    item_of = pair_table[0]
    turn_total = pair_table[3]
    slot_total = item_of.shape[0]

    def fetch(turn_at):
        item_ids, columns, slot_live = batch_at(pair_table, ranking, live_count, turn_at)
        tile_ids = work_head[item_ids][:, None] * block_total + columns
        keep_mask = jnp.repeat(slot_live, tile_rows, axis=1)[:, None, :]
        key_tile = key_all[tile_ids].reshape(lane_count, GROUP * tile_rows, head_width)
        value_tile = value_all[tile_ids].reshape(lane_count, GROUP * tile_rows, head_width)
        scores = (
            jnp.einsum(
                "rqd,rkd->rqk", work_query[item_ids], key_tile, preferred_element_type=jnp.float32
            )
            * inv_root
        )
        return (item_ids, tile_ids, keep_mask, key_tile, value_tile, scores)

    def stats_step(turn_at, running):
        top_store, mass_store = running
        item_ids, tile_ids, keep_mask, key_tile, value_tile, scores = fetch(turn_at)
        masked = jnp.where(keep_mask, scores, masked_score)
        row_top = jnp.max(masked, axis=2)
        row_mass = jnp.sum(jnp.where(keep_mask, jnp.exp(masked - row_top[:, :, None]), 0.0), axis=2)
        top_store = lax.dynamic_update_slice_in_dim(top_store, row_top, turn_at * lane_count, 0)
        mass_store = lax.dynamic_update_slice_in_dim(mass_store, row_mass, turn_at * lane_count, 0)
        return (top_store, mass_store)

    stats_init = (
        jnp.full((slot_total, tile_rows), masked_score, jnp.float32),
        jnp.zeros((slot_total, tile_rows), jnp.float32),
    )
    top_store, mass_store = lax.fori_loop(0, turn_total, stats_step, stats_init)
    row_top = jnp.full((row_total, tile_rows), masked_score, jnp.float32).at[item_of].max(top_store)
    row_mass = (
        jnp.zeros((row_total, tile_rows), jnp.float32)
        .at[item_of]
        .add(mass_store * jnp.exp(top_store - row_top[item_of]))
    )
    row_lse = row_top + jnp.log(row_mass)

    def output_step(turn_at, attended):
        item_ids, tile_ids, keep_mask, key_tile, value_tile, scores = fetch(turn_at)
        weights = jnp.exp(
            jnp.where(keep_mask, scores - row_lse[item_ids][:, :, None], masked_score)
        )
        update = jnp.einsum(
            "rqk,rkd->rqd",
            weights.astype(jnp.bfloat16),
            value_tile,
            preferred_element_type=jnp.float32,
        )
        return attended.at[item_ids].add(update)

    zero_rows = jnp.zeros((row_total, tile_rows, head_width), jnp.float32)
    attended = lax.fori_loop(0, turn_total, output_step, zero_rows).astype(jnp.bfloat16)
    row_delta = jnp.sum(work_grad.astype(jnp.float32) * attended.astype(jnp.float32), axis=2)

    def grad_step(turn_at, running):
        item_ids, tile_ids, keep_mask, key_tile, value_tile, scores = fetch(turn_at)
        weights = jnp.exp(
            jnp.where(keep_mask, scores - row_lse[item_ids][:, :, None], masked_score)
        )
        grad_rows = work_grad[item_ids]
        dprobs = jnp.einsum(
            "rqd,rkd->rqk", grad_rows, value_tile, preferred_element_type=jnp.float32
        )
        dscores = (weights * (dprobs - row_delta[item_ids][:, :, None]) * inv_root).astype(
            jnp.bfloat16
        )
        query_grad = (
            running[0]
            .at[item_ids]
            .add(jnp.einsum("rqk,rkd->rqd", dscores, key_tile, preferred_element_type=jnp.float32))
        )
        flat_ids = tile_ids.reshape(-1)
        key_part = jnp.einsum(
            "rqk,rqd->rkd", dscores, work_query[item_ids], preferred_element_type=jnp.float32
        )
        value_part = jnp.einsum(
            "rqk,rqd->rkd",
            weights.astype(jnp.bfloat16),
            grad_rows,
            preferred_element_type=jnp.float32,
        )
        key_grad = running[1].at[flat_ids].add(key_part.reshape(-1, tile_rows, head_width))
        value_grad = running[2].at[flat_ids].add(value_part.reshape(-1, tile_rows, head_width))
        return (query_grad, key_grad, value_grad)

    zero_keys = jnp.zeros(key_all.shape, jnp.float32)
    query_grad, key_grad, value_grad = lax.fori_loop(
        0, turn_total, grad_step, (zero_rows, zero_keys, zero_keys)
    )
    return (attended, row_lse, row_delta, query_grad.astype(jnp.bfloat16), key_grad, value_grad)


def per_device(queries, key_vectors, value_vectors, out_grad, key_tiles, tile_count):
    head_at = lax.axis_index("head")
    seq_at = lax.axis_index("seq")
    local_query, local_key, local_value, local_grad = (
        lax.all_to_all(queries, "head", split_axis=1, concat_axis=0, tiled=True),
        lax.all_to_all(key_vectors, "head", split_axis=1, concat_axis=0, tiled=True),
        lax.all_to_all(value_vectors, "head", split_axis=1, concat_axis=0, tiled=True),
        lax.all_to_all(out_grad, "head", split_axis=1, concat_axis=0, tiled=True),
    )
    row_total = local_query.shape[0]
    head_local = local_query.shape[1] // DH
    block_span = row_total // TILE
    item_total = head_local * block_span
    every_key, every_value = (
        lax.all_gather(local_key, "seq", axis=0, tiled=True),
        lax.all_gather(local_value, "seq", axis=0, tiled=True),
    )
    key_all = to_tiles(every_key, head_local, TILE)
    value_all = to_tiles(every_value, head_local, TILE)
    own_query = to_tiles(local_query, head_local, TILE)
    own_grad = to_tiles(local_grad, head_local, TILE)
    heads_here = lax.dynamic_slice_in_dim(key_tiles, head_at * head_local, head_local, 0)
    counts_here = lax.dynamic_slice_in_dim(tile_count, head_at * head_local, head_local, 0)
    tile_mask = tile_graph(heads_here, counts_here)
    item_head = jnp.repeat(jnp.arange(head_local, dtype=jnp.int32), block_span)
    item_step = jnp.tile(jnp.arange(block_span, dtype=jnp.int32), head_local)
    work_owner = jnp.full((item_total,), seq_at, jnp.int32)
    work_item = jnp.arange(item_total, dtype=jnp.int32)
    work_head = item_head[work_item]
    work_block = work_owner * block_span + item_step[work_item]
    attended, row_lse, row_delta, query_grad, key_grad, value_grad = query_passes(
        own_query, own_grad, work_head, work_block, tile_mask, key_all, value_all
    )
    key_sum, value_sum = (
        lax.psum_scatter(from_tiles(key_grad, head_local), "seq", scatter_dimension=0, tiled=True),
        lax.psum_scatter(
            from_tiles(value_grad, head_local), "seq", scatter_dimension=0, tiled=True
        ),
    )
    key_out = key_sum.astype(jnp.bfloat16)
    value_out = value_sum.astype(jnp.bfloat16)
    return (
        lax.all_to_all(
            from_tiles(attended, head_local), "head", split_axis=0, concat_axis=1, tiled=True
        ),
        lax.all_to_all(
            from_tiles(query_grad, head_local), "head", split_axis=0, concat_axis=1, tiled=True
        ),
        lax.all_to_all(key_out, "head", split_axis=0, concat_axis=1, tiled=True),
        lax.all_to_all(value_out, "head", split_axis=0, concat_axis=1, tiled=True),
    )


def solution(mesh):
    in_specs = (
        P(("seq", "head"), None),
        P(("seq", "head"), None),
        P(("seq", "head"), None),
        P(("seq", "head"), None),
        P(),
        P(),
    )
    out_specs = (
        P(("seq", "head"), None),
        P(("seq", "head"), None),
        P(("seq", "head"), None),
        P(("seq", "head"), None),
    )
    return jax.shard_map(
        per_device, mesh=mesh, in_specs=in_specs, out_specs=out_specs, check_vma=False
    )
```

profile of v0, /device:TPU:1, one launch (start us, length us, event | category | flops | bytes accessed | tf_op | source)
XLA Modules:
  0.0 580.0 jit_solution(16064074868427668099)
XLA Ops:
  8.1 19.0 %all_to_all.146 = bf16[32,16,128]{2,0,1:T(8,128)(2,1)} all-to-all(bf16[32,16,128]{2,0,1:T(8,128)(2,1)S(1)} %copy_bitcast_fusion.9), channel_id=1, replica_groups=mesh['head'=16,'seq'=16] {'head'}, dimensions={1} | all-to-all | bytes 262144 | tf_op jit(solution)/shard_map/all_to_all | solution.py:189
  28.8 3.5 all-to-all-start.2
  36.4 18.0 %scatter_custom_fusion.6 = s32[4096]{0:T(1024)S(1)} fusion(s32[2432]{0:T(1024)S(1)} %reshape.588, s32[2432]{0:T(1024)S(1)} %reshape.590, s32[]{:T(128)} %constant.74.clone.1), kind=kCustom, calls=%fused_computation.129 | custom fusion | flops 2432 | bytes 16388
  55.9 2.6 iota_add_fusion.4
  64.6 6.8 %all-to-all-start = ((bf16[32,16,128]{2,0,1:T(8,128)(2,1)}), bf16[32,16,128]{2,0,1:T(8,128)(2,1)S(1)}, u32[]{:S(2)}, u32[]{:S(2)}) async-start(bf16[32,16,128]{2,0,1:T(8,128)(2,1)} %copy_bitcast_fusion.10), calls=%async_computation | async-start | bytes 262144 | tf_op jit(solution)/shard_map/all_to_all | solution.py:188
  76.6 4.0 all-to-all-done
  80.5 4.1 all-to-all-start.4
  85.9 46.2 %while.36 = (s32[]{:T(128)}, f32[32,128]{1,0:T(8,128)}, f32[32,128]{1,0:T(8,128)}, s32[]{:T(128)}, pred[32]{0:T(512)(128)(4,1)}, /*index=5*/s32[32]{0:T(128)}, s...) while((s32[]{:T(128)}, f32[32,128]{1,0:T(8,128)}, ...), condition=%wide.region_8.10_spmd, body=%wide.region_5.9_spmd.sunk | while | flops 138413856 | bytes 16169467 | solution.py:120
  134.9 67.8 %while.37 = (s32[]{:T(128)}, f32[4,128,128]{2,1,0:T(8,128)}, s32[]{:T(128)}, s32[32]{0:T(128)}, pred[32]{0:T(512)(128)(4,1)}, /*index=5*/s32[32]{0:T(128)}, s32[...) while((s32[]{:T(128)}, f32[4,128,128]{2,1,0:T(8,128)}, ...), condition=%wide.region_13.15_spmd, body=%wide.region_11.14_spmd.sunk | while | flops 270600992 | bytes 18279364 | solution.py:143
  143.5 2.5 gather_fusion.9
  157.1 2.5 gather_fusion.9
  170.6 2.5 gather_fusion.9
  184.2 2.5 gather_fusion.9
  197.8 2.5 gather_fusion.9
  202.7 2.3 multiply_reduce_fusion
  205.7 2.5 broadcast_in_dim.184.clone
  208.2 2.4 broadcast_in_dim.184
  210.6 174.3 %while.38 = (s32[]{:T(128)}, f32[4,128,128]{2,1,0:T(8,128)}, f32[64,128,128]{2,1,0:T(8,128)}, f32[64,128,128]{2,1,0:T(8,128)}, s32[]{:T(128)}, /*index=5*/s32[32...) while((s32[]{:T(128)}, f32[4,128,128]{2,1,0:T(8,128)}, ...), condition=%wide.region_19.21_spmd, body=%wide.region_15.20_spmd.sunk | while | flops 676400000 | bytes 46713248 | solution.py:178
  218.3 2.1 gather_fusion.21
  221.0 2.3 gather_fusion.22
  223.3 2.3 gather_fusion.18
  232.0 7.2 %scatter_fusion.2 = f32[64,128,128]{2,1,0:T(8,128)} fusion(f32[64,128,128]{2,1,0:T(8,128)} %get-tuple-element.911, s32[32]{0:T(128)S(1)} %copy-done.19, f32[32,128,128]{2,1,0:T(8,128)} %bitcast.207), kind=kCustom, calls=%fused_computation.33.clone.1 | custom fusion | flops 524288 | bytes 6291584 | tf_op jit(solution)/shard_map/while/body/scatter-add | solution.py:173
  239.2 6.3 %scatter_fusion.3 = f32[64,128,128]{2,1,0:T(8,128)} fusion(f32[64,128,128]{2,1,0:T(8,128)} %get-tuple-element.912, s32[32]{0:T(128)S(1)} %copy-done.19, f32[32,128,128]{2,1,0:T(8,128)S(1)} %bitcast.206), kind=kCustom, calls=%fused_computation.34.clone.1 | custom fusion | flops 524288 | bytes 6291584 | tf_op jit(solution)/shard_map/while/body/scatter-add | solution.py:174
  253.2 2.1 gather_fusion.21
  255.9 2.3 gather_fusion.22
  258.2 2.3 gather_fusion.18
  266.9 7.2 %scatter_fusion.2 = f32[64,128,128]{2,1,0:T(8,128)} fusion(f32[64,128,128]{2,1,0:T(8,128)} %get-tuple-element.911, s32[32]{0:T(128)S(1)} %copy-done.19, f32[32,128,128]{2,1,0:T(8,128)} %bitcast.207), kind=kCustom, calls=%fused_computation.33.clone.1 | custom fusion | flops 524288 | bytes 6291584 | tf_op jit(solution)/shard_map/while/body/scatter-add | solution.py:173
  274.1 6.3 %scatter_fusion.3 = f32[64,128,128]{2,1,0:T(8,128)} fusion(f32[64,128,128]{2,1,0:T(8,128)} %get-tuple-element.912, s32[32]{0:T(128)S(1)} %copy-done.19, f32[32,128,128]{2,1,0:T(8,128)S(1)} %bitcast.206), kind=kCustom, calls=%fused_computation.34.clone.1 | custom fusion | flops 524288 | bytes 6291584 | tf_op jit(solution)/shard_map/while/body/scatter-add | solution.py:174
  290.7 2.3 gather_fusion.22
  293.1 2.3 gather_fusion.18
  301.8 7.2 %scatter_fusion.2 = f32[64,128,128]{2,1,0:T(8,128)} fusion(f32[64,128,128]{2,1,0:T(8,128)} %get-tuple-element.911, s32[32]{0:T(128)S(1)} %copy-done.19, f32[32,128,128]{2,1,0:T(8,128)} %bitcast.207), kind=kCustom, calls=%fused_computation.33.clone.1 | custom fusion | flops 524288 | bytes 6291584 | tf_op jit(solution)/shard_map/while/body/scatter-add | solution.py:173
  309.0 6.3 %scatter_fusion.3 = f32[64,128,128]{2,1,0:T(8,128)} fusion(f32[64,128,128]{2,1,0:T(8,128)} %get-tuple-element.912, s32[32]{0:T(128)S(1)} %copy-done.19, f32[32,128,128]{2,1,0:T(8,128)S(1)} %bitcast.206), kind=kCustom, calls=%fused_computation.34.clone.1 | custom fusion | flops 524288 | bytes 6291584 | tf_op jit(solution)/shard_map/while/body/scatter-add | solution.py:174
  325.6 2.3 gather_fusion.22
  328.0 2.3 gather_fusion.18
  336.7 7.2 %scatter_fusion.2 = f32[64,128,128]{2,1,0:T(8,128)} fusion(f32[64,128,128]{2,1,0:T(8,128)} %get-tuple-element.911, s32[32]{0:T(128)S(1)} %copy-done.19, f32[32,128,128]{2,1,0:T(8,128)} %bitcast.207), kind=kCustom, calls=%fused_computation.33.clone.1 | custom fusion | flops 524288 | bytes 6291584 | tf_op jit(solution)/shard_map/while/body/scatter-add | solution.py:173
  343.9 6.3 %scatter_fusion.3 = f32[64,128,128]{2,1,0:T(8,128)} fusion(f32[64,128,128]{2,1,0:T(8,128)} %get-tuple-element.912, s32[32]{0:T(128)S(1)} %copy-done.19, f32[32,128,128]{2,1,0:T(8,128)S(1)} %bitcast.206), kind=kCustom, calls=%fused_computation.34.clone.1 | custom fusion | flops 524288 | bytes 6291584 | tf_op jit(solution)/shard_map/while/body/scatter-add | solution.py:174
  360.5 2.3 gather_fusion.22
  362.8 2.3 gather_fusion.18
  371.5 7.2 %scatter_fusion.2 = f32[64,128,128]{2,1,0:T(8,128)} fusion(f32[64,128,128]{2,1,0:T(8,128)} %get-tuple-element.911, s32[32]{0:T(128)S(1)} %copy-done.19, f32[32,128,128]{2,1,0:T(8,128)} %bitcast.207), kind=kCustom, calls=%fused_computation.33.clone.1 | custom fusion | flops 524288 | bytes 6291584 | tf_op jit(solution)/shard_map/while/body/scatter-add | solution.py:173
  378.7 6.2 %scatter_fusion.3 = f32[64,128,128]{2,1,0:T(8,128)} fusion(f32[64,128,128]{2,1,0:T(8,128)} %get-tuple-element.912, s32[32]{0:T(128)S(1)} %copy-done.19, f32[32,128,128]{2,1,0:T(8,128)S(1)} %bitcast.206), kind=kCustom, calls=%fused_computation.34.clone.1 | custom fusion | flops 524288 | bytes 6291584 | tf_op jit(solution)/shard_map/while/body/scatter-add | solution.py:174
  385.5 6.6 %all-to-all-start.3 = ((bf16[16,32,128]{2,1,0:T(8,128)(2,1)}), bf16[16,32,128]{2,1,0:T(8,128)(2,1)S(1)}, u32[]{:S(2)}, u32[]{:S(2)}) async-start(bf16[16,32,128]{2,1,0:T(8,128)(2,1)} %bitcast.32), calls=%async_computation.3 | async-start | bytes 262144 | tf_op jit(solution)/shard_map/all_to_all | solution.py:226
  392.8 8.5 %all-to-all-done.3 = bf16[16,32,128]{2,1,0:T(8,128)(2,1)S(1)} async-done(((bf16[16,32,128]{2,1,0:T(8,128)(2,1)}), bf16[16,32,128]{2,1,0:T(8,128)(2,1)S(1)}, u32[]{:S(2)}, u32[]{:S(2)}) %all-to-all-start.3) | async-done | bytes 131104 | tf_op jit(solution)/shard_map/all_to_all | solution.py:226
  401.3 3.4 all-to-all-start.5
  405.4 61.3 %reduce-scatter.3.cloned.1.call-done = f32[512,128]{1,0:T(8,128)} async-done(((f32[8192,128]{1,0:T(8,128)}), f32[512,128]{1,0:T(8,128)}) %reduce-scatter.3.cloned.1.call-update) | async-done | bytes 262160 | tf_op jit(solution)/shard_map/reduce_scatter | solution.py:218
  468.3 9.4 %all-to-all-start.6 = ((bf16[16,32,128]{2,1,0:T(8,128)(2,1)}), bf16[16,32,128]{2,1,0:T(8,128)(2,1)S(1)}, u32[]{:S(2)}, u32[]{:S(2)}) async-start(bf16[16,32,128]{2,1,0:T(8,128)(2,1)} %bitcast.40), calls=%async_computation.7 | async-start | bytes 262144 | tf_op jit(solution)/shard_map/all_to_all | solution.py:232
  478.4 74.2 %reduce-scatter.5.cloned.1.call-done = f32[512,128]{1,0:T(8,128)} async-done(((f32[8192,128]{1,0:T(8,128)}), f32[512,128]{1,0:T(8,128)}) %reduce-scatter.5.cloned.1.call-update) | async-done | bytes 262160 | tf_op jit(solution)/shard_map/reduce_scatter | solution.py:219
  554.2 9.3 %all-to-all-start.7 = ((bf16[16,32,128]{2,1,0:T(8,128)(2,1)}), bf16[16,32,128]{2,1,0:T(8,128)(2,1)S(1)}, u32[]{:S(2)}, u32[]{:S(2)}) async-start(bf16[16,32,128]{2,1,0:T(8,128)(2,1)} %bitcast.43), calls=%async_computation.9 | async-start | bytes 262144 | tf_op jit(solution)/shard_map/all_to_all | solution.py:233
  564.2 8.5 %all-to-all-done.7 = bf16[16,32,128]{2,1,0:T(8,128)(2,1)S(1)} async-done(((bf16[16,32,128]{2,1,0:T(8,128)(2,1)}), bf16[16,32,128]{2,1,0:T(8,128)(2,1)S(1)}, u32[]{:S(2)}, u32[]{:S(2)}) %all-to-all-start.7) | async-done | bytes 131104 | tf_op jit(solution)/shard_map/all_to_all | solution.py:233
  (618 shorter events, 210.1 us)
Async XLA Ops:
  7.2 28.6 %copy-start.22 = (s32[3]{0:T(128)S(1)}, s32[3]{0:T(128)}, u32[]{:S(2)}) copy-start(s32[3]{0:T(128)} %constant.97) | copy-start | bytes 40
  7.2 28.8 %copy-start.21 = (s32[3]{0:T(128)S(1)}, s32[3]{0:T(128)}, u32[]{:S(2)}) copy-start(s32[3]{0:T(128)} %constant.100) | copy-start | bytes 40
  7.2 56.7 %copy-start.12 = (bf16[32,2048]{1,0:T(8,128)(2,1)S(1)}, bf16[32,2048]{1,0:T(8,128)(2,1)}, u32[]{:S(2)}) copy-start(bf16[32,2048]{1,0:T(8,128)(2,1)} %param.14) | copy-start | bytes 393220
  7.2 77.5 %all-gather.3.cloned.1.call-start = ((), (), s32[]{:S(2)}) async-start(), calls=%async_computation.10 | async-start | bytes 2228224 | tf_op jit(solution)/shard_map/all_gather | solution.py:198
  28.8 47.1 %copy-start.13 = (bf16[32,2048]{1,0:T(8,128)(2,1)S(1)}, bf16[32,2048]{1,0:T(8,128)(2,1)}, u32[]{:S(2)}) copy-start(bf16[32,2048]{1,0:T(8,128)(2,1)} %param.17) | copy-start | bytes 393220
  28.8 35.8 %all-to-all-start.2 = ((bf16[32,16,128]{2,0,1:T(8,128)(2,1)}), bf16[32,16,128]{2,0,1:T(8,128)(2,1)S(1)}, u32[]{:S(2)}, u32[]{:S(2)}) async-start(bf16[32,16,128]{2,0,1:T(8,128)(2,1)} %copy_bitcast_fusion.8), calls=%async_computation.2 | async-start | bytes 262144 | tf_op jit(solution)/shard_map/all_to_all | solution.py:190
  62.0 23.9 %copy-start.23 = (s32[32]{0:T(128)}, s32[32]{0:T(128)S(1)}, u32[]{:S(2)}) copy-start(s32[32]{0:T(128)S(1)} %fusion.44) | copy-start | bytes 388
  64.6 12.0 %copy-start.10 = (bf16[32,16,128]{2,0,1:T(8,128)(2,1)}, bf16[32,16,128]{2,0,1:T(8,128)(2,1)S(1)}, u32[]{:S(2)}) copy-start(bf16[32,16,128]{2,0,1:T(8,128)(2,1)S(1)} %all-to-all-done.2) | copy-start | bytes 393220
  64.6 16.0 %all-to-all-start = ((bf16[32,16,128]{2,0,1:T(8,128)(2,1)}), bf16[32,16,128]{2,0,1:T(8,128)(2,1)S(1)}, u32[]{:S(2)}, u32[]{:S(2)}) async-start(bf16[32,16,128]{2,0,1:T(8,128)(2,1)} %copy_bitcast_fusion.10), calls=%async_computation | async-start | bytes 262144 | tf_op jit(solution)/shard_map/all_to_all | solution.py:188
  71.4 62.8 %all-gather.5.cloned.1.call-start = ((), (), s32[]{:S(2)}) async-start(), calls=%async_computation.11 | async-start | bytes 2228224 | tf_op jit(solution)/shard_map/all_gather | solution.py:199
  80.5 122.1 %all-to-all-start.4 = ((bf16[32,16,128]{2,0,1:T(8,128)(2,1)}), bf16[32,16,128]{2,0,1:T(8,128)(2,1)}, u32[]{:S(2)}, u32[]{:S(2)}) async-start(bf16[32,16,128]{2,0,1:T(8,128)(2,1)} %copy_bitcast_fusion.7), calls=%async_computation.4 | async-start | bytes 262144 | tf_op jit(solution)/shard_map/all_to_all | solution.py:191
  84.6 382.1 %reduce-scatter.3.cloned.1.call-start = ((), (), s32[]{:S(2)}) async-start(), calls=%async_computation.12 | async-start | bytes 4456448 | tf_op jit(solution)/shard_map/reduce_scatter | solution.py:218
  85.9 6.0 %copy-start.2 = (bf16[64,128,128]{2,1,0:T(8,128)(2,1)S(1)}, bf16[64,128,128]{2,1,0:T(8,128)(2,1)}, u32[]{:S(2)}) copy-start(bf16[64,128,128]{2,1,0:T(8,128)(2,1)} %get-tuple-element.832) | copy-start | bytes 6291460 | tf_op jit(solution)/shard_map/while
  95.2 6.0 %copy-start.2 = (bf16[64,128,128]{2,1,0:T(8,128)(2,1)S(1)}, bf16[64,128,128]{2,1,0:T(8,128)(2,1)}, u32[]{:S(2)}) copy-start(bf16[64,128,128]{2,1,0:T(8,128)(2,1)} %get-tuple-element.832) | copy-start | bytes 6291460 | tf_op jit(solution)/shard_map/while
  104.4 6.0 %copy-start.2 = (bf16[64,128,128]{2,1,0:T(8,128)(2,1)S(1)}, bf16[64,128,128]{2,1,0:T(8,128)(2,1)}, u32[]{:S(2)}) copy-start(bf16[64,128,128]{2,1,0:T(8,128)(2,1)} %get-tuple-element.832) | copy-start | bytes 6291460 | tf_op jit(solution)/shard_map/while
  113.7 6.0 %copy-start.2 = (bf16[64,128,128]{2,1,0:T(8,128)(2,1)S(1)}, bf16[64,128,128]{2,1,0:T(8,128)(2,1)}, u32[]{:S(2)}) copy-start(bf16[64,128,128]{2,1,0:T(8,128)(2,1)} %get-tuple-element.832) | copy-start | bytes 6291460 | tf_op jit(solution)/shard_map/while
  122.9 6.0 %copy-start.2 = (bf16[64,128,128]{2,1,0:T(8,128)(2,1)S(1)}, bf16[64,128,128]{2,1,0:T(8,128)(2,1)}, u32[]{:S(2)}) copy-start(bf16[64,128,128]{2,1,0:T(8,128)(2,1)} %get-tuple-element.832) | copy-start | bytes 6291460 | tf_op jit(solution)/shard_map/while
  134.9 7.7 %copy-start.3 = (bf16[64,128,128]{2,1,0:T(8,128)(2,1)S(1)}, bf16[64,128,128]{2,1,0:T(8,128)(2,1)}, u32[]{:S(2)}) copy-start(bf16[64,128,128]{2,1,0:T(8,128)(2,1)} %get-tuple-element.881) | copy-start | bytes 6291460 | tf_op jit(solution)/shard_map/while
  136.5 2.7 copy-start.16
  148.5 7.7 %copy-start.3 = (bf16[64,128,128]{2,1,0:T(8,128)(2,1)S(1)}, bf16[64,128,128]{2,1,0:T(8,128)(2,1)}, u32[]{:S(2)}) copy-start(bf16[64,128,128]{2,1,0:T(8,128)(2,1)} %get-tuple-element.881) | copy-start | bytes 6291460 | tf_op jit(solution)/shard_map/while
  150.1 2.7 copy-start.16
  162.0 7.7 %copy-start.3 = (bf16[64,128,128]{2,1,0:T(8,128)(2,1)S(1)}, bf16[64,128,128]{2,1,0:T(8,128)(2,1)}, u32[]{:S(2)}) copy-start(bf16[64,128,128]{2,1,0:T(8,128)(2,1)} %get-tuple-element.881) | copy-start | bytes 6291460 | tf_op jit(solution)/shard_map/while
  163.6 2.7 copy-start.16
  175.6 7.7 %copy-start.3 = (bf16[64,128,128]{2,1,0:T(8,128)(2,1)S(1)}, bf16[64,128,128]{2,1,0:T(8,128)(2,1)}, u32[]{:S(2)}) copy-start(bf16[64,128,128]{2,1,0:T(8,128)(2,1)} %get-tuple-element.881) | copy-start | bytes 6291460 | tf_op jit(solution)/shard_map/while
  177.2 2.7 copy-start.16
  189.1 7.7 %copy-start.3 = (bf16[64,128,128]{2,1,0:T(8,128)(2,1)S(1)}, bf16[64,128,128]{2,1,0:T(8,128)(2,1)}, u32[]{:S(2)}) copy-start(bf16[64,128,128]{2,1,0:T(8,128)(2,1)} %get-tuple-element.881) | copy-start | bytes 6291460 | tf_op jit(solution)/shard_map/while
  190.7 2.7 copy-start.16
  212.1 3.9 copy-start.14
  230.1 9.1 %copy-start.6 = (f32[4,128,128]{2,1,0:T(8,128)}, f32[4,128,128]{2,1,0:T(8,128)S(1)}, u32[]{:S(2)}) copy-start(f32[4,128,128]{2,1,0:T(8,128)S(1)} %scatter_fusion.1) | copy-start | bytes 786436 | tf_op jit(solution)/shard_map/while
  232.0 7.2 %copy-start.1 = (f32[4,1024,128]{2,1,0:T(8,128)S(1)}, f32[4,1024,128]{2,1,0:T(8,128)}, u32[]{:S(2)}) copy-start(f32[4,1024,128]{2,1,0:T(8,128)} %fusion.120) | copy-start | bytes 6291460 | tf_op jit(solution)/shard_map/while
  247.0 3.9 copy-start.14
  265.0 9.1 %copy-start.6 = (f32[4,128,128]{2,1,0:T(8,128)}, f32[4,128,128]{2,1,0:T(8,128)S(1)}, u32[]{:S(2)}) copy-start(f32[4,128,128]{2,1,0:T(8,128)S(1)} %scatter_fusion.1) | copy-start | bytes 786436 | tf_op jit(solution)/shard_map/while
  266.9 7.2 %copy-start.1 = (f32[4,1024,128]{2,1,0:T(8,128)S(1)}, f32[4,1024,128]{2,1,0:T(8,128)}, u32[]{:S(2)}) copy-start(f32[4,1024,128]{2,1,0:T(8,128)} %fusion.120) | copy-start | bytes 6291460 | tf_op jit(solution)/shard_map/while
  281.9 3.9 copy-start.14
  299.9 9.1 %copy-start.6 = (f32[4,128,128]{2,1,0:T(8,128)}, f32[4,128,128]{2,1,0:T(8,128)S(1)}, u32[]{:S(2)}) copy-start(f32[4,128,128]{2,1,0:T(8,128)S(1)} %scatter_fusion.1) | copy-start | bytes 786436 | tf_op jit(solution)/shard_map/while
  301.8 7.2 %copy-start.1 = (f32[4,1024,128]{2,1,0:T(8,128)S(1)}, f32[4,1024,128]{2,1,0:T(8,128)}, u32[]{:S(2)}) copy-start(f32[4,1024,128]{2,1,0:T(8,128)} %fusion.120) | copy-start | bytes 6291460 | tf_op jit(solution)/shard_map/while
  316.7 3.9 copy-start.14
  334.8 9.1 %copy-start.6 = (f32[4,128,128]{2,1,0:T(8,128)}, f32[4,128,128]{2,1,0:T(8,128)S(1)}, u32[]{:S(2)}) copy-start(f32[4,128,128]{2,1,0:T(8,128)S(1)} %scatter_fusion.1) | copy-start | bytes 786436 | tf_op jit(solution)/shard_map/while
  336.7 7.2 %copy-start.1 = (f32[4,1024,128]{2,1,0:T(8,128)S(1)}, f32[4,1024,128]{2,1,0:T(8,128)}, u32[]{:S(2)}) copy-start(f32[4,1024,128]{2,1,0:T(8,128)} %fusion.120) | copy-start | bytes 6291460 | tf_op jit(solution)/shard_map/while
  351.6 3.9 copy-start.14
  369.7 9.0 %copy-start.6 = (f32[4,128,128]{2,1,0:T(8,128)}, f32[4,128,128]{2,1,0:T(8,128)S(1)}, u32[]{:S(2)}) copy-start(f32[4,128,128]{2,1,0:T(8,128)S(1)} %scatter_fusion.1) | copy-start | bytes 786436 | tf_op jit(solution)/shard_map/while
  371.5 7.2 %copy-start.1 = (f32[4,1024,128]{2,1,0:T(8,128)S(1)}, f32[4,1024,128]{2,1,0:T(8,128)}, u32[]{:S(2)}) copy-start(f32[4,1024,128]{2,1,0:T(8,128)} %fusion.120) | copy-start | bytes 6291460 | tf_op jit(solution)/shard_map/while
  385.0 167.7 %reduce-scatter.5.cloned.1.call-start = ((), (), s32[]{:S(2)}) async-start(), calls=%async_computation.13 | async-start | bytes 4456448 | tf_op jit(solution)/shard_map/reduce_scatter | solution.py:219
  385.0 7.1 %copy-start.7 = (f32[4,128,128]{2,1,0:T(8,128)S(1)}, f32[4,128,128]{2,1,0:T(8,128)}, u32[]{:S(2)}) copy-start(f32[4,128,128]{2,1,0:T(8,128)} %get-tuple-element.234) | copy-start | bytes 786436
  385.5 15.8 %all-to-all-start.3 = ((bf16[16,32,128]{2,1,0:T(8,128)(2,1)}), bf16[16,32,128]{2,1,0:T(8,128)(2,1)S(1)}, u32[]{:S(2)}, u32[]{:S(2)}) async-start(bf16[16,32,128]{2,1,0:T(8,128)(2,1)} %bitcast.32), calls=%async_computation.3 | async-start | bytes 262144 | tf_op jit(solution)/shard_map/all_to_all | solution.py:226
  401.3 67.0 %all-to-all-start.5 = ((bf16[16,32,128]{2,1,0:T(8,128)(2,1)}), bf16[16,32,128]{2,1,0:T(8,128)(2,1)S(1)}, u32[]{:S(2)}, u32[]{:S(2)}) async-start(bf16[16,32,128]{2,1,0:T(8,128)(2,1)} %bitcast.37), calls=%async_computation.5 | async-start | bytes 262144 | tf_op jit(solution)/shard_map/all_to_all | solution.py:229
  468.3 85.9 %all-to-all-start.6 = ((bf16[16,32,128]{2,1,0:T(8,128)(2,1)}), bf16[16,32,128]{2,1,0:T(8,128)(2,1)S(1)}, u32[]{:S(2)}, u32[]{:S(2)}) async-start(bf16[16,32,128]{2,1,0:T(8,128)(2,1)} %bitcast.40), calls=%async_computation.7 | async-start | bytes 262144 | tf_op jit(solution)/shard_map/all_to_all | solution.py:232
  554.2 18.5 %all-to-all-start.7 = ((bf16[16,32,128]{2,1,0:T(8,128)(2,1)}), bf16[16,32,128]{2,1,0:T(8,128)(2,1)S(1)}, u32[]{:S(2)}, u32[]{:S(2)}) async-start(bf16[16,32,128]{2,1,0:T(8,128)(2,1)} %bitcast.43), calls=%async_computation.9 | async-start | bytes 262144 | tf_op jit(solution)/shard_map/all_to_all | solution.py:233
  (51 other events, 80.5 us)
Sparse Core Ops, SparseCore 0:
  27.3 44.3 all-gather.2
  76.7 50.3 all-gather.4
  385.1 81.5 reduce-scatter.2
  470.6 81.9 reduce-scatter.4
where the time goes:
time: 583 us; the launch traced here: 580 us
  local copies, waits for them, and re-layouts  174 us (30%)
  waiting for transfers between devices  157 us (27%)
  other arithmetic  137 us (23%)
  starting transfers between devices  43.3 us (7%)
  matrix products  33.4 us (6%)
  blocking collectives  19 us (3%)
  between operations  14.7 us (3%)
    reduce_scatter x1, waiting for transfers between devices, per_device(): lax.psum_scatter(from_tiles(value_grad, head_local), 'seq', scatter_dimen...  74.2 us
    reduce_scatter x1, waiting for transfers between devices, per_device(): lax.psum_scatter(from_tiles(key_grad, head_local), 'seq', scatter_dimensi...  61.3 us
    scatter-add x5, other arithmetic, grad_step(): running[1].at[flat_ids].add(key_part.reshape(-1, tile_rows, head_width))  35.9 us
    scatter-add x5, other arithmetic, grad_step(): running[2].at[flat_ids].add(value_part.reshape(-1, tile_rows, head_width))  31.3 us
    gather x10, local copies, waits for them, and re-layouts, fetch(): value_all[tile_ids].reshape(lane_count, GROUP * tile_rows, head_width)  24 us
    gather x60, local copies, waits for them, and re-layouts, batch_at(): columns = jnp.take_along_axis(ranking[item_ids], offsets, axis=1)  22.2 us
    gather x15, local copies, waits for them, and re-layouts, fetch(): key_all[tile_ids].reshape(lane_count, GROUP * tile_rows, head_width)  20.4 us
    all_to_all x1, blocking collectives, per_device(): lax.all_to_all(key_vectors, 'head', split_axis=1, concat_axis=0, tiled=True)  19 us
  transfers between devices with their start and end apart: 11, of which 5 were waited for; matrix products, arithmetic and copies ran while one was open for 27% of the time, Pallas kernels for 0%

commit v1 on v0

v1 whole, which is shorter than its diff:
```python
import math

import jax
import jax.numpy as jnp
from jax import lax
from jax.experimental import pallas as pl
from jax.experimental.pallas import tpu as pltpu
from jax.sharding import PartitionSpec as P

DH = 128
TILE = 128
SCALE = 1.0 / math.sqrt(DH)
LOG2E = math.log2(math.e)
C1 = SCALE * LOG2E
QB = 256
KC = 512
NEG = -1e30
SHIFTS = (1, 3, 2)
BACK = (0, 1, 3, 2)

NT = (((1,), (1,)), ((), ()))
NN = (((1,), (0,)), ((), ()))


def dot(a, b, dims):
    return lax.dot_general(a, b, dims, preferred_element_type=jnp.float32)


def stats_kernel(*refs):
    qg, kv = refs[0:4], refs[4:8]
    bias_ref = refs[8]
    stat_ref, out_ref = refs[9:11]
    q_s, g_s, k_s, vt_s, xa_s, xb_s = refs[11:17]
    for j in range(4):
        rows = slice(j * 512, (j + 1) * 512)
        q_s[rows] = qg[j][:, 0].reshape(512, DH)
        g_s[rows] = qg[j][:, 1].reshape(512, DH)
        k_s[rows] = kv[j][:, 0].reshape(512, DH)
        vt_s[:, rows] = kv[j][:, 1].reshape(512, DH).T

    def score(qb, x_s):
        start = pl.multiple_of(qb * QB, QB)
        q = q_s[pl.ds(start, QB)]
        top = jnp.full((1, QB), NEG, jnp.float32)
        for c in range(4):
            s = dot(k_s[c * KC:(c + 1) * KC], q, NT) * C1
            bias = bias_ref[c * 4:(c + 1) * 4, pl.ds(start, QB)]
            x = (s.reshape(4, TILE, QB) + bias[:, None, :]).reshape(KC, QB)
            x_s[c * KC:(c + 1) * KC] = x
            top = jnp.maximum(top, jnp.max(x, axis=0, keepdims=True))
        return top

    def finish(qb, x_s, top):
        start = pl.multiple_of(qb * QB, QB)
        mass = jnp.zeros((1, QB), jnp.float32)
        acc = jnp.zeros((DH, QB), jnp.float32)
        for c in range(4):
            e = jnp.exp2(x_s[c * KC:(c + 1) * KC] - top)
            mass = mass + jnp.sum(e, axis=0, keepdims=True)
            acc = acc + dot(vt_s[:, c * KC:(c + 1) * KC], e.astype(jnp.bfloat16), NN)
        gt = g_s[pl.ds(start, QB)].astype(jnp.float32).T
        delta = jnp.sum(gt * acc, axis=0, keepdims=True)
        stat_ref[0, pl.ds(qb, 1)] = top
        stat_ref[1, pl.ds(qb, 1)] = mass
        stat_ref[2, pl.ds(qb, 1)] = delta
        out_ref[:, pl.ds(start, QB)] = acc

    def pair(i, top):
        top_b = score(2 * i + 1, xb_s)
        finish(2 * i, xa_s, top)
        top_a = score(jnp.minimum(2 * i + 2, 7), xa_s)
        finish(2 * i + 1, xb_s, top_b)
        return top_a

    lax.fori_loop(0, 4, pair, score(0, xa_s))


def grad_kernel(*refs):
    qg, kv = refs[0:4], refs[4:8]
    bias_ref, acc_ref = refs[8:10]
    stats = refs[10:14]
    o_ref, dq_ref, dk_ref, dv_ref = refs[14:18]
    q_s, g_s, k_s, v_s, kt_s, dk_s, dv_s, lse_s, delta_s, fade_s = refs[18:28]
    for j in range(4):
        rows = slice(j * 512, (j + 1) * 512)
        q_s[rows] = qg[j][:, 0].reshape(512, DH)
        g_s[rows] = qg[j][:, 1].reshape(512, DH)
        k = kv[j][:, 0].reshape(512, DH)
        k_s[rows] = k
        kt_s[:, rows] = k.T
        v_s[rows] = kv[j][:, 1].reshape(512, DH)
    tops, masses, deltas = [], [], []
    for shift, stat in zip((0,) + SHIFTS, stats):
        order = [BACK.index((BACK[j] - shift) % 4) for j in range(4)]
        for held, n in ((tops, 0), (masses, 1), (deltas, 2)):
            held.append(jnp.concatenate([stat[n, 2 * p:2 * p + 2] for p in order], axis=0))
    top = jnp.maximum(jnp.maximum(tops[0], tops[1]), jnp.maximum(tops[2], tops[3]))
    fades = [jnp.exp2(t - top) for t in tops]
    mass = sum(m * f for m, f in zip(masses, fades))
    inv_mass = 1.0 / mass
    delta_s[...] = sum(d * f for d, f in zip(deltas, fades)) * inv_mass
    lse_s[...] = top + jnp.log2(mass)
    fade_s[...] = fades[0] * inv_mass
    dk_s[...] = jnp.zeros_like(dk_s)
    dv_s[...] = jnp.zeros_like(dv_s)

    def block(qb, carry):
        start = pl.multiple_of(qb * QB, QB)
        q = q_s[pl.ds(start, QB)]
        g = g_s[pl.ds(start, QB)]
        lse = lse_s[pl.ds(qb, 1)]
        delta = delta_s[pl.ds(qb, 1)]
        out = acc_ref[:, pl.ds(start, QB)] * fade_s[pl.ds(qb, 1)]
        o_ref[pl.ds(start, QB)] = out.T.astype(jnp.bfloat16)
        dqt = jnp.zeros((DH, QB), jnp.float32)
        for c in range(4):
            rows = slice(c * KC, (c + 1) * KC)
            s = dot(k_s[rows], q, NT) * C1
            shift = bias_ref[c * 4:(c + 1) * 4, pl.ds(start, QB)] - lse
            w = jnp.exp2((s.reshape(4, TILE, QB) + shift[:, None, :]).reshape(KC, QB))
            dp = dot(v_s[rows], g, NT)
            ds = (w * (dp - delta)).astype(jnp.bfloat16)
            dv_s[rows] += dot(w.astype(jnp.bfloat16), g, NN)
            dk_s[rows] += dot(ds, q, NN)
            dqt = dqt + dot(kt_s[:, rows], ds, NN)
        dq_ref[pl.ds(start, QB)] = (dqt * SCALE).T.astype(jnp.bfloat16)
        return carry

    lax.fori_loop(0, 8, block, 0)
    dk_ref[...] = (dk_s[...] * SCALE).astype(jnp.bfloat16)
    dv_ref[...] = dv_s[...].astype(jnp.bfloat16)


VM = pl.BlockSpec(memory_space=pltpu.VMEM)
PARAMS = pltpu.CompilerParams(vmem_limit_bytes=40 * 1024 * 1024)


def run_stats(qg, kv, bias):
    return pl.pallas_call(
        stats_kernel,
        out_shape=(
            jax.ShapeDtypeStruct((3, 8, QB), jnp.float32),
            jax.ShapeDtypeStruct((DH, 2048), jnp.float32),
        ),
        in_specs=[VM] * 9,
        out_specs=(VM, VM),
        scratch_shapes=[pltpu.VMEM((2048, DH), jnp.bfloat16)] * 3
        + [pltpu.VMEM((DH, 2048), jnp.bfloat16)]
        + [pltpu.VMEM((2048, QB), jnp.float32)] * 2,
        compiler_params=PARAMS,
        name="stats",
    )(*qg, *kv, bias)


def run_grads(qg, kv, bias, acc, stats):
    half = jax.ShapeDtypeStruct((2048, DH), jnp.bfloat16)
    return pl.pallas_call(
        grad_kernel,
        out_shape=(half,) * 4,
        in_specs=[VM] * 14,
        out_specs=(VM,) * 4,
        scratch_shapes=[pltpu.VMEM((2048, DH), jnp.bfloat16)] * 4
        + [pltpu.VMEM((DH, 2048), jnp.bfloat16)]
        + [pltpu.VMEM((2048, DH), jnp.float32)] * 2
        + [pltpu.VMEM((8, QB), jnp.float32)] * 3,
        compiler_params=PARAMS,
        name="grads",
    )(*qg, *kv, bias, acc, *stats)


def ring(n, k):
    return [(i, (i + k) % n) for i in range(n)]


def per_device(queries, key_vectors, value_vectors, out_grad, key_tiles, tile_count):
    x_at = lax.axis_index("x")
    y_at = lax.axis_index("y")
    head_at = lax.axis_index("z") * 2 + lax.axis_index("core")

    back = jnp.array(BACK, jnp.int32)
    q_tiles = x_at * 16 + ((y_at - back) % 4)[:, None] * 4 + jnp.arange(4, dtype=jnp.int32)[None]
    k_tiles = ((x_at - back) % 4)[:, None] * 16 + y_at * 4 + jnp.arange(4, dtype=jnp.int32)[None]
    lists = lax.dynamic_slice(key_tiles, (head_at, 0, 0), (1, 64, key_tiles.shape[2]))[0]
    counts = lax.dynamic_slice(tile_count, (head_at, 0), (1, 64))[0]
    live = jnp.arange(key_tiles.shape[2], dtype=jnp.int32)[None, :] < counts[:, None]
    lists = jnp.where(live, lists, -1)[q_tiles.reshape(16)]
    hit = jnp.any(lists[None, :, :] == k_tiles.reshape(16)[:, None, None], axis=2)
    bias = jnp.repeat(jnp.where(hit, 0.0, NEG).astype(jnp.float32), TILE, axis=1)

    def by_head(a):
        return a.reshape(32, 16, DH).transpose(1, 0, 2)

    packed = jnp.stack(
        [by_head(queries), by_head(out_grad), by_head(key_vectors), by_head(value_vectors)], axis=1
    )
    got = lax.all_to_all(packed, ("z", "core"), split_axis=0, concat_axis=0, tiled=True)
    qg_own, kv_own = got[:, 0:2], got[:, 2:4]
    qg = [qg_own] + [lax.ppermute(qg_own, "y", ring(4, k)) for k in SHIFTS]
    kv = [kv_own] + [lax.ppermute(kv_own, "x", ring(4, k)) for k in SHIFTS]
    stat, acc = run_stats(qg, kv, bias)
    stats = [stat] + [lax.ppermute(stat, "y", ring(4, k)) for k in SHIFTS]
    out, dq, dk, dv = run_grads(qg, kv, bias, acc, stats)

    def scatter_pair(a, b, axis):
        pa, pb = a.reshape(4, 512, DH), b.reshape(4, 512, DH)
        both = [jnp.stack([pa[j], pb[j]]) for j in range(4)]
        total = both[0].astype(jnp.float32)
        for j, k in enumerate((3, 1, 2)):
            total = total + lax.ppermute(both[j + 1], axis, ring(4, k)).astype(jnp.float32)
        return total.astype(jnp.bfloat16).reshape(2, 16, 32, DH)

    od = scatter_pair(out, dq, "y")
    kvd = scatter_pair(dk, dv, "x")
    send = jnp.concatenate([od, kvd], axis=0).transpose(1, 0, 2, 3)
    back_home = lax.all_to_all(send, ("z", "core"), split_axis=0, concat_axis=0, tiled=True)

    def by_row(a):
        return a.transpose(1, 0, 2).reshape(32, 16 * DH)

    return tuple(by_row(back_home[:, j]) for j in range(4))


def solution(mesh):
    grid = jax.sharding.Mesh(mesh.devices.reshape(8, 2, 4, 4), ("z", "core", "x", "y"))
    rows = P(("x", "y", "z", "core"), None)
    return jax.shard_map(
        per_device,
        mesh=grid,
        in_specs=(rows, rows, rows, rows, P(), P()),
        out_specs=(rows,) * 4,
        check_vma=False,
    )
```

time: 583 us -> 121 us (0.21)
  local copies, waits for them, and re-layouts: 174 us -> 6.42 us
  other arithmetic: 137 us -> 1.98 us
  waiting for transfers between devices: 157 us -> 39.2 us
  matrix products: 33.4 us -> 0 us
  Pallas kernels: 0 us -> 18.6 us
  starting transfers between devices: 43.3 us -> 28.6 us
  between operations: 14.7 us -> 0.85 us
  blocking collectives: 19 us -> 25.2 us
    reduce_scatter x2 -> x0, waiting for transfers between devices: 136 us -> none  [the longest x1 74.2 us: per_device(): lax.psum_scatter(from_tiles(value_grad, head_local), 'seq', scatter_dimen...]
    gather x157 -> x1, local copies, waits for them, and re-layouts: 129 us -> 0.57 us  [per_device(): lists = jnp.where(live, lists, -1)[q_tiles.reshape(16)]]
    scatter-add x21 -> x0, other arithmetic: 75.8 us -> none  [the longest x5 35.9 us: grad_step(): running[1].at[flat_ids].add(key_part.reshape(-1, tile_rows, head_width))]
    dot_general x35 -> x0, matrix products: 33.4 us -> none  [the longest x5 9.51 us: grad_step(): jnp.einsum('rqk,rqd->rkd', weights.astype(jnp.bfloat16), grad_rows, prefe...]
    all_to_all x7 -> x1, starting transfers between devices: 43.2 us -> 9.98 us  [per_device(): lax.all_to_all(packed, ('z', 'core'), split_axis=0, concat_axis=0, tiled=...]
    ppermute x0 -> x15, waiting for transfers between devices: none -> 22.8 us  [the longest x6 9.39 us: scatter_pair(): lax.ppermute(both[j + 1], axis, ring(4, k)).astype(jnp.float32)]
    ppermute x0 -> x15, starting transfers between devices: none -> 18.6 us  [the longest x6 5.09 us: scatter_pair(): lax.ppermute(both[j + 1], axis, ring(4, k)).astype(jnp.float32)]
    pallas_call x0 -> x2, Pallas kernels: none -> 18.6 us  [the longest x1 12.4 us: run_grads(): pl.pallas_call(grad_kernel, out_shape=(half,) * 4, in_specs=[VM] * 14, ou...]
  transfers between devices with their start and end apart: 11 -> 16, of which waited for: 5 -> 13; matrix products, arithmetic and copies ran while one was open for 27% -> 2% of each run, Pallas kernels for 0% -> 0%
where the time goes in v1:
time: 121 us
  waiting for transfers between devices  39.2 us (32%)
  starting transfers between devices  28.6 us (24%)
  blocking collectives  25.2 us (21%)
  Pallas kernels  18.6 us (15%)
  local copies, waits for them, and re-layouts  6.42 us (5%)
  other arithmetic  1.98 us (2%)
    all_to_all x1, blocking collectives, per_device(): lax.all_to_all(send, ('z', 'core'), split_axis=0, concat_axis=0, tiled=True)  25.2 us
    all_to_all x1, waiting for transfers between devices, per_device(): lax.all_to_all(packed, ('z', 'core'), split_axis=0, concat_axis=0, tiled=...  16.4 us
    pallas_call x1, Pallas kernels, run_grads(): pl.pallas_call(grad_kernel, out_shape=(half,) * 4, in_specs=[VM] * 14, ou...  12.4 us
    all_to_all x1, starting transfers between devices, per_device(): lax.all_to_all(packed, ('z', 'core'), split_axis=0, concat_axis=0, tiled=...  9.98 us
    ppermute x6, waiting for transfers between devices, scatter_pair(): lax.ppermute(both[j + 1], axis, ring(4, k)).astype(jnp.float32)  9.39 us
    ppermute x3, waiting for transfers between devices, per_device(): qg = [qg_own] + [lax.ppermute(qg_own, 'y', ring(4, k)) for k in SHIFTS]  6.54 us
    pallas_call x1, Pallas kernels, run_stats(): pl.pallas_call(stats_kernel, out_shape=(jax.ShapeDtypeStruct((3, 8, QB),...  6.17 us
    ppermute x6, starting transfers between devices, scatter_pair(): lax.ppermute(both[j + 1], axis, ring(4, k)).astype(jnp.float32)  5.09 us
  transfers between devices with their start and end apart: 16, of which 13 were waited for; matrix products, arithmetic and copies ran while one was open for 2% of the time, Pallas kernels for 0%

profile of v1, /device:TPU:1, one launch (start us, length us, event | category | flops | bytes accessed | tf_op | source)
XLA Modules:
  0.0 120.8 jit_solution(7659190967702011087)
XLA Ops:
  0.7 1.1 bitcast_bitcast_fusion.2
  1.8 0.9 pad_maximum_fusion
  2.7 10.0 %all-to-all-start = ((bf16[16,4,32,128]{3,2,1,0:T(8,128)(2,1)}), bf16[16,4,32,128]{3,2,1,0:T(8,128)(2,1)S(1)}, u32[]{:S(2)}, u32[]{:S(2)}) async-start(bf16[16,4,32,128]{3,2,1,0:T(8,128)(2,1)} %pad_maximum_fusion), calls=%async_computation | async-start | bytes 1048576 | tf_op jit(solution)/shard_map/all_to_all | solution.py:196
  12.7 0.6 copy-done.3
  13.4 0.1 add.111
  13.6 16.4 %all-to-all-done = bf16[16,4,32,128]{3,2,1,0:T(8,128)(2,1)S(1)} async-done(((bf16[16,4,32,128]{3,2,1,0:T(8,128)(2,1)}), bf16[16,4,32,128]{3,2,1,0:T(8,128)(2,1)S(1)}, u32[]{:S(2)}, u32[]{:S(2)}) %all-to-all-start) | async-done | bytes 524320 | tf_op jit(solution)/shard_map/all_to_all | solution.py:196
  30.1 2.8 %collective-permute-start.5 = (bf16[16,2,32,128]{3,2,1,0:T(8,128)(2,1)S(1)}, bf16[16,2,32,128]{3,2,1,0:T(8,128)(2,1)S(1)}, u32[]{:S(2)}, u32[]{:S(2)}) collective-permute-start(bf16[16,2,32,128]{3,2,1,0:T(8,128)(2,1)S(1)} %get-tuple-element.36.refs_4_), channel_id=1, source_target_pairs={{0,8},{4,12},{8,0},{12,4},{1,9},{5,13},{9,1},{13,5},{2,10},{6,14},... | collective-permute-start | bytes 786440 | tf_op jit(solution)/shard_map/ppermute | solution.py:199
  32.9 0.7 dynamic-slice_bitcast_fusion
  33.6 0.1 add.119
  33.7 0.1 copy.47
  33.8 0.6 gather_fusion
  34.4 0.9 collective-permute-start.4
  35.3 0.6 collective-permute-start.3
  35.9 2.9 %collective-permute-start.2 = (bf16[16,2,32,128]{3,2,1,0:T(8,128)(2,1)S(1)}, bf16[16,2,32,128]{3,2,1,0:T(8,128)(2,1)S(1)}, u32[]{:S(2)}, u32[]{:S(2)}) collective-permute-start(bf16[16,2,32,128]{3,2,1,0:T(8,128)(2,1)S(1)} %get-tuple-element.37.refs_0_), channel_id=1, source_target_pairs={{0,2},{1,3},{2,0},{3,1},{4,6},{5,7},{6,4},{7,5},{8,10},{9,11},{10,... | collective-permute-start | bytes 786440 | tf_op jit(solution)/shard_map/ppermute | solution.py:198
  38.9 0.8 collective-permute-start.1
  39.6 1.3 %collective-permute-start = (bf16[16,2,32,128]{3,2,1,0:T(8,128)(2,1)S(1)}, bf16[16,2,32,128]{3,2,1,0:T(8,128)(2,1)S(1)}, u32[]{:S(2)}, u32[]{:S(2)}) collective-permute-start(bf16[16,2,32,128]{3,2,1,0:T(8,128)(2,1)S(1)} %get-tuple-element.37.refs_0_), channel_id=1, source_target_pairs={{0,1},{1,2},{2,3},{3,0},{4,5},{5,6},{6,7},{7,4},{8,9},{9,10},{10,1... | collective-permute-start | bytes 786440 | tf_op jit(solution)/shard_map/ppermute | solution.py:198
  40.9 0.4 compare_reduce_fusion
  41.4 0.1 broadcast_in_dim.25
  41.5 3.5 %collective-permute-done.4.refs_6_ = bf16[16,2,32,128]{3,2,1,0:T(8,128)(2,1)S(1)} collective-permute-done((bf16[16,2,32,128]{3,2,1,0:T(8,128)(2,1)S(1)}, bf16[16,2,32,128]{3,2,1,0:T(8,128)(2,1)S(1)}, u32[]{:S(2)}, u32[]{:S(2)}) %collective-permute-start.4) | collective-permute-done | bytes 262176 | tf_op jit(solution)/shard_map/ppermute | solution.py:199
  45.0 0.1 collective-permute-done.3.refs_5_
  45.1 0.6 collective-permute-done.2.refs_3_
  45.7 6.0 %collective-permute-done.1.refs_2_ = bf16[16,2,32,128]{3,2,1,0:T(8,128)(2,1)S(1)} collective-permute-done((bf16[16,2,32,128]{3,2,1,0:T(8,128)(2,1)S(1)}, bf16[16,2,32,128]{3,2,1,0:T(8,128)(2,1)S(1)}, u32[]{:S(2)}, u32[]{:S(2)}) %collective-permute-start.1) | collective-permute-done | bytes 262176 | tf_op jit(solution)/shard_map/ppermute | solution.py:198
  51.7 6.2 %stats.1 = (f32[3,8,256]{2,1,0:T(8,128)S(1)}, f32[128,2048]{1,0:T(8,128)S(1)}) custom-call(bf16[16,2,32,128]{3,2,1,0:T(8,128)(2,1)S(1)} %get-tuple-element.37.refs_0_, bf16[16,2,32,128]{3,2,1,0:T(8,128)(2,1)S(1)} %collective-permute-done.refs_1_, bf16[16,2,32,128]{3,2,1,0:T(8,128)(2,1)S(1)} %collective-permute-done.1.refs_2_, ...), custom_call_target="tpu_custom_call" | custom-call | tf_op jit(solution)/shard_map/stats/pallas_call | solution.py:139
  57.9 2.7 %collective-permute-start.8 = (f32[3,8,256]{2,1,0:T(8,128)S(1)}, f32[3,8,256]{2,1,0:T(8,128)S(1)}, u32[]{:S(2)}, u32[]{:S(2)}) collective-permute-start(f32[3,8,256]{2,1,0:T(8,128)S(1)} %get-tuple-element.11.refs_10_), channel_id=1, source_target_pairs={{0,2},{1,3},{2,0},{3,1},{4,6},{5,7},{6,4},{7,5},{8,10},{9,11},{10,... | collective-permute-start | bytes 73736 | tf_op jit(solution)/shard_map/ppermute | solution.py:201
  60.6 0.8 collective-permute-start.7
  61.4 0.6 collective-permute-start.6
  62.0 0.1 collective-permute-done.8.refs_13_
  62.1 1.3 %collective-permute-done.7.refs_12_ = f32[3,8,256]{2,1,0:T(8,128)S(1)} collective-permute-done((f32[3,8,256]{2,1,0:T(8,128)S(1)}, f32[3,8,256]{2,1,0:T(8,128)S(1)}, u32[]{:S(2)}, u32[]{:S(2)}) %collective-permute-start.7) | collective-permute-done | bytes 24608 | tf_op jit(solution)/shard_map/ppermute | solution.py:201
  63.4 1.9 %collective-permute-done.6.refs_11_ = f32[3,8,256]{2,1,0:T(8,128)S(1)} collective-permute-done((f32[3,8,256]{2,1,0:T(8,128)S(1)}, f32[3,8,256]{2,1,0:T(8,128)S(1)}, u32[]{:S(2)}, u32[]{:S(2)}) %collective-permute-start.6) | collective-permute-done | bytes 24608 | tf_op jit(solution)/shard_map/ppermute | solution.py:201
  65.3 12.4 %grads.1 = (bf16[2048,128]{1,0:T(8,128)(2,1)S(1)}, bf16[2048,128]{1,0:T(8,128)(2,1)S(1)}, bf16[2048,128]{1,0:T(8,128)(2,1)S(1)}, bf16[2048,128]{1,0:T(8,128)(2,1)S(1)}) custom-call(bf16[16,2,32,128]{3,2,1,0:T(8,128)(2,1)S(1)} %get-tuple-element.37.refs_0_, bf16[16,2,32,128]{3,2,1,0:T(8,128)(2,1)S(1)} %collective-permute-done.refs_1_, ...), custom_call_target="tpu_custom_call" | custom-call | tf_op jit(solution)/shard_map/grads/pallas_call | solution.py:157
  77.8 0.4 collective-permute-start.9
  78.2 1.4 %collective-permute-start.10 = (bf16[2,512,128]{2,1,0:T(8,128)(2,1)S(1)}, bf16[2,512,128]{2,1,0:T(8,128)(2,1)S(1)}, u32[]{:S(2)}, u32[]{:S(2)}) collective-permute-start(bf16[2,512,128]{2,1,0:T(8,128)(2,1)S(1)} %pad_maximum_fusion.3), channel_id=1, source_target_pairs={{0,1},{1,2},{2,3},{3,0},{4,5},{5,6},{6,7},{7,4},{8,9},{9,10},{10,1... | collective-permute-start | bytes 786440 | tf_op jit(solution)/shard_map/ppermute | solution.py:209
  79.7 0.5 collective-permute-start.11
  80.3 2.1 %collective-permute-start.12 = (bf16[2,512,128]{2,1,0:T(8,128)(2,1)S(1)}, bf16[2,512,128]{2,1,0:T(8,128)(2,1)S(1)}, u32[]{:S(2)}, u32[]{:S(2)}) collective-permute-start(bf16[2,512,128]{2,1,0:T(8,128)(2,1)S(1)} %pad_maximum_fusion.5), channel_id=1, source_target_pairs={{0,12},{4,0},{8,4},{12,8},{1,13},{5,1},{9,5},{13,9},{2,14},{6,2},{... | collective-permute-start | bytes 786440 | tf_op jit(solution)/shard_map/ppermute | solution.py:209
  82.4 0.1 collective-permute-start.13
  82.6 1.0 collective-permute-done.9
  83.5 0.6 collective-permute-start.14
  84.1 3.4 %collective-permute-done.10 = bf16[2,512,128]{2,1,0:T(8,128)(2,1)S(1)} collective-permute-done((bf16[2,512,128]{2,1,0:T(8,128)(2,1)S(1)}, bf16[2,512,128]{2,1,0:T(8,128)(2,1)S(1)}, u32[]{:S(2)}, u32[]{:S(2)}) %collective-permute-start.10) | collective-permute-done | bytes 262176 | tf_op jit(solution)/shard_map/ppermute | solution.py:209
  87.5 2.4 %collective-permute-done.11 = bf16[2,512,128]{2,1,0:T(8,128)(2,1)S(1)} collective-permute-done((bf16[2,512,128]{2,1,0:T(8,128)(2,1)S(1)}, bf16[2,512,128]{2,1,0:T(8,128)(2,1)S(1)}, u32[]{:S(2)}, u32[]{:S(2)}) %collective-permute-start.11) | collective-permute-done | bytes 262176 | tf_op jit(solution)/shard_map/ppermute | solution.py:209
  89.9 0.1 add_convert_fusion.1
  90.0 2.2 %collective-permute-done.13 = bf16[2,512,128]{2,1,0:T(8,128)(2,1)S(1)} collective-permute-done((bf16[2,512,128]{2,1,0:T(8,128)(2,1)S(1)}, bf16[2,512,128]{2,1,0:T(8,128)(2,1)S(1)}, u32[]{:S(2)}, u32[]{:S(2)}) %collective-permute-start.13) | collective-permute-done | bytes 262176 | tf_op jit(solution)/shard_map/ppermute | solution.py:209
  92.2 0.5 collective-permute-done.14
  92.7 0.1 add_convert_fusion
  92.9 25.2 %all_to_all.10 = bf16[16,4,32,128]{3,2,1,0:T(8,128)(2,1)S(1)} all-to-all(bf16[16,4,32,128]{3,2,1,0:T(8,128)(2,1)S(1)} %copy_bitcast_fusion), channel_id=1, replica_groups=mesh['z'=8,'core'=2,'x'=4,'y'=4] {'z','core'}, dimensions={0} | all-to-all | bytes 1048576 | tf_op jit(solution)/shard_map/all_to_all | solution.py:215
  118.1 0.7 copy.75
  118.8 0.7 copy.76
  119.5 0.7 copy.77
  120.1 0.7 copy.78
  (32 shorter events, 0.8 us)
Async XLA Ops:
  0.6 12.9 %copy-start = (s32[16,64,38]{1,0,2:T(8,128)S(1)}, s32[16,64,38]{1,0,2:T(8,128)}, u32[]{:S(2)}) copy-start(s32[16,64,38]{1,0,2:T(8,128)} %param.11) | copy-start | bytes 466948
  0.6 1.1 copy-start.2
  0.7 1.1 copy-start.1
  2.7 27.3 %all-to-all-start = ((bf16[16,4,32,128]{3,2,1,0:T(8,128)(2,1)}), bf16[16,4,32,128]{3,2,1,0:T(8,128)(2,1)S(1)}, u32[]{:S(2)}, u32[]{:S(2)}) async-start(bf16[16,4,32,128]{3,2,1,0:T(8,128)(2,1)} %pad_maximum_fusion), calls=%async_computation | async-start | bytes 1048576 | tf_op jit(solution)/shard_map/all_to_all | solution.py:196
  12.7 0.7 copy-start.3
  30.1 9.6 %collective-permute-start.5 = (bf16[16,2,32,128]{3,2,1,0:T(8,128)(2,1)S(1)}, bf16[16,2,32,128]{3,2,1,0:T(8,128)(2,1)S(1)}, u32[]{:S(2)}, u32[]{:S(2)}) collective-permute-start(bf16[16,2,32,128]{3,2,1,0:T(8,128)(2,1)S(1)} %get-tuple-element.36.refs_4_), channel_id=1, source_target_pairs={{0,8},{4,12},{8,0},{12,4},{1,9},{5,13},{9,1},{13,5},{2,10},{6,14},... | collective-permute-start | bytes 786440 | tf_op jit(solution)/shard_map/ppermute | solution.py:199
  34.4 10.6 %collective-permute-start.4 = (bf16[16,2,32,128]{3,2,1,0:T(8,128)(2,1)S(1)}, bf16[16,2,32,128]{3,2,1,0:T(8,128)(2,1)S(1)}, u32[]{:S(2)}, u32[]{:S(2)}) collective-permute-start(bf16[16,2,32,128]{3,2,1,0:T(8,128)(2,1)S(1)} %get-tuple-element.36.refs_4_), channel_id=1, source_target_pairs={{0,12},{4,0},{8,4},{12,8},{1,13},{5,1},{9,5},{13,9},{2,14},{6,2},{... | collective-permute-start | bytes 786440 | tf_op jit(solution)/shard_map/ppermute | solution.py:199
  35.3 9.8 %collective-permute-start.3 = (bf16[16,2,32,128]{3,2,1,0:T(8,128)(2,1)S(1)}, bf16[16,2,32,128]{3,2,1,0:T(8,128)(2,1)S(1)}, u32[]{:S(2)}, u32[]{:S(2)}) collective-permute-start(bf16[16,2,32,128]{3,2,1,0:T(8,128)(2,1)S(1)} %get-tuple-element.36.refs_4_), channel_id=1, source_target_pairs={{0,4},{4,8},{8,12},{12,0},{1,5},{5,9},{9,13},{13,1},{2,6},{6,10},{... | collective-permute-start | bytes 786440 | tf_op jit(solution)/shard_map/ppermute | solution.py:199
  35.9 9.8 %collective-permute-start.2 = (bf16[16,2,32,128]{3,2,1,0:T(8,128)(2,1)S(1)}, bf16[16,2,32,128]{3,2,1,0:T(8,128)(2,1)S(1)}, u32[]{:S(2)}, u32[]{:S(2)}) collective-permute-start(bf16[16,2,32,128]{3,2,1,0:T(8,128)(2,1)S(1)} %get-tuple-element.37.refs_0_), channel_id=1, source_target_pairs={{0,2},{1,3},{2,0},{3,1},{4,6},{5,7},{6,4},{7,5},{8,10},{9,11},{10,... | collective-permute-start | bytes 786440 | tf_op jit(solution)/shard_map/ppermute | solution.py:198
  38.9 12.8 %collective-permute-start.1 = (bf16[16,2,32,128]{3,2,1,0:T(8,128)(2,1)S(1)}, bf16[16,2,32,128]{3,2,1,0:T(8,128)(2,1)S(1)}, u32[]{:S(2)}, u32[]{:S(2)}) collective-permute-start(bf16[16,2,32,128]{3,2,1,0:T(8,128)(2,1)S(1)} %get-tuple-element.37.refs_0_), channel_id=1, source_target_pairs={{0,3},{1,0},{2,1},{3,2},{4,7},{5,4},{6,5},{7,6},{8,11},{9,8},{10,9... | collective-permute-start | bytes 786440 | tf_op jit(solution)/shard_map/ppermute | solution.py:198
  39.6 12.0 %collective-permute-start = (bf16[16,2,32,128]{3,2,1,0:T(8,128)(2,1)S(1)}, bf16[16,2,32,128]{3,2,1,0:T(8,128)(2,1)S(1)}, u32[]{:S(2)}, u32[]{:S(2)}) collective-permute-start(bf16[16,2,32,128]{3,2,1,0:T(8,128)(2,1)S(1)} %get-tuple-element.37.refs_0_), channel_id=1, source_target_pairs={{0,1},{1,2},{2,3},{3,0},{4,5},{5,6},{6,7},{7,4},{8,9},{9,10},{10,1... | collective-permute-start | bytes 786440 | tf_op jit(solution)/shard_map/ppermute | solution.py:198
  57.9 4.3 %collective-permute-start.8 = (f32[3,8,256]{2,1,0:T(8,128)S(1)}, f32[3,8,256]{2,1,0:T(8,128)S(1)}, u32[]{:S(2)}, u32[]{:S(2)}) collective-permute-start(f32[3,8,256]{2,1,0:T(8,128)S(1)} %get-tuple-element.11.refs_10_), channel_id=1, source_target_pairs={{0,2},{1,3},{2,0},{3,1},{4,6},{5,7},{6,4},{7,5},{8,10},{9,11},{10,... | collective-permute-start | bytes 73736 | tf_op jit(solution)/shard_map/ppermute | solution.py:201
  60.6 2.8 %collective-permute-start.7 = (f32[3,8,256]{2,1,0:T(8,128)S(1)}, f32[3,8,256]{2,1,0:T(8,128)S(1)}, u32[]{:S(2)}, u32[]{:S(2)}) collective-permute-start(f32[3,8,256]{2,1,0:T(8,128)S(1)} %get-tuple-element.11.refs_10_), channel_id=1, source_target_pairs={{0,3},{1,0},{2,1},{3,2},{4,7},{5,4},{6,5},{7,6},{8,11},{9,8},{10,9... | collective-permute-start | bytes 73736 | tf_op jit(solution)/shard_map/ppermute | solution.py:201
  61.4 3.9 %collective-permute-start.6 = (f32[3,8,256]{2,1,0:T(8,128)S(1)}, f32[3,8,256]{2,1,0:T(8,128)S(1)}, u32[]{:S(2)}, u32[]{:S(2)}) collective-permute-start(f32[3,8,256]{2,1,0:T(8,128)S(1)} %get-tuple-element.11.refs_10_), channel_id=1, source_target_pairs={{0,1},{1,2},{2,3},{3,0},{4,5},{5,6},{6,7},{7,4},{8,9},{9,10},{10,1... | collective-permute-start | bytes 73736 | tf_op jit(solution)/shard_map/ppermute | solution.py:201
  77.8 5.7 %collective-permute-start.9 = (bf16[2,512,128]{2,1,0:T(8,128)(2,1)S(1)}, bf16[2,512,128]{2,1,0:T(8,128)(2,1)S(1)}, u32[]{:S(2)}, u32[]{:S(2)}) collective-permute-start(bf16[2,512,128]{2,1,0:T(8,128)(2,1)S(1)} %pad_maximum_fusion.2), channel_id=1, source_target_pairs={{0,3},{1,0},{2,1},{3,2},{4,7},{5,4},{6,5},{7,6},{8,11},{9,8},{10,9... | collective-permute-start | bytes 786440 | tf_op jit(solution)/shard_map/ppermute | solution.py:209
  78.2 9.3 %collective-permute-start.10 = (bf16[2,512,128]{2,1,0:T(8,128)(2,1)S(1)}, bf16[2,512,128]{2,1,0:T(8,128)(2,1)S(1)}, u32[]{:S(2)}, u32[]{:S(2)}) collective-permute-start(bf16[2,512,128]{2,1,0:T(8,128)(2,1)S(1)} %pad_maximum_fusion.3), channel_id=1, source_target_pairs={{0,1},{1,2},{2,3},{3,0},{4,5},{5,6},{6,7},{7,4},{8,9},{9,10},{10,1... | collective-permute-start | bytes 786440 | tf_op jit(solution)/shard_map/ppermute | solution.py:209
  79.7 10.2 %collective-permute-start.11 = (bf16[2,512,128]{2,1,0:T(8,128)(2,1)S(1)}, bf16[2,512,128]{2,1,0:T(8,128)(2,1)S(1)}, u32[]{:S(2)}, u32[]{:S(2)}) collective-permute-start(bf16[2,512,128]{2,1,0:T(8,128)(2,1)S(1)} %pad_maximum_fusion.4), channel_id=1, source_target_pairs={{0,2},{1,3},{2,0},{3,1},{4,6},{5,7},{6,4},{7,5},{8,10},{9,11},{10,... | collective-permute-start | bytes 786440 | tf_op jit(solution)/shard_map/ppermute | solution.py:209
  80.3 9.7 %collective-permute-start.12 = (bf16[2,512,128]{2,1,0:T(8,128)(2,1)S(1)}, bf16[2,512,128]{2,1,0:T(8,128)(2,1)S(1)}, u32[]{:S(2)}, u32[]{:S(2)}) collective-permute-start(bf16[2,512,128]{2,1,0:T(8,128)(2,1)S(1)} %pad_maximum_fusion.5), channel_id=1, source_target_pairs={{0,12},{4,0},{8,4},{12,8},{1,13},{5,1},{9,5},{13,9},{2,14},{6,2},{... | collective-permute-start | bytes 786440 | tf_op jit(solution)/shard_map/ppermute | solution.py:209
  82.4 9.8 %collective-permute-start.13 = (bf16[2,512,128]{2,1,0:T(8,128)(2,1)S(1)}, bf16[2,512,128]{2,1,0:T(8,128)(2,1)S(1)}, u32[]{:S(2)}, u32[]{:S(2)}) collective-permute-start(bf16[2,512,128]{2,1,0:T(8,128)(2,1)S(1)} %pad_maximum_fusion.6), channel_id=1, source_target_pairs={{0,4},{4,8},{8,12},{12,0},{1,5},{5,9},{9,13},{13,1},{2,6},{6,10},{... | collective-permute-start | bytes 786440 | tf_op jit(solution)/shard_map/ppermute | solution.py:209
  83.5 9.2 %collective-permute-start.14 = (bf16[2,512,128]{2,1,0:T(8,128)(2,1)S(1)}, bf16[2,512,128]{2,1,0:T(8,128)(2,1)S(1)}, u32[]{:S(2)}, u32[]{:S(2)}) collective-permute-start(bf16[2,512,128]{2,1,0:T(8,128)(2,1)S(1)} %pad_maximum_fusion.7), channel_id=1, source_target_pairs={{0,8},{4,12},{8,0},{12,4},{1,9},{5,13},{9,1},{13,5},{2,10},{6,14},... | collective-permute-start | bytes 786440 | tf_op jit(solution)/shard_map/ppermute | solution.py:209

commit v2 on v1

v2 whole, which is shorter than its diff:
```python
import math

import jax
import jax.numpy as jnp
from jax import lax
from jax.experimental import pallas as pl
from jax.experimental.pallas import tpu as pltpu
from jax.sharding import PartitionSpec as P
from jax.sharding import PartitionSpec as P

DH = 128
TILE = 128
SCALE = 1.0 / math.sqrt(DH)
LOG2E = math.log2(math.e)
C1 = SCALE * LOG2E
QB = 256
KC = 512
NEG = -1e30
SHIFTS = (1, 3, 2)
BACK = (0, 1, 3, 2)
HALF = TILE // 2

NT = (((1,), (1,)), ((), ()))
NN = (((1,), (0,)), ((), ()))


def dot(a, b, dims):
    return lax.dot_general(a, b, dims, preferred_element_type=jnp.float32)


def load_queries(place, qg, q5_s, g5_s):
    for j in range(4):
        y1_at, core_at = place[0] ^ (j // 2), place[1] ^ (j % 2)
        q5_s[y1_at, :, core_at] = qg[j][:, 0]
        g5_s[y1_at, :, core_at] = qg[j][:, 1]
    return q5_s.reshape(2048, DH), g5_s.reshape(2048, DH)


def stats_kernel(*refs):
    place, qg, kv = refs[0], refs[1:5], refs[5:9]
    bias_ref = refs[9]
    stat_ref, out_ref, e_ref = refs[10:13]
    q5_s, g5_s, k_s, vt_s, xa_s, xb_s = refs[13:19]
    q_s, g_s = load_queries(place, qg, q5_s, g5_s)
    for j in range(4):
        rows = slice(j * 512, (j + 1) * 512)
        k_s[rows] = kv[j][:, 0].reshape(512, DH)
        vt_s[:, rows] = kv[j][:, 1].reshape(512, DH).T

    def score(qb, x_s):
        start = pl.multiple_of(qb * QB, QB)
        q = q_s[pl.ds(start, QB)]
        top = jnp.full((1, QB), NEG, jnp.float32)
        for c in range(4):
            s = dot(k_s[c * KC:(c + 1) * KC], q, NT) * C1
            bias = bias_ref[c * 8:(c + 1) * 8, pl.ds(start, QB)]
            x = (s.reshape(8, HALF, QB) + bias[:, None, :]).reshape(KC, QB)
            x_s[c * KC:(c + 1) * KC] = x
            top = jnp.maximum(top, jnp.max(x, axis=0, keepdims=True))
        return top

    def finish(qb, x_s, top):
        start = pl.multiple_of(qb * QB, QB)
        mass = jnp.zeros((1, QB), jnp.float32)
        acc = jnp.zeros((DH, QB), jnp.float32)
        for c in range(4):
            rows = slice(c * KC, (c + 1) * KC)
            e = jnp.exp2(x_s[rows] - top)
            mass = mass + jnp.sum(e, axis=0, keepdims=True)
            low = e.astype(jnp.bfloat16)
            e_ref[rows, pl.ds(start, QB)] = low
            acc = acc + dot(vt_s[:, rows], low, NN)
        gt = g_s[pl.ds(start, QB)].astype(jnp.float32).T
        delta = jnp.sum(gt * acc, axis=0, keepdims=True)
        stat_ref[0, pl.ds(qb, 1)] = top
        stat_ref[1, pl.ds(qb, 1)] = mass
        stat_ref[2, pl.ds(qb, 1)] = delta
        out_ref[:, pl.ds(start, QB)] = acc

    def pair(i, top):
        top_b = score(2 * i + 1, xb_s)
        finish(2 * i, xa_s, top)
        top_a = score(jnp.minimum(2 * i + 2, 7), xa_s)
        finish(2 * i + 1, xb_s, top_b)
        return top_a

    lax.fori_loop(0, 4, pair, score(0, xa_s), unroll=2)


def grad_kernel(*refs):
    place, qg, kv = refs[0], refs[1:5], refs[5:9]
    e_ref, acc_ref = refs[9:11]
    stats = refs[11:15]
    keep_ref, send_ref, dk_ref, dv_ref = refs[15:19]
    q5_s, g5_s, o5_s, dq5_s, v_s, kt_s, dk_s, dv_s, delta_s, fade_s = refs[19:29]
    q_s, g_s = load_queries(place, qg, q5_s, g5_s)
    o_s, dq_s = o5_s.reshape(2048, DH), dq5_s.reshape(2048, DH)
    for j in range(4):
        rows = slice(j * 512, (j + 1) * 512)
        kt_s[:, rows] = kv[j][:, 0].reshape(512, DH).T
        v_s[rows] = kv[j][:, 1].reshape(512, DH)
    tops, masses, deltas = [[s[n] for s in stats] for n in range(3)]
    top = jnp.maximum(jnp.maximum(tops[0], tops[1]), jnp.maximum(tops[2], tops[3]))
    fades = [jnp.exp2(t - top) for t in tops]
    mass = sum(m * f for m, f in zip(masses, fades))
    inv_mass = 1.0 / mass
    delta_s[...] = sum(d * f for d, f in zip(deltas, fades)) * inv_mass
    fade_s[...] = fades[0] * inv_mass
    dk_s[...] = jnp.zeros_like(dk_s)
    dv_s[...] = jnp.zeros_like(dv_s)

    def block(qb, carry):
        start = pl.multiple_of(qb * QB, QB)
        q = q_s[pl.ds(start, QB)]
        g = g_s[pl.ds(start, QB)]
        delta = delta_s[pl.ds(qb, 1)]
        fade = fade_s[pl.ds(qb, 1)]
        gf = (g.astype(jnp.float32).T * fade).T.astype(jnp.bfloat16)
        out = acc_ref[:, pl.ds(start, QB)] * fade
        o_s[pl.ds(start, QB)] = out.T.astype(jnp.bfloat16)
        dqt = jnp.zeros((DH, QB), jnp.float32)
        for c in range(4):
            rows = slice(c * KC, (c + 1) * KC)
            e = e_ref[rows, pl.ds(start, QB)]
            dp = dot(v_s[rows], g, NT)
            ds = (e.astype(jnp.float32) * ((dp - delta) * fade)).astype(jnp.bfloat16)
            dv_s[rows] += dot(e, gf, NN)
            dk_s[rows] += dot(ds, q, NN)
            dqt = dqt + dot(kt_s[:, rows], ds, NN)
        dq_s[pl.ds(start, QB)] = (dqt * SCALE).T.astype(jnp.bfloat16)
        return carry

    lax.fori_loop(0, 8, block, 0, unroll=8)
    for n, rows5 in enumerate((o5_s, dq5_s)):
        for far in range(2):
            keep_ref[n, far] = rows5[place[0] ^ far, :, place[1]]
            send_ref[n, far] = rows5[place[0] ^ far, :, 1 - place[1]]
    dk_ref[...] = (dk_s[...] * SCALE).astype(jnp.bfloat16)
    dv_ref[...] = dv_s[...].astype(jnp.bfloat16)


VM = pl.BlockSpec(memory_space=pltpu.VMEM)
SM = pl.BlockSpec(memory_space=pltpu.SMEM)
PARAMS = pltpu.CompilerParams(vmem_limit_bytes=16 * 1024 * 1024)
ROWS5 = pltpu.VMEM((2, 16, 2, 32, DH), jnp.bfloat16)


def run_stats(place, qg, kv, bias):
    return pl.pallas_call(
        stats_kernel,
        out_shape=(
            jax.ShapeDtypeStruct((3, 8, QB), jnp.float32),
            jax.ShapeDtypeStruct((DH, 2048), jnp.float32),
            jax.ShapeDtypeStruct((2048, 2048), jnp.bfloat16),
        ),
        in_specs=[SM] + [VM] * 9,
        out_specs=(VM,) * 3,
        scratch_shapes=[ROWS5] * 2
        + [pltpu.VMEM((2048, DH), jnp.bfloat16), pltpu.VMEM((DH, 2048), jnp.bfloat16)]
        + [pltpu.VMEM((2048, QB), jnp.float32)] * 2,
        compiler_params=PARAMS,
        name="stats",
    )(place, *qg, *kv, bias)


def run_grads(place, qg, kv, e, acc, stats):
    side = jax.ShapeDtypeStruct((2, 2, 16, 32, DH), jnp.bfloat16)
    keys = jax.ShapeDtypeStruct((2048, DH), jnp.bfloat16)
    return pl.pallas_call(
        grad_kernel,
        out_shape=(side, side, keys, keys),
        in_specs=[SM] + [VM] * 14,
        out_specs=(VM,) * 4,
        scratch_shapes=[ROWS5] * 4
        + [pltpu.VMEM((2048, DH), jnp.bfloat16), pltpu.VMEM((DH, 2048), jnp.bfloat16)]
        + [pltpu.VMEM((2048, DH), jnp.float32)] * 2
        + [pltpu.VMEM((8, QB), jnp.float32)] * 2,
        compiler_params=PARAMS,
        name="grads",
    )(place, *qg, *kv, e, acc, *stats)


def ring(n, k):
    return [(i, (i + k) % n) for i in range(n)]


SWAP = [(0, 1), (1, 0)]
HEADS = ("y0", "z")


def per_device(queries, key_vectors, value_vectors, out_grad, key_tiles, tile_count):
    x_at, y1_at, core_at = [lax.axis_index(a) for a in ("x", "y1", "core")]
    head_at = lax.axis_index("y0") * 8 + lax.axis_index("z")
    place = jnp.stack([y1_at, core_at]).astype(jnp.int32)

    back = jnp.array(BACK, jnp.int32)
    tiles = jnp.arange(16, dtype=jnp.int32)
    k_tiles = (((x_at - back) % 4)[:, None] * 16 + y1_at * 8 + tiles[None, :8]).reshape(32)
    slots = key_tiles.shape[2]
    lists = lax.dynamic_slice(key_tiles, (head_at, x_at * 16, 0), (1, 16, slots))[0]
    counts = lax.dynamic_slice(tile_count, (head_at, x_at * 16), (1, 16))[0]
    live = jnp.arange(slots, dtype=jnp.int32)[None, :] < counts[:, None]
    lists = jnp.where(live, lists, -1)
    hit = jnp.any(lists[None, :, :] == k_tiles[:, None, None], axis=2)
    bias = jnp.repeat(jnp.where(hit, 0.0, NEG).astype(jnp.float32), TILE, axis=1)

    def by_head(a):
        return a.reshape(32, 16, DH).transpose(1, 0, 2)

    packed = jnp.stack(
        [by_head(queries), by_head(out_grad), by_head(key_vectors), by_head(value_vectors)], axis=1
    )
    got = lax.all_to_all(packed, HEADS, split_axis=0, concat_axis=0, tiled=True)
    got, bias = lax.optimization_barrier((got, bias))
    qg_own, kv_own = got[:, 0:2], got[:, 2:4]
    kv = [kv_own] + [lax.ppermute(kv_own, "x", ring(4, k)) for k in SHIFTS]
    qg_far = lax.ppermute(qg_own, "y1", SWAP)
    qg = [
        qg_own,
        lax.ppermute(qg_own, "core", SWAP),
        qg_far,
        lax.ppermute(qg_far, "core", SWAP),
    ]
    stat, acc, e = run_stats(place, qg, kv, bias)
    stats = [
        stat,
        lax.ppermute(stat, "core", SWAP),
        lax.ppermute(stat, "y1", SWAP),
        lax.ppermute(stat, ("core", "y1"), [(i, 3 - i) for i in range(4)]),
    ]
    keep, away, dk, dv = run_grads(place, qg, kv, e, acc, stats)

    def pair(a, b, j):
        rows = slice(512 * j, 512 * (j + 1))
        return jnp.stack([a[rows], b[rows]])

    came = [lax.ppermute(pair(dk, dv, j), "x", ring(4, -k)) for j, k in enumerate(BACK) if j]
    near, far = add_core(keep, lax.ppermute(away, "core", SWAP))
    send = add_up(dk, dv, came, near, lax.ppermute(far, "y1", SWAP))
    back_home = lax.all_to_all(send, HEADS, split_axis=0, concat_axis=0, tiled=True)
    return unpack(back_home)


def add_core_kernel(keep_ref, came_ref, near_ref, far_ref):
    for n in range(2):
        for far, out in enumerate((near_ref, far_ref)):
            total = keep_ref[n, far].astype(jnp.float32) + came_ref[n, far].astype(jnp.float32)
            out[n] = total.astype(out.dtype)


def add_core(keep, came):
    return pl.pallas_call(
        add_core_kernel,
        out_shape=(
            jax.ShapeDtypeStruct((2, 16, 32, DH), jnp.float32),
            jax.ShapeDtypeStruct((2, 16, 32, DH), jnp.bfloat16),
        ),
        in_specs=[VM] * 2,
        out_specs=(VM,) * 2,
        compiler_params=PARAMS,
        name="add_core",
    )(keep, came)


def add_kernel(dk_ref, dv_ref, *refs):
    came, near_ref, far_ref, send_ref = refs[0:3], refs[3], refs[4], refs[5]
    for n in range(2):
        rows = near_ref[n] + far_ref[n].astype(jnp.float32)
        send_ref[:, n] = rows.astype(jnp.bfloat16)
    for n, own in enumerate((dk_ref, dv_ref)):
        total = own[0:512].astype(jnp.float32)
        for part in came:
            total = total + part[n].astype(jnp.float32)
        send_ref[:, 2 + n] = total.astype(jnp.bfloat16).reshape(16, 32, DH)


def add_up(dk, dv, came, near, far):
    return pl.pallas_call(
        add_kernel,
        out_shape=jax.ShapeDtypeStruct((16, 4, 32, DH), jnp.bfloat16),
        in_specs=[VM] * 7,
        out_specs=VM,
        compiler_params=PARAMS,
        name="add_up",
    )(dk, dv, *came, near, far)


def unpack_kernel(src_ref, *outs):
    for n, out in enumerate(outs):
        for h in range(16):
            out[:, h * DH:(h + 1) * DH] = src_ref[h, n]


def unpack(a):
    rows = jax.ShapeDtypeStruct((32, 16 * DH), jnp.bfloat16)
    return pl.pallas_call(
        unpack_kernel,
        out_shape=(rows,) * 4,
        in_specs=[VM],
        out_specs=(VM,) * 4,
        compiler_params=PARAMS,
        name="unpack",
    )(a)


def solution(mesh):
    grid = jax.sharding.Mesh(mesh.devices.reshape(8, 2, 4, 2, 2), ("z", "core", "x", "y1", "y0"))
    rows = P(("x", "y1", "y0", "z", "core"), None)
    return jax.shard_map(
        per_device,
        mesh=grid,
        in_specs=(rows, rows, rows, rows, P(), P()),
        out_specs=(rows,) * 4,
        check_vma=False,
    )
```

time: 121 us -> 108 us (0.89); the launches traced: 121 us -> 106 us
  blocking collectives: 25.2 us -> 17 us
  waiting for transfers between devices: 39.2 us -> 32.9 us
  starting transfers between devices: 28.6 us -> 32.5 us
  local copies, waits for them, and re-layouts: 6.42 us -> 3.42 us
  Pallas kernels: 18.6 us -> 17.1 us
    all_to_all x1, blocking collectives: 25.2 us -> 17 us  [per_device(): lax.all_to_all(send, HEADS, split_axis=0, concat_axis=0, tiled=True)]
    ppermute x12 -> x11, waiting for transfers between devices: 19.2 us -> 11.8 us  [the longest x3 9.77 us: per_device(): lax.ppermute(pair(dk, dv, j), 'x', ring(4, -k))]
    ppermute x3, waiting for transfers between devices: 3.61 us -> 10.2 us  [per_device(): kv = [kv_own] + [lax.ppermute(kv_own, 'x', ring(4, k)) for k in SHIFTS]]
    all_to_all x1, waiting for transfers between devices: 16.4 us -> 10.9 us  [per_device(): got = lax.all_to_all(packed, HEADS, split_axis=0, concat_axis=0, tiled=True)]
    ppermute x12 -> x11, starting transfers between devices: 14.2 us -> 18.1 us  [the longest x3 4.37 us: per_device(): lax.ppermute(pair(dk, dv, j), 'x', ring(4, -k))]
    reshape x4 -> x0, local copies, waits for them, and re-layouts: 2.71 us -> none  [by_row(): return a.transpose(1, 0, 2).reshape(32, 16 * DH)]
    pallas_call x1 -> x4, Pallas kernels: 12.4 us -> 10.1 us  [the longest x1 8.9 us: run_grads(): pl.pallas_call(grad_kernel, out_shape=(side, side, keys, keys), in_specs=...]
  transfers between devices with their start and end apart: 16 -> 15, of which waited for: 13 -> 8; matrix products, arithmetic and copies ran while one was open for 2% -> 3% of each run, Pallas kernels for 0% -> 0%
where the time goes in v2:
time: 108 us; the launch traced here: 106 us
  waiting for transfers between devices  32.9 us (30%)
  starting transfers between devices  32.5 us (30%)
  Pallas kernels  17.1 us (16%)
  blocking collectives  17 us (16%)
  local copies, waits for them, and re-layouts  3.42 us (3%)
  other arithmetic  2.55 us (2%)
    all_to_all x1, blocking collectives, per_device(): lax.all_to_all(send, HEADS, split_axis=0, concat_axis=0, tiled=True)  17 us
    all_to_all x1, waiting for transfers between devices, per_device(): got = lax.all_to_all(packed, HEADS, split_axis=0, concat_axis=0, tiled=True)  10.9 us
    ppermute x3, waiting for transfers between devices, per_device(): kv = [kv_own] + [lax.ppermute(kv_own, 'x', ring(4, k)) for k in SHIFTS]  10.2 us
    all_to_all x1, starting transfers between devices, per_device(): got = lax.all_to_all(packed, HEADS, split_axis=0, concat_axis=0, tiled=True)  10.1 us
    ppermute x3, waiting for transfers between devices, per_device(): lax.ppermute(pair(dk, dv, j), 'x', ring(4, -k))  9.77 us
    pallas_call x1, Pallas kernels, run_grads(): pl.pallas_call(grad_kernel, out_shape=(side, side, keys, keys), in_specs=...  8.9 us
    pallas_call x1, Pallas kernels, run_stats(): pl.pallas_call(stats_kernel, out_shape=(jax.ShapeDtypeStruct((3, 8, QB),...  7.06 us
    ppermute x3, starting transfers between devices, per_device(): lax.ppermute(pair(dk, dv, j), 'x', ring(4, -k))  4.37 us
  transfers between devices with their start and end apart: 15, of which 8 were waited for; matrix products, arithmetic and copies ran while one was open for 3% of the time, Pallas kernels for 0%

profile of v2, /device:TPU:1, one launch (start us, length us, event | category | flops | bytes accessed | tf_op | source)
XLA Modules:
  0.0 106.3 jit_solution(17943512001970434622)
XLA Ops:
  0.6 0.0 copy-start
  0.6 1.1 bitcast_bitcast_fusion.2
  1.7 1.0 bitcast_bitcast_fusion
  2.7 0.9 pad_maximum_fusion
  3.6 10.1 %all-to-all-start = ((bf16[16,4,32,128]{3,2,1,0:T(8,128)(2,1)}), bf16[16,4,32,128]{3,2,1,0:T(8,128)(2,1)S(1)}, u32[]{:S(2)}, u32[]{:S(2)}) async-start(bf16[16,4,32,128]{3,2,1,0:T(8,128)(2,1)} %pad_maximum_fusion), calls=%async_computation | async-start | bytes 1048576 | tf_op jit(solution)/shard_map/all_to_all | solution.py:213
  13.8 0.7 fusion.2
  14.4 0.1 broadcast_add_fusion
  14.5 0.1 add.53
  14.6 0.1 constant_dynamic-slice_fusion
  14.7 0.1 copy.22
  14.8 0.8 dynamic-slice_bitcast_fusion
  15.5 0.1 select_bitcast_fusion
  15.6 0.7 compare_reduce_fusion
  16.3 0.1 broadcast_in_dim.22
  16.5 0.1 copy.33
  16.6 10.9 %all-to-all-done = bf16[16,4,32,128]{3,2,1,0:T(8,128)(2,1)S(1)} async-done(((bf16[16,4,32,128]{3,2,1,0:T(8,128)(2,1)}), bf16[16,4,32,128]{3,2,1,0:T(8,128)(2,1)S(1)}, u32[]{:S(2)}, u32[]{:S(2)}) %all-to-all-start) | async-done | bytes 524320 | tf_op jit(solution)/shard_map/all_to_all | solution.py:213
  27.5 2.7 %collective-permute-start.1 = (bf16[16,2,32,128]{3,2,1,0:T(8,128)(2,1)S(1)}, bf16[16,2,32,128]{3,2,1,0:T(8,128)(2,1)S(1)}, u32[]{:S(2)}, u32[]{:S(2)}) collective-permute-start(bf16[16,2,32,128]{3,2,1,0:T(8,128)(2,1)S(1)} %get-tuple-element.33.refs_1_), channel_id=1, source_target_pairs={{0,2},{2,0},{1,3},{3,1},{4,6},{6,4},{5,7},{7,5},{8,10},{10,8},{9,1... | collective-permute-start | bytes 786440 | tf_op jit(solution)/shard_map/ppermute | solution.py:217
  30.2 3.2 %collective-permute-start = (bf16[16,2,32,128]{3,2,1,0:T(8,128)(2,1)S(1)}, bf16[16,2,32,128]{3,2,1,0:T(8,128)(2,1)S(1)}, u32[]{:S(2)}, u32[]{:S(2)}) collective-permute-start(bf16[16,2,32,128]{3,2,1,0:T(8,128)(2,1)S(1)} %get-tuple-element.33.refs_1_), channel_id=1, source_target_pairs={{0,16},{16,0},{1,17},{17,1},{2,18},{18,2},{3,19},{19,3},{4,20},{20... | collective-permute-start | bytes 786440 | tf_op jit(solution)/shard_map/ppermute | solution.py:220
  33.4 2.7 %collective-permute-start.5 = (bf16[16,2,32,128]{3,2,1,0:T(8,128)(2,1)S(1)}, bf16[16,2,32,128]{3,2,1,0:T(8,128)(2,1)S(1)}, u32[]{:S(2)}, u32[]{:S(2)}) collective-permute-start(bf16[16,2,32,128]{3,2,1,0:T(8,128)(2,1)S(1)} %get-tuple-element.32.refs_5_), channel_id=1, source_target_pairs={{0,8},{4,12},{8,0},{12,4},{1,9},{5,13},{9,1},{13,5},{2,10},{6,14},... | collective-permute-start | bytes 786440 | tf_op jit(solution)/shard_map/ppermute | solution.py:216
  36.2 0.9 collective-permute-start.4
  37.0 0.6 collective-permute-start.3
  37.6 0.8 collective-permute-start.2
  38.5 0.1 pad_add_fusion.refs_0_
  38.6 0.0 collective-permute-done.refs_2_
  38.6 4.3 %collective-permute-done.5.refs_8_ = bf16[16,2,32,128]{3,2,1,0:T(8,128)(2,1)S(1)} collective-permute-done((bf16[16,2,32,128]{3,2,1,0:T(8,128)(2,1)S(1)}, bf16[16,2,32,128]{3,2,1,0:T(8,128)(2,1)S(1)}, u32[]{:S(2)}, u32[]{:S(2)}) %collective-permute-start.5) | collective-permute-done | bytes 262176 | tf_op jit(solution)/shard_map/ppermute | solution.py:216
  42.9 5.7 %collective-permute-done.4.refs_7_ = bf16[16,2,32,128]{3,2,1,0:T(8,128)(2,1)S(1)} collective-permute-done((bf16[16,2,32,128]{3,2,1,0:T(8,128)(2,1)S(1)}, bf16[16,2,32,128]{3,2,1,0:T(8,128)(2,1)S(1)}, u32[]{:S(2)}, u32[]{:S(2)}) %collective-permute-start.4) | collective-permute-done | bytes 262176 | tf_op jit(solution)/shard_map/ppermute | solution.py:216
  48.6 0.2 collective-permute-done.3.refs_6_
  48.8 0.0 collective-permute-done.2.refs_4_
  48.8 7.1 %stats.1 = (f32[3,8,256]{2,1,0:T(8,128)S(1)}, f32[128,2048]{1,0:T(8,128)S(1)}, bf16[2048,2048]{1,0:T(8,128)(2,1)S(1)}) custom-call(s32[2]{0:T(128)S(1)} %pad_add_fusion.refs_0_, bf16[16,2,32,128]{3,2,1,0:T(8,128)(2,1)S(1)} %get-tuple-element.33.refs_1_, bf16[16,2,32,128]{3,2,1,0:T(8,128)(2,1)S(1)} %collective-permute-done.refs_2_, ...), custom_call_target="tpu_custom_call" | custom-call | tf_op jit(solution)/shard_map/stats/pallas_call | solution.py:149
  55.8 0.9 collective-permute-start.8
  56.8 2.6 %collective-permute-start.7 = (f32[3,8,256]{2,1,0:T(8,128)S(1)}, f32[3,8,256]{2,1,0:T(8,128)S(1)}, u32[]{:S(2)}, u32[]{:S(2)}) collective-permute-start(f32[3,8,256]{2,1,0:T(8,128)S(1)} %get-tuple-element.19.refs_11_), channel_id=1, source_target_pairs={{0,2},{2,0},{1,3},{3,1},{4,6},{6,4},{5,7},{7,5},{8,10},{10,8},{9,1... | collective-permute-start | bytes 73736 | tf_op jit(solution)/shard_map/ppermute | solution.py:228
  59.4 0.2 collective-permute-start.6
  59.6 1.5 %collective-permute-done.8.refs_14_ = f32[3,8,256]{2,1,0:T(8,128)S(1)} collective-permute-done((f32[3,8,256]{2,1,0:T(8,128)S(1)}, f32[3,8,256]{2,1,0:T(8,128)S(1)}, u32[]{:S(2)}, u32[]{:S(2)}) %collective-permute-start.8) | collective-permute-done | bytes 24608 | tf_op jit(solution)/shard_map/ppermute | solution.py:229
  61.1 0.5 collective-permute-done.7.refs_13_
  61.6 0.0 collective-permute-done.6.refs_12_
  61.6 8.9 %grads.1 = (bf16[2,2,16,32,128]{4,3,2,1,0:T(8,128)(2,1)S(1)}, bf16[2,2,16,32,128]{4,3,2,1,0:T(8,128)(2,1)S(1)}, bf16[2048,128]{1,0:T(8,128)(2,1)S(1)}, bf16[2048,128]{1,0:T(8,128)(2,1)S(1)}) custom-call(s32[2]{0:T(128)S(1)} %pad_add_fusion.refs_0_, bf16[16,2,32,128]{3,2,1,0:T(8,128)(2,1)S(1)} %get-tuple-element.33.refs_1_, ...), custom_call_target="tpu_custom_call" | custom-call | tf_op jit(solution)/shard_map/grads/pallas_call | solution.py:169
  70.5 0.6 collective-permute-start.12
  71.2 2.5 %collective-permute-start.9 = (bf16[2,512,128]{2,1,0:T(8,128)(2,1)S(1)}, bf16[2,512,128]{2,1,0:T(8,128)(2,1)S(1)}, u32[]{:S(2)}, u32[]{:S(2)}) collective-permute-start(bf16[2,512,128]{2,1,0:T(8,128)(2,1)S(1)} %pad_maximum_fusion.1), channel_id=1, source_target_pairs={{0,12},{4,0},{8,4},{12,8},{1,13},{5,1},{9,5},{13,9},{2,14},{6,2},{... | collective-permute-start | bytes 786440 | tf_op jit(solution)/shard_map/ppermute | solution.py:237
  73.7 0.1 collective-permute-start.10
  73.9 1.8 %collective-permute-start.11 = (bf16[2,512,128]{2,1,0:T(8,128)(2,1)S(1)}, bf16[2,512,128]{2,1,0:T(8,128)(2,1)S(1)}, u32[]{:S(2)}, u32[]{:S(2)}) collective-permute-start(bf16[2,512,128]{2,1,0:T(8,128)(2,1)S(1)} %pad_maximum_fusion.3), channel_id=1, source_target_pairs={{0,8},{4,12},{8,0},{12,4},{1,9},{5,13},{9,1},{13,5},{2,10},{6,14},... | collective-permute-start | bytes 786440 | tf_op jit(solution)/shard_map/ppermute | solution.py:237
  75.7 0.1 add_core.1
  75.8 2.7 %collective-permute-start.13 = (bf16[2,16,32,128]{3,2,1,0:T(8,128)(2,1)S(1)}, bf16[2,16,32,128]{3,2,1,0:T(8,128)(2,1)S(1)}, u32[]{:S(2)}, u32[]{:S(2)}) collective-permute-start(bf16[2,16,32,128]{3,2,1,0:T(8,128)(2,1)S(1)} %get-tuple-element.25), channel_id=1, source_target_pairs={{0,2},{2,0},{1,3},{3,1},{4,6},{6,4},{5,7},{7,5},{8,10},{10,8},{9,1... | collective-permute-start | bytes 786440 | tf_op jit(solution)/shard_map/ppermute | solution.py:239
  78.5 6.4 %collective-permute-done.9.refs_0_ = bf16[2,512,128]{2,1,0:T(8,128)(2,1)S(1)} collective-permute-done((bf16[2,512,128]{2,1,0:T(8,128)(2,1)S(1)}, bf16[2,512,128]{2,1,0:T(8,128)(2,1)S(1)}, u32[]{:S(2)}, u32[]{:S(2)}) %collective-permute-start.9) | collective-permute-done | bytes 262176 | tf_op jit(solution)/shard_map/ppermute | solution.py:237
  84.9 3.3 %collective-permute-done.10.refs_1_ = bf16[2,512,128]{2,1,0:T(8,128)(2,1)S(1)} collective-permute-done((bf16[2,512,128]{2,1,0:T(8,128)(2,1)S(1)}, bf16[2,512,128]{2,1,0:T(8,128)(2,1)S(1)}, u32[]{:S(2)}, u32[]{:S(2)}) %collective-permute-start.10) | collective-permute-done | bytes 262176 | tf_op jit(solution)/shard_map/ppermute | solution.py:237
  88.2 0.0 collective-permute-done.11.refs_2_
  88.2 0.2 add_up.1
  88.4 17.0 %all_to_all.10.src_ref = bf16[16,4,32,128]{3,2,1,0:T(8,128)(2,1)S(1)} all-to-all(bf16[16,4,32,128]{3,2,1,0:T(8,128)(2,1)S(1)} %add_up.1), channel_id=1, replica_groups=mesh['z'=8,'core'=2,'x'=4,'y1'=2,'y0'=2] {'y0','z'}, dimensions={0} | all-to-all | bytes 1048576 | tf_op jit(solution)/shard_map/all_to_all | solution.py:240
  105.5 0.9 unpack.1
  (12 shorter events, 0.2 us)
Async XLA Ops:
  0.6 14.0 %copy-start = (s32[16,64,38]{1,0,2:T(8,128)S(1)}, s32[16,64,38]{1,0,2:T(8,128)}, u32[]{:S(2)}) copy-start(s32[16,64,38]{1,0,2:T(8,128)} %param.11) | copy-start | bytes 466948
  3.6 23.9 %all-to-all-start = ((bf16[16,4,32,128]{3,2,1,0:T(8,128)(2,1)}), bf16[16,4,32,128]{3,2,1,0:T(8,128)(2,1)S(1)}, u32[]{:S(2)}, u32[]{:S(2)}) async-start(bf16[16,4,32,128]{3,2,1,0:T(8,128)(2,1)} %pad_maximum_fusion), calls=%async_computation | async-start | bytes 1048576 | tf_op jit(solution)/shard_map/all_to_all | solution.py:213
  27.5 10.1 %collective-permute-start.1 = (bf16[16,2,32,128]{3,2,1,0:T(8,128)(2,1)S(1)}, bf16[16,2,32,128]{3,2,1,0:T(8,128)(2,1)S(1)}, u32[]{:S(2)}, u32[]{:S(2)}) collective-permute-start(bf16[16,2,32,128]{3,2,1,0:T(8,128)(2,1)S(1)} %get-tuple-element.33.refs_1_), channel_id=1, source_target_pairs={{0,2},{2,0},{1,3},{3,1},{4,6},{6,4},{5,7},{7,5},{8,10},{10,8},{9,1... | collective-permute-start | bytes 786440 | tf_op jit(solution)/shard_map/ppermute | solution.py:217
  30.2 8.3 %collective-permute-start = (bf16[16,2,32,128]{3,2,1,0:T(8,128)(2,1)S(1)}, bf16[16,2,32,128]{3,2,1,0:T(8,128)(2,1)S(1)}, u32[]{:S(2)}, u32[]{:S(2)}) collective-permute-start(bf16[16,2,32,128]{3,2,1,0:T(8,128)(2,1)S(1)} %get-tuple-element.33.refs_1_), channel_id=1, source_target_pairs={{0,16},{16,0},{1,17},{17,1},{2,18},{18,2},{3,19},{19,3},{4,20},{20... | collective-permute-start | bytes 786440 | tf_op jit(solution)/shard_map/ppermute | solution.py:220
  33.4 9.5 %collective-permute-start.5 = (bf16[16,2,32,128]{3,2,1,0:T(8,128)(2,1)S(1)}, bf16[16,2,32,128]{3,2,1,0:T(8,128)(2,1)S(1)}, u32[]{:S(2)}, u32[]{:S(2)}) collective-permute-start(bf16[16,2,32,128]{3,2,1,0:T(8,128)(2,1)S(1)} %get-tuple-element.32.refs_5_), channel_id=1, source_target_pairs={{0,8},{4,12},{8,0},{12,4},{1,9},{5,13},{9,1},{13,5},{2,10},{6,14},... | collective-permute-start | bytes 786440 | tf_op jit(solution)/shard_map/ppermute | solution.py:216
  36.2 12.4 %collective-permute-start.4 = (bf16[16,2,32,128]{3,2,1,0:T(8,128)(2,1)S(1)}, bf16[16,2,32,128]{3,2,1,0:T(8,128)(2,1)S(1)}, u32[]{:S(2)}, u32[]{:S(2)}) collective-permute-start(bf16[16,2,32,128]{3,2,1,0:T(8,128)(2,1)S(1)} %get-tuple-element.32.refs_5_), channel_id=1, source_target_pairs={{0,12},{4,0},{8,4},{12,8},{1,13},{5,1},{9,5},{13,9},{2,14},{6,2},{... | collective-permute-start | bytes 786440 | tf_op jit(solution)/shard_map/ppermute | solution.py:216
  37.0 11.7 %collective-permute-start.3 = (bf16[16,2,32,128]{3,2,1,0:T(8,128)(2,1)S(1)}, bf16[16,2,32,128]{3,2,1,0:T(8,128)(2,1)S(1)}, u32[]{:S(2)}, u32[]{:S(2)}) collective-permute-start(bf16[16,2,32,128]{3,2,1,0:T(8,128)(2,1)S(1)} %get-tuple-element.32.refs_5_), channel_id=1, source_target_pairs={{0,4},{4,8},{8,12},{12,0},{1,5},{5,9},{9,13},{13,1},{2,6},{6,10},{... | collective-permute-start | bytes 786440 | tf_op jit(solution)/shard_map/ppermute | solution.py:216
  37.6 11.1 %collective-permute-start.2 = (bf16[16,2,32,128]{3,2,1,0:T(8,128)(2,1)S(1)}, bf16[16,2,32,128]{3,2,1,0:T(8,128)(2,1)S(1)}, u32[]{:S(2)}, u32[]{:S(2)}) collective-permute-start(bf16[16,2,32,128]{3,2,1,0:T(8,128)(2,1)S(1)} %collective-permute-done.1.refs_3_), channel_id=1, source_target_pairs={{0,16},{16,0},{1,17},{17,1},{2,18},{18,2},{3,19},{19,3},{4,20},{20... | collective-permute-start | bytes 786440 | tf_op jit(solution)/shard_map/ppermute | solution.py:222
  55.8 5.3 %collective-permute-start.8 = (f32[3,8,256]{2,1,0:T(8,128)S(1)}, f32[3,8,256]{2,1,0:T(8,128)S(1)}, u32[]{:S(2)}, u32[]{:S(2)}) collective-permute-start(f32[3,8,256]{2,1,0:T(8,128)S(1)} %get-tuple-element.19.refs_11_), channel_id=1, source_target_pairs={{0,18},{2,16},{16,2},{18,0},{1,19},{3,17},{17,3},{19,1},{4,22},{6,... | collective-permute-start | bytes 73736 | tf_op jit(solution)/shard_map/ppermute | solution.py:229
  56.8 4.8 %collective-permute-start.7 = (f32[3,8,256]{2,1,0:T(8,128)S(1)}, f32[3,8,256]{2,1,0:T(8,128)S(1)}, u32[]{:S(2)}, u32[]{:S(2)}) collective-permute-start(f32[3,8,256]{2,1,0:T(8,128)S(1)} %get-tuple-element.19.refs_11_), channel_id=1, source_target_pairs={{0,2},{2,0},{1,3},{3,1},{4,6},{6,4},{5,7},{7,5},{8,10},{10,8},{9,1... | collective-permute-start | bytes 73736 | tf_op jit(solution)/shard_map/ppermute | solution.py:228
  59.4 2.2 %collective-permute-start.6 = (f32[3,8,256]{2,1,0:T(8,128)S(1)}, f32[3,8,256]{2,1,0:T(8,128)S(1)}, u32[]{:S(2)}, u32[]{:S(2)}) collective-permute-start(f32[3,8,256]{2,1,0:T(8,128)S(1)} %get-tuple-element.19.refs_11_), channel_id=1, source_target_pairs={{0,16},{16,0},{1,17},{17,1},{2,18},{18,2},{3,19},{19,3},{4,20},{20... | collective-permute-start | bytes 73736 | tf_op jit(solution)/shard_map/ppermute | solution.py:227
  70.5 5.1 %collective-permute-start.12 = (bf16[2,2,16,32,128]{4,3,2,1,0:T(8,128)(2,1)S(1)}, bf16[2,2,16,32,128]{4,3,2,1,0:T(8,128)(2,1)S(1)}, u32[]{:S(2)}, u32[]{:S(2)}) collective-permute-start(bf16[2,2,16,32,128]{4,3,2,1,0:T(8,128)(2,1)S(1)} %get-tuple-element.23), channel_id=1, source_target_pairs={{0,16},{16,0},{1,17},{17,1},{2,18},{18,2},{3,19},{19,3},{4,20},{20... | collective-permute-start | bytes 1572872 | tf_op jit(solution)/shard_map/ppermute | solution.py:238
  71.2 13.7 %collective-permute-start.9 = (bf16[2,512,128]{2,1,0:T(8,128)(2,1)S(1)}, bf16[2,512,128]{2,1,0:T(8,128)(2,1)S(1)}, u32[]{:S(2)}, u32[]{:S(2)}) collective-permute-start(bf16[2,512,128]{2,1,0:T(8,128)(2,1)S(1)} %pad_maximum_fusion.1), channel_id=1, source_target_pairs={{0,12},{4,0},{8,4},{12,8},{1,13},{5,1},{9,5},{13,9},{2,14},{6,2},{... | collective-permute-start | bytes 786440 | tf_op jit(solution)/shard_map/ppermute | solution.py:237
  73.7 14.5 %collective-permute-start.10 = (bf16[2,512,128]{2,1,0:T(8,128)(2,1)S(1)}, bf16[2,512,128]{2,1,0:T(8,128)(2,1)S(1)}, u32[]{:S(2)}, u32[]{:S(2)}) collective-permute-start(bf16[2,512,128]{2,1,0:T(8,128)(2,1)S(1)} %pad_maximum_fusion.2), channel_id=1, source_target_pairs={{0,4},{4,8},{8,12},{12,0},{1,5},{5,9},{9,13},{13,1},{2,6},{6,10},{... | collective-permute-start | bytes 786440 | tf_op jit(solution)/shard_map/ppermute | solution.py:237
  73.9 14.4 %collective-permute-start.11 = (bf16[2,512,128]{2,1,0:T(8,128)(2,1)S(1)}, bf16[2,512,128]{2,1,0:T(8,128)(2,1)S(1)}, u32[]{:S(2)}, u32[]{:S(2)}) collective-permute-start(bf16[2,512,128]{2,1,0:T(8,128)(2,1)S(1)} %pad_maximum_fusion.3), channel_id=1, source_target_pairs={{0,8},{4,12},{8,0},{12,4},{1,9},{5,13},{9,1},{13,5},{2,10},{6,14},... | collective-permute-start | bytes 786440 | tf_op jit(solution)/shard_map/ppermute | solution.py:237
  75.8 12.5 %collective-permute-start.13 = (bf16[2,16,32,128]{3,2,1,0:T(8,128)(2,1)S(1)}, bf16[2,16,32,128]{3,2,1,0:T(8,128)(2,1)S(1)}, u32[]{:S(2)}, u32[]{:S(2)}) collective-permute-start(bf16[2,16,32,128]{3,2,1,0:T(8,128)(2,1)S(1)} %get-tuple-element.25), channel_id=1, source_target_pairs={{0,2},{2,0},{1,3},{3,1},{4,6},{6,4},{5,7},{7,5},{8,10},{10,8},{9,1... | collective-permute-start | bytes 786440 | tf_op jit(solution)/shard_map/ppermute | solution.py:239

commit v3 on v2

--- a/solution.py
+++ b/solution.py
@@ -19,6 +19,7 @@
 SHIFTS = (1, 3, 2)
 BACK = (0, 1, 3, 2)
 HALF = TILE // 2
+NEAR, FAR = (0, 3), (1, 2)
 
 NT = (((1,), (1,)), ((), ()))
 NN = (((1,), (0,)), ((), ()))
@@ -28,30 +29,33 @@
     return lax.dot_general(a, b, dims, preferred_element_type=jnp.float32)
 
 
-def load_queries(place, qg, q5_s, g5_s):
+def load_rows(place, qg, n, rows5_s):
     for j in range(4):
-        y1_at, core_at = place[0] ^ (j // 2), place[1] ^ (j % 2)
-        q5_s[y1_at, :, core_at] = qg[j][:, 0]
-        g5_s[y1_at, :, core_at] = qg[j][:, 1]
-    return q5_s.reshape(2048, DH), g5_s.reshape(2048, DH)
+        rows5_s[place[0] ^ (j // 2), :, place[1] ^ (j % 2)] = qg[j][:, n]
 
 
 def stats_kernel(*refs):
-    place, qg, kv = refs[0], refs[1:5], refs[5:9]
-    bias_ref = refs[9]
-    stat_ref, out_ref, e_ref = refs[10:13]
-    q5_s, g5_s, k_s, vt_s, xa_s, xb_s = refs[13:19]
-    q_s, g_s = load_queries(place, qg, q5_s, g5_s)
-    for j in range(4):
-        rows = slice(j * 512, (j + 1) * 512)
-        k_s[rows] = kv[j][:, 0].reshape(512, DH)
-        vt_s[:, rows] = kv[j][:, 1].reshape(512, DH).T
+    second = len(refs) == 15
+    if second:
+        q5_ref, g5_ref, kv, bias_ref, near_ref, near_out_ref = *refs[0:2], refs[2:4], *refs[4:7]
+        stat_ref, out_ref, e_ref, part_ref = refs[7:11]
+    else:
+        place, qg, kv, bias_ref = refs[0], refs[1:5], refs[5:7], refs[7]
+        stat_ref, out_ref, e_ref, q5_ref, g5_ref = refs[8:13]
+        load_rows(place, qg, 0, q5_ref)
+        load_rows(place, qg, 1, g5_ref)
+    q_s, g_s = q5_ref.reshape(2048, DH), g5_ref.reshape(2048, DH)
+    k_s, vt_s, xa_s, xb_s = refs[-4:]
+    for j in range(2):
+        rows = slice(j * KC, (j + 1) * KC)
+        k_s[rows] = kv[j][:, 0].reshape(KC, DH)
+        vt_s[:, rows] = kv[j][:, 1].reshape(KC, DH).T
 
     def score(qb, x_s):
         start = pl.multiple_of(qb * QB, QB)
         q = q_s[pl.ds(start, QB)]
         top = jnp.full((1, QB), NEG, jnp.float32)
-        for c in range(4):
+        for c in range(2):
             s = dot(k_s[c * KC:(c + 1) * KC], q, NT) * C1
             bias = bias_ref[c * 8:(c + 1) * 8, pl.ds(start, QB)]
             x = (s.reshape(8, HALF, QB) + bias[:, None, :]).reshape(KC, QB)
@@ -63,18 +67,26 @@
         start = pl.multiple_of(qb * QB, QB)
         mass = jnp.zeros((1, QB), jnp.float32)
         acc = jnp.zeros((DH, QB), jnp.float32)
-        for c in range(4):
+        for c in range(2):
             rows = slice(c * KC, (c + 1) * KC)
             e = jnp.exp2(x_s[rows] - top)
             mass = mass + jnp.sum(e, axis=0, keepdims=True)
             low = e.astype(jnp.bfloat16)
             e_ref[rows, pl.ds(start, QB)] = low
             acc = acc + dot(vt_s[:, rows], low, NN)
-        gt = g_s[pl.ds(start, QB)].astype(jnp.float32).T
-        delta = jnp.sum(gt * acc, axis=0, keepdims=True)
+        if second:
+            near_top = near_ref[0, pl.ds(qb, 1)]
+            new_top = jnp.maximum(near_top, top)
+            fades = jnp.exp2(near_top - new_top), jnp.exp2(top - new_top)
+            acc = near_out_ref[:, pl.ds(start, QB)] * fades[0] + acc * fades[1]
+            mass = near_ref[1, pl.ds(qb, 1)] * fades[0] + mass * fades[1]
+            gt = g_s[pl.ds(start, QB)].astype(jnp.float32).T
+            stat_ref[2, pl.ds(qb, 1)] = jnp.sum(gt * acc, axis=0, keepdims=True)
+            part_ref[0, pl.ds(qb, 1)] = fades[0]
+            part_ref[1, pl.ds(qb, 1)] = fades[1]
+            top = new_top
         stat_ref[0, pl.ds(qb, 1)] = top
         stat_ref[1, pl.ds(qb, 1)] = mass
-        stat_ref[2, pl.ds(qb, 1)] = delta
         out_ref[:, pl.ds(start, QB)] = acc
 
     def pair(i, top):
@@ -88,17 +100,15 @@
 
 
 def grad_kernel(*refs):
-    place, qg, kv = refs[0], refs[1:5], refs[5:9]
-    e_ref, acc_ref = refs[9:11]
+    place, kv, q5_ref, g5_ref = refs[0], refs[1:5], *refs[5:7]
+    e_refs, part_ref, acc_ref = refs[7:9], refs[9], refs[10]
     stats = refs[11:15]
     keep_ref, send_ref, dk_ref, dv_ref = refs[15:19]
-    q5_s, g5_s, o5_s, dq5_s, v_s, kt_s, dk_s, dv_s, delta_s, fade_s = refs[19:29]
-    q_s, g_s = load_queries(place, qg, q5_s, g5_s)
+    o5_s, dq5_s, kt_s, dk_s, dv_s, delta_s, fade_s = refs[19:26]
+    q_s, g_s = q5_ref.reshape(2048, DH), g5_ref.reshape(2048, DH)
     o_s, dq_s = o5_s.reshape(2048, DH), dq5_s.reshape(2048, DH)
     for j in range(4):
-        rows = slice(j * 512, (j + 1) * 512)
-        kt_s[:, rows] = kv[j][:, 0].reshape(512, DH).T
-        v_s[rows] = kv[j][:, 1].reshape(512, DH)
+        kt_s[:, j * KC:(j + 1) * KC] = kv[j][:, 0].reshape(KC, DH).T
     tops, masses, deltas = [[s[n] for s in stats] for n in range(3)]
     top = jnp.maximum(jnp.maximum(tops[0], tops[1]), jnp.maximum(tops[2], tops[3]))
     fades = [jnp.exp2(t - top) for t in tops]
@@ -109,28 +119,29 @@
     dk_s[...] = jnp.zeros_like(dk_s)
     dv_s[...] = jnp.zeros_like(dv_s)
 
-    def block(qb, carry):
-        start = pl.multiple_of(qb * QB, QB)
-        q = q_s[pl.ds(start, QB)]
-        g = g_s[pl.ds(start, QB)]
-        delta = delta_s[pl.ds(qb, 1)]
-        fade = fade_s[pl.ds(qb, 1)]
-        gf = (g.astype(jnp.float32).T * fade).T.astype(jnp.bfloat16)
-        out = acc_ref[:, pl.ds(start, QB)] * fade
-        o_s[pl.ds(start, QB)] = out.T.astype(jnp.bfloat16)
+    def block(qb):
+        cols = slice(qb * QB, (qb + 1) * QB)
+        q, g = q_s[cols], g_s[cols]
+        gt = g.astype(jnp.float32).T
+        delta, fade = delta_s[qb:qb + 1], fade_s[qb:qb + 1]
+        o_s[cols] = (acc_ref[:, cols] * fade).T.astype(jnp.bfloat16)
         dqt = jnp.zeros((DH, QB), jnp.float32)
-        for c in range(4):
+        for n, c in enumerate(NEAR + FAR):
             rows = slice(c * KC, (c + 1) * KC)
-            e = e_ref[rows, pl.ds(start, QB)]
-            dp = dot(v_s[rows], g, NT)
-            ds = (e.astype(jnp.float32) * ((dp - delta) * fade)).astype(jnp.bfloat16)
+            half = slice(n % 2 * KC, (n % 2 + 1) * KC)
+            if n % 2 == 0:
+                local = fade * part_ref[n // 2, qb:qb + 1]
+                gf = (gt * local).T.astype(jnp.bfloat16)
+            e = e_refs[n // 2][half, cols]
+            dp = dot(kv[c][:, 1].reshape(KC, DH), g, NT)
+            ds = (e.astype(jnp.float32) * ((dp - delta) * local)).astype(jnp.bfloat16)
             dv_s[rows] += dot(e, gf, NN)
             dk_s[rows] += dot(ds, q, NN)
             dqt = dqt + dot(kt_s[:, rows], ds, NN)
-        dq_s[pl.ds(start, QB)] = (dqt * SCALE).T.astype(jnp.bfloat16)
-        return carry
-
-    lax.fori_loop(0, 8, block, 0, unroll=8)
+        dq_s[cols] = (dqt * SCALE).T.astype(jnp.bfloat16)
+
+    for qb in range(8):
+        block(qb)
     for n, rows5 in enumerate((o5_s, dq5_s)):
         for far in range(2):
             keep_ref[n, far] = rows5[place[0] ^ far, :, place[1]]
@@ -145,25 +156,40 @@
 ROWS5 = pltpu.VMEM((2, 16, 2, 32, DH), jnp.bfloat16)
 
 
-def run_stats(place, qg, kv, bias):
+def cost(products):
+    return pl.CostEstimate(
+        flops=products * 2 * 2048 * 2048 * DH, bytes_accessed=1 << 22, transcendentals=1 << 21
+    )
+
+
+def run_stats(rows, kv, bias, *before):
+    out_shape = [
+        jax.ShapeDtypeStruct((3, 8, QB), jnp.float32),
+        jax.ShapeDtypeStruct((DH, 2048), jnp.float32),
+        jax.ShapeDtypeStruct((1024, 2048), jnp.bfloat16),
+    ]
+    if before:
+        out_shape.append(jax.ShapeDtypeStruct((2, 8, QB), jnp.float32))
+    else:
+        out_shape += [jax.ShapeDtypeStruct((2, 16, 2, 32, DH), jnp.bfloat16)] * 2
     return pl.pallas_call(
         stats_kernel,
-        out_shape=(
-            jax.ShapeDtypeStruct((3, 8, QB), jnp.float32),
-            jax.ShapeDtypeStruct((DH, 2048), jnp.float32),
-            jax.ShapeDtypeStruct((2048, 2048), jnp.bfloat16),
-        ),
-        in_specs=[SM] + [VM] * 9,
-        out_specs=(VM,) * 3,
-        scratch_shapes=[ROWS5] * 2
-        + [pltpu.VMEM((2048, DH), jnp.bfloat16), pltpu.VMEM((DH, 2048), jnp.bfloat16)]
-        + [pltpu.VMEM((2048, QB), jnp.float32)] * 2,
-        compiler_params=PARAMS,
-        name="stats",
-    )(place, *qg, *kv, bias)
-
-
-def run_grads(place, qg, kv, e, acc, stats):
+        out_shape=out_shape,
+        in_specs=[VM] * 7 if before else [SM] + [VM] * 7,
+        out_specs=[VM] * len(out_shape),
+        scratch_shapes=[
+            pltpu.VMEM((1024, DH), jnp.bfloat16),
+            pltpu.VMEM((DH, 1024), jnp.bfloat16),
+            pltpu.VMEM((1024, QB), jnp.float32),
+            pltpu.VMEM((1024, QB), jnp.float32),
+        ],
+        compiler_params=PARAMS,
+        cost_estimate=cost(1),
+        name="stats_far" if before else "stats_near",
+    )(*rows, *kv, bias, *before)
+
+
+def run_grads(place, rows, kv, e, part, acc, stats):
     side = jax.ShapeDtypeStruct((2, 2, 16, 32, DH), jnp.bfloat16)
     keys = jax.ShapeDtypeStruct((2048, DH), jnp.bfloat16)
     return pl.pallas_call(
@@ -171,13 +197,14 @@
         out_shape=(side, side, keys, keys),
         in_specs=[SM] + [VM] * 14,
         out_specs=(VM,) * 4,
-        scratch_shapes=[ROWS5] * 4
-        + [pltpu.VMEM((2048, DH), jnp.bfloat16), pltpu.VMEM((DH, 2048), jnp.bfloat16)]
+        scratch_shapes=[ROWS5] * 2
+        + [pltpu.VMEM((DH, 2048), jnp.bfloat16)]
         + [pltpu.VMEM((2048, DH), jnp.float32)] * 2
         + [pltpu.VMEM((8, QB), jnp.float32)] * 2,
         compiler_params=PARAMS,
+        cost_estimate=cost(4),
         name="grads",
-    )(place, *qg, *kv, e, acc, *stats)
+    )(place, *kv, *rows, *e, part, acc, *stats)
 
 
 def ring(n, k):
@@ -193,7 +220,7 @@
     head_at = lax.axis_index("y0") * 8 + lax.axis_index("z")
     place = jnp.stack([y1_at, core_at]).astype(jnp.int32)
 
-    back = jnp.array(BACK, jnp.int32)
+    back = jnp.array([BACK[j] for j in NEAR + FAR], jnp.int32)
     tiles = jnp.arange(16, dtype=jnp.int32)
     k_tiles = (((x_at - back) % 4)[:, None] * 16 + y1_at * 8 + tiles[None, :8]).reshape(32)
     slots = key_tiles.shape[2]
@@ -204,12 +231,7 @@
     hit = jnp.any(lists[None, :, :] == k_tiles[:, None, None], axis=2)
     bias = jnp.repeat(jnp.where(hit, 0.0, NEG).astype(jnp.float32), TILE, axis=1)
 
-    def by_head(a):
-        return a.reshape(32, 16, DH).transpose(1, 0, 2)
-
-    packed = jnp.stack(
-        [by_head(queries), by_head(out_grad), by_head(key_vectors), by_head(value_vectors)], axis=1
-    )
+    packed = pack(queries, out_grad, key_vectors, value_vectors)
     got = lax.all_to_all(packed, HEADS, split_axis=0, concat_axis=0, tiled=True)
     got, bias = lax.optimization_barrier((got, bias))
     qg_own, kv_own = got[:, 0:2], got[:, 2:4]
@@ -221,20 +243,25 @@
         qg_far,
         lax.ppermute(qg_far, "core", SWAP),
     ]
-    stat, acc, e = run_stats(place, qg, kv, bias)
+    near, near_acc, e_near, *full = run_stats(
+        [place, *qg], [kv[j] for j in NEAR], bias[:16]
+    )
+    stat, acc, e_far, part = run_stats(
+        full, [kv[j] for j in FAR], bias[16:], near, near_acc
+    )
     stats = [
         stat,
         lax.ppermute(stat, "core", SWAP),
         lax.ppermute(stat, "y1", SWAP),
         lax.ppermute(stat, ("core", "y1"), [(i, 3 - i) for i in range(4)]),
     ]
-    keep, away, dk, dv = run_grads(place, qg, kv, e, acc, stats)
+    keep, away, dk, dv = run_grads(place, full, kv, (e_near, e_far), part, acc, stats)
 
     def pair(a, b, j):
         rows = slice(512 * j, 512 * (j + 1))
         return jnp.stack([a[rows], b[rows]])
 
-    came = [lax.ppermute(pair(dk, dv, j), "x", ring(4, -k)) for j, k in enumerate(BACK) if j]
+    came = [lax.ppermute(pair(dk, dv, j), "x", ring(4, -BACK[j])) for j in (3, 1, 2)]
     near, far = add_core(keep, lax.ppermute(away, "core", SWAP))
     send = add_up(dk, dv, came, near, lax.ppermute(far, "y1", SWAP))
     back_home = lax.all_to_all(send, HEADS, split_axis=0, concat_axis=0, tiled=True)
@@ -285,6 +312,32 @@
     )(dk, dv, *came, near, far)
 
 
+def pack_kernel(*refs):
+    arrays, out_ref, held, sems = refs[0:4], refs[4], refs[5], refs[6]
+    copies = [pltpu.make_async_copy(arrays[n], held.at[n], sems.at[n]) for n in range(4)]
+    for copy in copies:
+        copy.start()
+    for n, copy in enumerate(copies):
+        copy.wait()
+        for h in range(16):
+            out_ref[h, n] = held[n, :, h * DH:(h + 1) * DH]
+
+
+def pack(*arrays):
+    return pl.pallas_call(
+        pack_kernel,
+        out_shape=jax.ShapeDtypeStruct((16, 4, 32, DH), jnp.bfloat16),
+        in_specs=[pl.BlockSpec(memory_space=pl.ANY)] * 4,
+        out_specs=VM,
+        scratch_shapes=[
+            pltpu.VMEM((4, 32, 16 * DH), jnp.bfloat16),
+            pltpu.SemaphoreType.DMA((4,)),
+        ],
+        compiler_params=pltpu.CompilerParams(vmem_limit_bytes=60 * 1024 * 1024),
+        name="pack",
+    )(*arrays)
+
+
 def unpack_kernel(src_ref, *outs):
     for n, out in enumerate(outs):
         for h in range(16):

time: 108 us -> 103 us (0.954)
  waiting for transfers between devices: 32.9 us -> 27.3 us
  Pallas kernels: 17.1 us -> 19.6 us
  local copies, waits for them, and re-layouts: 3.42 us -> 1.36 us
    ppermute x3, waiting for transfers between devices: 10.2 us -> 6.15 us  [per_device(): kv = [kv_own] + [lax.ppermute(kv_own, 'x', ring(4, k)) for k in SHIFTS]]
    pallas_call x1 -> x3, Pallas kernels: 7.06 us -> 9.58 us  [the longest x2 7.58 us: run_stats(): pl.pallas_call(stats_kernel, out_shape=out_shape, in_specs=[VM] * 7 if be...]
    another operation x2 -> x0, local copies, waits for them, and re-layouts: 2.08 us -> none  [per_device(): jnp.stack([by_head(queries), by_head(out_grad), by_head(key_vectors), by_...]
    ppermute x3, waiting for transfers between devices: 9.77 us -> 8.19 us  [per_device(): lax.ppermute(pair(dk, dv, j), 'x', ring(4, -BACK[j]))]
  transfers between devices with their start and end apart: 15 -> 15, of which waited for: 8 -> 9; matrix products, arithmetic and copies ran while one was open for 3% -> 3% of each run, Pallas kernels for 0% -> 4%
where the time goes in v3:
time: 103 us; the launch traced here: 101 us
  starting transfers between devices  32.6 us (32%)
  waiting for transfers between devices  27.3 us (27%)
  Pallas kernels  19.6 us (19%)
  blocking collectives  17.6 us (17%)
  other arithmetic  1.68 us (2%)
  local copies, waits for them, and re-layouts  1.36 us (1%)
    all_to_all x1, blocking collectives, per_device(): lax.all_to_all(send, HEADS, split_axis=0, concat_axis=0, tiled=True)  17.6 us
    all_to_all x1, waiting for transfers between devices, per_device(): got = lax.all_to_all(packed, HEADS, split_axis=0, concat_axis=0, tiled=True)  10.9 us
    all_to_all x1, starting transfers between devices, per_device(): got = lax.all_to_all(packed, HEADS, split_axis=0, concat_axis=0, tiled=True)  10.1 us
    pallas_call x1, Pallas kernels, run_grads(): pl.pallas_call(grad_kernel, out_shape=(side, side, keys, keys), in_specs=...  8.83 us
    ppermute x3, waiting for transfers between devices, per_device(): lax.ppermute(pair(dk, dv, j), 'x', ring(4, -BACK[j]))  8.19 us
    pallas_call x2, Pallas kernels, run_stats(): pl.pallas_call(stats_kernel, out_shape=out_shape, in_specs=[VM] * 7 if be...  7.58 us
    ppermute x3, waiting for transfers between devices, per_device(): kv = [kv_own] + [lax.ppermute(kv_own, 'x', ring(4, k)) for k in SHIFTS]  6.15 us
    ppermute x3, starting transfers between devices, per_device(): lax.ppermute(pair(dk, dv, j), 'x', ring(4, -BACK[j]))  4.37 us
  transfers between devices with their start and end apart: 15, of which 9 were waited for; matrix products, arithmetic and copies ran while one was open for 3% of the time, Pallas kernels for 4%

profile of v3, /device:TPU:1, one launch (start us, length us, event | category | flops | bytes accessed | tf_op | source)
XLA Modules:
  0.0 100.9 jit_solution(11464198333165919710)
XLA Ops:
  0.6 0.0 copy-start
  0.6 2.0 %pack.1 = bf16[16,4,32,128]{3,2,1,0:T(8,128)(2,1)} custom-call(bf16[32,2048]{1,0:T(8,128)(2,1)} %refs_0_.1, bf16[32,2048]{1,0:T(8,128)(2,1)} %refs_1_.1, bf16[32,2048]{1,0:T(8,128)(2,1)} %refs_2_.1, bf16[32,2048]{1,0:T(8,128)(2,1)} %refs_3_.1), custom_call_target="tpu_custom_call" | custom-call | tf_op jit(solution)/shard_map/pack/pallas_call | solution.py:327
  2.7 10.1 %all-to-all-start = ((bf16[16,4,32,128]{3,2,1,0:T(8,128)(2,1)}), bf16[16,4,32,128]{3,2,1,0:T(8,128)(2,1)S(1)}, u32[]{:S(2)}, u32[]{:S(2)}) async-start(bf16[16,4,32,128]{3,2,1,0:T(8,128)(2,1)} %pack.1), calls=%async_computation | async-start | bytes 1048576 | tf_op jit(solution)/shard_map/all_to_all | solution.py:235
  12.8 0.7 fusion.2
  13.5 0.1 broadcast_add_fusion
  13.6 0.1 add.53
  13.7 0.1 constant_dynamic-slice_fusion
  13.8 0.1 copy.14
  13.8 0.8 dynamic-slice_bitcast_fusion
  14.6 0.1 select_bitcast_fusion
  14.7 0.7 compare_reduce_fusion
  15.4 0.1 broadcast_in_dim.22
  15.5 0.1 copy.17
  15.6 10.9 %all-to-all-done = bf16[16,4,32,128]{3,2,1,0:T(8,128)(2,1)S(1)} async-done(((bf16[16,4,32,128]{3,2,1,0:T(8,128)(2,1)}), bf16[16,4,32,128]{3,2,1,0:T(8,128)(2,1)S(1)}, u32[]{:S(2)}, u32[]{:S(2)}) %all-to-all-start) | async-done | bytes 524320 | tf_op jit(solution)/shard_map/all_to_all | solution.py:235
  26.6 2.7 %collective-permute-start.4 = (bf16[16,2,32,128]{3,2,1,0:T(8,128)(2,1)S(1)}, bf16[16,2,32,128]{3,2,1,0:T(8,128)(2,1)S(1)}, u32[]{:S(2)}, u32[]{:S(2)}) collective-permute-start(bf16[16,2,32,128]{3,2,1,0:T(8,128)(2,1)S(1)} %get-tuple-element.44.refs_1_), channel_id=1, source_target_pairs={{0,2},{2,0},{1,3},{3,1},{4,6},{6,4},{5,7},{7,5},{8,10},{10,8},{9,1... | collective-permute-start | bytes 786440 | tf_op jit(solution)/shard_map/ppermute | solution.py:239
  29.3 0.1 pad_add_fusion.refs_0_
  29.4 3.2 %collective-permute-start.3 = (bf16[16,2,32,128]{3,2,1,0:T(8,128)(2,1)S(1)}, bf16[16,2,32,128]{3,2,1,0:T(8,128)(2,1)S(1)}, u32[]{:S(2)}, u32[]{:S(2)}) collective-permute-start(bf16[16,2,32,128]{3,2,1,0:T(8,128)(2,1)S(1)} %get-tuple-element.44.refs_1_), channel_id=1, source_target_pairs={{0,16},{16,0},{1,17},{17,1},{2,18},{18,2},{3,19},{19,3},{4,20},{20... | collective-permute-start | bytes 786440 | tf_op jit(solution)/shard_map/ppermute | solution.py:242
  32.6 2.8 %collective-permute-start.2 = (bf16[16,2,32,128]{3,2,1,0:T(8,128)(2,1)S(1)}, bf16[16,2,32,128]{3,2,1,0:T(8,128)(2,1)S(1)}, u32[]{:S(2)}, u32[]{:S(2)}) collective-permute-start(bf16[16,2,32,128]{3,2,1,0:T(8,128)(2,1)S(1)} %get-tuple-element.45.refs_5_.refs_1_), channel_id=1, source_target_pairs={{0,8},{4,12},{8,0},{12,4},{1,9},{5,13},{9,1},{13,5},{2,10},{6,14},... | collective-permute-start | bytes 786440 | tf_op jit(solution)/shard_map/ppermute | solution.py:238
  35.3 0.9 collective-permute-start.1
  36.2 0.6 collective-permute-start
  36.8 0.0 collective-permute-done.4.refs_3_
  36.8 0.9 collective-permute-start.5
  37.8 4.2 %collective-permute-done.2.refs_6_.refs_4_ = bf16[16,2,32,128]{3,2,1,0:T(8,128)(2,1)S(1)} collective-permute-done((bf16[16,2,32,128]{3,2,1,0:T(8,128)(2,1)S(1)}, bf16[16,2,32,128]{3,2,1,0:T(8,128)(2,1)S(1)}, u32[]{:S(2)}, u32[]{:S(2)}) %collective-permute-start.2) | collective-permute-done | bytes 262176 | tf_op jit(solution)/shard_map/ppermute | solution.py:238
  42.0 0.0 collective-permute-done.5.refs_4_
  42.0 4.0 %stats_near.1 = (f32[3,8,256]{2,1,0:T(8,128)S(1)}, f32[128,2048]{1,0:T(8,128)S(1)}, bf16[1024,2048]{1,0:T(8,128)(2,1)S(1)}, bf16[2,16,2,32,128]{4,3,2,1,0:T(8,128)(2,1)S(1)}, bf16[2,16,2,32,128]{4,3,2,1,0:T(8,128)(2,1)S(1)}) custom-call(s32[2]{0:T(128)S(1)} %pad_add_fusion.refs_0_, bf16[16,2,32,128]{3,2,1,0:T(8,128)(2,1)S(1)} %get-tuple-element.44.refs_1_, ...), custom_call_target="tpu_custom_call" | custom-call | flops 1073741824 | bytes 4194304 | tf_op jit(solution)/shard_map/stats_near/pallas_call | solution.py:175
  46.0 1.7 %collective-permute-done.1.refs_3_ = bf16[16,2,32,128]{3,2,1,0:T(8,128)(2,1)S(1)} collective-permute-done((bf16[16,2,32,128]{3,2,1,0:T(8,128)(2,1)S(1)}, bf16[16,2,32,128]{3,2,1,0:T(8,128)(2,1)S(1)}, u32[]{:S(2)}, u32[]{:S(2)}) %collective-permute-start.1) | collective-permute-done | bytes 262176 | tf_op jit(solution)/shard_map/ppermute | solution.py:238
  47.7 0.2 collective-permute-done.refs_2_
  47.9 3.6 %stats_far.1 = (f32[3,8,256]{2,1,0:T(8,128)S(1)}, f32[128,2048]{1,0:T(8,128)S(1)}, bf16[1024,2048]{1,0:T(8,128)(2,1)S(1)}, f32[2,8,256]{2,1,0:T(8,128)S(1)}) custom-call(bf16[2,16,2,32,128]{4,3,2,1,0:T(8,128)(2,1)S(1)} %get-tuple-element.23.refs_0_.refs_5_, bf16[2,16,2,32,128]{4,3,2,1,0:T(8,128)(2,1)S(1)} %get-tuple-element.24.refs_1_.refs_6_, ...), custom_call_target="tpu_custom_call" | custom-call | flops 1073741824 | bytes 4194304 | tf_op jit(solution)/shard_map/stats_far/pallas_call | solution.py:175
  51.5 1.0 collective-permute-start.8
  52.5 2.6 %collective-permute-start.7 = (f32[3,8,256]{2,1,0:T(8,128)S(1)}, f32[3,8,256]{2,1,0:T(8,128)S(1)}, u32[]{:S(2)}, u32[]{:S(2)}) collective-permute-start(f32[3,8,256]{2,1,0:T(8,128)S(1)} %get-tuple-element.31.refs_11_), channel_id=1, source_target_pairs={{0,2},{2,0},{1,3},{3,1},{4,6},{6,4},{5,7},{7,5},{8,10},{10,8},{9,1... | collective-permute-start | bytes 73736 | tf_op jit(solution)/shard_map/ppermute | solution.py:255
  55.1 0.2 collective-permute-start.6
  55.2 1.5 %collective-permute-done.8.refs_14_ = f32[3,8,256]{2,1,0:T(8,128)S(1)} collective-permute-done((f32[3,8,256]{2,1,0:T(8,128)S(1)}, f32[3,8,256]{2,1,0:T(8,128)S(1)}, u32[]{:S(2)}, u32[]{:S(2)}) %collective-permute-start.8) | collective-permute-done | bytes 24608 | tf_op jit(solution)/shard_map/ppermute | solution.py:256
  56.8 0.5 collective-permute-done.7.refs_13_
  57.2 0.0 collective-permute-done.6.refs_12_
  57.2 8.8 %grads.1 = (bf16[2,2,16,32,128]{4,3,2,1,0:T(8,128)(2,1)S(1)}, bf16[2,2,16,32,128]{4,3,2,1,0:T(8,128)(2,1)S(1)}, bf16[2048,128]{1,0:T(8,128)(2,1)S(1)}, bf16[2048,128]{1,0:T(8,128)(2,1)S(1)}) custom-call(s32[2]{0:T(128)S(1)} %pad_add_fusion.refs_0_, bf16[16,2,32,128]{3,2,1,0:T(8,128)(2,1)S(1)} %get-tuple-element.45.refs_5_.refs_1_, ...), custom_call_target="tpu_custom_call" | custom-call | flops 4294967296 | bytes 4194304 | tf_op jit(solution)/shard_map/grads/pallas_call | solution.py:195
  66.1 0.6 collective-permute-start.12
  66.7 0.1 slice_bitcast_fusion
  66.8 2.8 %collective-permute-start.9 = (bf16[2,512,128]{2,1,0:T(8,128)(2,1)S(1)}, bf16[2,512,128]{2,1,0:T(8,128)(2,1)S(1)}, u32[]{:S(2)}, u32[]{:S(2)}) collective-permute-start(bf16[2,512,128]{2,1,0:T(8,128)(2,1)S(1)} %pad_maximum_fusion), channel_id=1, source_target_pairs={{0,8},{4,12},{8,0},{12,4},{1,9},{5,13},{9,1},{13,5},{2,10},{6,14},... | collective-permute-start | bytes 786440 | tf_op jit(solution)/shard_map/ppermute | solution.py:264
  69.6 1.0 collective-permute-start.10
  70.6 0.7 collective-permute-start.11
  71.2 0.1 add_core.1
  71.3 2.7 %collective-permute-start.13 = (bf16[2,16,32,128]{3,2,1,0:T(8,128)(2,1)S(1)}, bf16[2,16,32,128]{3,2,1,0:T(8,128)(2,1)S(1)}, u32[]{:S(2)}, u32[]{:S(2)}) collective-permute-start(bf16[2,16,32,128]{3,2,1,0:T(8,128)(2,1)S(1)} %get-tuple-element.37), channel_id=1, source_target_pairs={{0,2},{2,0},{1,3},{3,1},{4,6},{6,4},{5,7},{7,5},{8,10},{10,8},{9,1... | collective-permute-start | bytes 786440 | tf_op jit(solution)/shard_map/ppermute | solution.py:266
  74.0 2.3 %collective-permute-done.9.refs_0_ = bf16[2,512,128]{2,1,0:T(8,128)(2,1)S(1)} collective-permute-done((bf16[2,512,128]{2,1,0:T(8,128)(2,1)S(1)}, bf16[2,512,128]{2,1,0:T(8,128)(2,1)S(1)}, u32[]{:S(2)}, u32[]{:S(2)}) %collective-permute-start.9) | collective-permute-done | bytes 262176 | tf_op jit(solution)/shard_map/ppermute | solution.py:264
  76.3 5.7 %collective-permute-done.10.refs_1_ = bf16[2,512,128]{2,1,0:T(8,128)(2,1)S(1)} collective-permute-done((bf16[2,512,128]{2,1,0:T(8,128)(2,1)S(1)}, bf16[2,512,128]{2,1,0:T(8,128)(2,1)S(1)}, u32[]{:S(2)}, u32[]{:S(2)}) %collective-permute-start.10) | collective-permute-done | bytes 262176 | tf_op jit(solution)/shard_map/ppermute | solution.py:264
  82.0 0.2 collective-permute-done.11.refs_2_
  82.2 0.2 add_up.1
  82.4 17.6 %all_to_all.10.src_ref = bf16[16,4,32,128]{3,2,1,0:T(8,128)(2,1)S(1)} all-to-all(bf16[16,4,32,128]{3,2,1,0:T(8,128)(2,1)S(1)} %add_up.1), channel_id=1, replica_groups=mesh['z'=8,'core'=2,'x'=4,'y1'=2,'y0'=2] {'y0','z'}, dimensions={0} | all-to-all | bytes 1048576 | tf_op jit(solution)/shard_map/all_to_all | solution.py:267
  100.0 0.9 unpack.1
  (11 shorter events, 0.2 us)
Async XLA Ops:
  0.6 13.0 %copy-start = (s32[16,64,38]{1,0,2:T(8,128)S(1)}, s32[16,64,38]{1,0,2:T(8,128)}, u32[]{:S(2)}) copy-start(s32[16,64,38]{1,0,2:T(8,128)} %param.11) | copy-start | bytes 466948
  2.7 23.9 %all-to-all-start = ((bf16[16,4,32,128]{3,2,1,0:T(8,128)(2,1)}), bf16[16,4,32,128]{3,2,1,0:T(8,128)(2,1)S(1)}, u32[]{:S(2)}, u32[]{:S(2)}) async-start(bf16[16,4,32,128]{3,2,1,0:T(8,128)(2,1)} %pack.1), calls=%async_computation | async-start | bytes 1048576 | tf_op jit(solution)/shard_map/all_to_all | solution.py:235
  26.6 10.2 %collective-permute-start.4 = (bf16[16,2,32,128]{3,2,1,0:T(8,128)(2,1)S(1)}, bf16[16,2,32,128]{3,2,1,0:T(8,128)(2,1)S(1)}, u32[]{:S(2)}, u32[]{:S(2)}) collective-permute-start(bf16[16,2,32,128]{3,2,1,0:T(8,128)(2,1)S(1)} %get-tuple-element.44.refs_1_), channel_id=1, source_target_pairs={{0,2},{2,0},{1,3},{3,1},{4,6},{6,4},{5,7},{7,5},{8,10},{10,8},{9,1... | collective-permute-start | bytes 786440 | tf_op jit(solution)/shard_map/ppermute | solution.py:239
  29.4 8.4 %collective-permute-start.3 = (bf16[16,2,32,128]{3,2,1,0:T(8,128)(2,1)S(1)}, bf16[16,2,32,128]{3,2,1,0:T(8,128)(2,1)S(1)}, u32[]{:S(2)}, u32[]{:S(2)}) collective-permute-start(bf16[16,2,32,128]{3,2,1,0:T(8,128)(2,1)S(1)} %get-tuple-element.44.refs_1_), channel_id=1, source_target_pairs={{0,16},{16,0},{1,17},{17,1},{2,18},{18,2},{3,19},{19,3},{4,20},{20... | collective-permute-start | bytes 786440 | tf_op jit(solution)/shard_map/ppermute | solution.py:242
  32.6 9.4 %collective-permute-start.2 = (bf16[16,2,32,128]{3,2,1,0:T(8,128)(2,1)S(1)}, bf16[16,2,32,128]{3,2,1,0:T(8,128)(2,1)S(1)}, u32[]{:S(2)}, u32[]{:S(2)}) collective-permute-start(bf16[16,2,32,128]{3,2,1,0:T(8,128)(2,1)S(1)} %get-tuple-element.45.refs_5_.refs_1_), channel_id=1, source_target_pairs={{0,8},{4,12},{8,0},{12,4},{1,9},{5,13},{9,1},{13,5},{2,10},{6,14},... | collective-permute-start | bytes 786440 | tf_op jit(solution)/shard_map/ppermute | solution.py:238
  35.3 12.4 %collective-permute-start.1 = (bf16[16,2,32,128]{3,2,1,0:T(8,128)(2,1)S(1)}, bf16[16,2,32,128]{3,2,1,0:T(8,128)(2,1)S(1)}, u32[]{:S(2)}, u32[]{:S(2)}) collective-permute-start(bf16[16,2,32,128]{3,2,1,0:T(8,128)(2,1)S(1)} %get-tuple-element.45.refs_5_.refs_1_), channel_id=1, source_target_pairs={{0,12},{4,0},{8,4},{12,8},{1,13},{5,1},{9,5},{13,9},{2,14},{6,2},{... | collective-permute-start | bytes 786440 | tf_op jit(solution)/shard_map/ppermute | solution.py:238
  36.2 11.7 %collective-permute-start = (bf16[16,2,32,128]{3,2,1,0:T(8,128)(2,1)S(1)}, bf16[16,2,32,128]{3,2,1,0:T(8,128)(2,1)S(1)}, u32[]{:S(2)}, u32[]{:S(2)}) collective-permute-start(bf16[16,2,32,128]{3,2,1,0:T(8,128)(2,1)S(1)} %get-tuple-element.45.refs_5_.refs_1_), channel_id=1, source_target_pairs={{0,4},{4,8},{8,12},{12,0},{1,5},{5,9},{9,13},{13,1},{2,6},{6,10},{... | collective-permute-start | bytes 786440 | tf_op jit(solution)/shard_map/ppermute | solution.py:238
  36.8 5.2 %collective-permute-start.5 = (bf16[16,2,32,128]{3,2,1,0:T(8,128)(2,1)S(1)}, bf16[16,2,32,128]{3,2,1,0:T(8,128)(2,1)S(1)}, u32[]{:S(2)}, u32[]{:S(2)}) collective-permute-start(bf16[16,2,32,128]{3,2,1,0:T(8,128)(2,1)S(1)} %collective-permute-done.4.refs_3_), channel_id=1, source_target_pairs={{0,16},{16,0},{1,17},{17,1},{2,18},{18,2},{3,19},{19,3},{4,20},{20... | collective-permute-start | bytes 786440 | tf_op jit(solution)/shard_map/ppermute | solution.py:244
  51.5 5.3 %collective-permute-start.8 = (f32[3,8,256]{2,1,0:T(8,128)S(1)}, f32[3,8,256]{2,1,0:T(8,128)S(1)}, u32[]{:S(2)}, u32[]{:S(2)}) collective-permute-start(f32[3,8,256]{2,1,0:T(8,128)S(1)} %get-tuple-element.31.refs_11_), channel_id=1, source_target_pairs={{0,18},{2,16},{16,2},{18,0},{1,19},{3,17},{17,3},{19,1},{4,22},{6,... | collective-permute-start | bytes 73736 | tf_op jit(solution)/shard_map/ppermute | solution.py:256
  52.5 4.8 %collective-permute-start.7 = (f32[3,8,256]{2,1,0:T(8,128)S(1)}, f32[3,8,256]{2,1,0:T(8,128)S(1)}, u32[]{:S(2)}, u32[]{:S(2)}) collective-permute-start(f32[3,8,256]{2,1,0:T(8,128)S(1)} %get-tuple-element.31.refs_11_), channel_id=1, source_target_pairs={{0,2},{2,0},{1,3},{3,1},{4,6},{6,4},{5,7},{7,5},{8,10},{10,8},{9,1... | collective-permute-start | bytes 73736 | tf_op jit(solution)/shard_map/ppermute | solution.py:255
  55.1 2.2 %collective-permute-start.6 = (f32[3,8,256]{2,1,0:T(8,128)S(1)}, f32[3,8,256]{2,1,0:T(8,128)S(1)}, u32[]{:S(2)}, u32[]{:S(2)}) collective-permute-start(f32[3,8,256]{2,1,0:T(8,128)S(1)} %get-tuple-element.31.refs_11_), channel_id=1, source_target_pairs={{0,16},{16,0},{1,17},{17,1},{2,18},{18,2},{3,19},{19,3},{4,20},{20... | collective-permute-start | bytes 73736 | tf_op jit(solution)/shard_map/ppermute | solution.py:254
  66.1 5.1 %collective-permute-start.12 = (bf16[2,2,16,32,128]{4,3,2,1,0:T(8,128)(2,1)S(1)}, bf16[2,2,16,32,128]{4,3,2,1,0:T(8,128)(2,1)S(1)}, u32[]{:S(2)}, u32[]{:S(2)}) collective-permute-start(bf16[2,2,16,32,128]{4,3,2,1,0:T(8,128)(2,1)S(1)} %get-tuple-element.35), channel_id=1, source_target_pairs={{0,16},{16,0},{1,17},{17,1},{2,18},{18,2},{3,19},{19,3},{4,20},{20... | collective-permute-start | bytes 1572872 | tf_op jit(solution)/shard_map/ppermute | solution.py:265
  66.8 9.5 %collective-permute-start.9 = (bf16[2,512,128]{2,1,0:T(8,128)(2,1)S(1)}, bf16[2,512,128]{2,1,0:T(8,128)(2,1)S(1)}, u32[]{:S(2)}, u32[]{:S(2)}) collective-permute-start(bf16[2,512,128]{2,1,0:T(8,128)(2,1)S(1)} %pad_maximum_fusion), channel_id=1, source_target_pairs={{0,8},{4,12},{8,0},{12,4},{1,9},{5,13},{9,1},{13,5},{2,10},{6,14},... | collective-permute-start | bytes 786440 | tf_op jit(solution)/shard_map/ppermute | solution.py:264
  69.6 12.4 %collective-permute-start.10 = (bf16[2,512,128]{2,1,0:T(8,128)(2,1)S(1)}, bf16[2,512,128]{2,1,0:T(8,128)(2,1)S(1)}, u32[]{:S(2)}, u32[]{:S(2)}) collective-permute-start(bf16[2,512,128]{2,1,0:T(8,128)(2,1)S(1)} %pad_maximum_fusion.1), channel_id=1, source_target_pairs={{0,12},{4,0},{8,4},{12,8},{1,13},{5,1},{9,5},{13,9},{2,14},{6,2},{... | collective-permute-start | bytes 786440 | tf_op jit(solution)/shard_map/ppermute | solution.py:264
  70.6 11.7 %collective-permute-start.11 = (bf16[2,512,128]{2,1,0:T(8,128)(2,1)S(1)}, bf16[2,512,128]{2,1,0:T(8,128)(2,1)S(1)}, u32[]{:S(2)}, u32[]{:S(2)}) collective-permute-start(bf16[2,512,128]{2,1,0:T(8,128)(2,1)S(1)} %pad_maximum_fusion.2), channel_id=1, source_target_pairs={{0,4},{4,8},{8,12},{12,0},{1,5},{5,9},{9,13},{13,1},{2,6},{6,10},{... | collective-permute-start | bytes 786440 | tf_op jit(solution)/shard_map/ppermute | solution.py:264
  71.3 10.9 %collective-permute-start.13 = (bf16[2,16,32,128]{3,2,1,0:T(8,128)(2,1)S(1)}, bf16[2,16,32,128]{3,2,1,0:T(8,128)(2,1)S(1)}, u32[]{:S(2)}, u32[]{:S(2)}) collective-permute-start(bf16[2,16,32,128]{3,2,1,0:T(8,128)(2,1)S(1)} %get-tuple-element.37), channel_id=1, source_target_pairs={{0,2},{2,0},{1,3},{3,1},{4,6},{6,4},{5,7},{7,5},{8,10},{10,8},{9,1... | collective-permute-start | bytes 786440 | tf_op jit(solution)/shard_map/ppermute | solution.py:266

commit v4 on v3

--- a/solution.py
+++ b/solution.py
@@ -16,10 +16,9 @@
 QB = 256
 KC = 512
 NEG = -1e30
-SHIFTS = (1, 3, 2)
-BACK = (0, 1, 3, 2)
 HALF = TILE // 2
 NEAR, FAR = (0, 3), (1, 2)
+AWAY = (0, 3, 1, 2)
 
 NT = (((1,), (1,)), ((), ()))
 NN = (((1,), (0,)), ((), ()))
@@ -49,31 +48,32 @@
     for j in range(2):
         rows = slice(j * KC, (j + 1) * KC)
         k_s[rows] = kv[j][:, 0].reshape(KC, DH)
-        vt_s[:, rows] = kv[j][:, 1].reshape(KC, DH).T
+        vt_s[:DH, rows] = kv[j][:, 1].reshape(KC, DH).T
+    vt_s[DH:] = jnp.ones((16, vt_s.shape[1]), jnp.bfloat16)
 
     def score(qb, x_s):
         start = pl.multiple_of(qb * QB, QB)
         q = q_s[pl.ds(start, QB)]
         top = jnp.full((1, QB), NEG, jnp.float32)
         for c in range(2):
-            s = dot(k_s[c * KC:(c + 1) * KC], q, NT) * C1
-            bias = bias_ref[c * 8:(c + 1) * 8, pl.ds(start, QB)]
-            x = (s.reshape(8, HALF, QB) + bias[:, None, :]).reshape(KC, QB)
-            x_s[c * KC:(c + 1) * KC] = x
-            top = jnp.maximum(top, jnp.max(x, axis=0, keepdims=True))
+            s = dot(k_s[c * KC:(c + 1) * KC], q, NT)
+            x_s[c * KC:(c + 1) * KC] = s
+            highs = jnp.max(s.reshape(8, HALF, QB), axis=1) * C1
+            highs = highs + bias_ref[c * 8:(c + 1) * 8, pl.ds(start, QB)]
+            top = jnp.maximum(top, jnp.max(highs, axis=0, keepdims=True))
         return top
 
     def finish(qb, x_s, top):
         start = pl.multiple_of(qb * QB, QB)
-        mass = jnp.zeros((1, QB), jnp.float32)
-        acc = jnp.zeros((DH, QB), jnp.float32)
+        acc = jnp.zeros((DH + 16, QB), jnp.float32)
         for c in range(2):
             rows = slice(c * KC, (c + 1) * KC)
-            e = jnp.exp2(x_s[rows] - top)
-            mass = mass + jnp.sum(e, axis=0, keepdims=True)
-            low = e.astype(jnp.bfloat16)
+            shift = bias_ref[c * 8:(c + 1) * 8, pl.ds(start, QB)] - jnp.maximum(top, NEG / 2)
+            x = x_s[rows].reshape(8, HALF, QB) * C1 + shift[:, None, :]
+            low = jnp.exp2(x).reshape(KC, QB).astype(jnp.bfloat16)
             e_ref[rows, pl.ds(start, QB)] = low
             acc = acc + dot(vt_s[:, rows], low, NN)
+        acc, mass = acc[:DH], acc[DH:DH + 1]
         if second:
             near_top = near_ref[0, pl.ds(qb, 1)]
             new_top = jnp.maximum(near_top, top)
@@ -179,7 +179,7 @@
         out_specs=[VM] * len(out_shape),
         scratch_shapes=[
             pltpu.VMEM((1024, DH), jnp.bfloat16),
-            pltpu.VMEM((DH, 1024), jnp.bfloat16),
+            pltpu.VMEM((DH + 16, 1024), jnp.bfloat16),
             pltpu.VMEM((1024, QB), jnp.float32),
             pltpu.VMEM((1024, QB), jnp.float32),
         ],
@@ -207,8 +207,8 @@
     )(place, *kv, *rows, *e, part, acc, *stats)
 
 
-def ring(n, k):
-    return [(i, (i + k) % n) for i in range(n)]
+def swap(a, j):
+    return lax.ppermute(a, "x", [(i, i ^ j) for i in range(4)])
 
 
 SWAP = [(0, 1), (1, 0)]
@@ -220,9 +220,9 @@
     head_at = lax.axis_index("y0") * 8 + lax.axis_index("z")
     place = jnp.stack([y1_at, core_at]).astype(jnp.int32)
 
-    back = jnp.array([BACK[j] for j in NEAR + FAR], jnp.int32)
+    away = jnp.array([AWAY[j] for j in NEAR + FAR], jnp.int32)
     tiles = jnp.arange(16, dtype=jnp.int32)
-    k_tiles = (((x_at - back) % 4)[:, None] * 16 + y1_at * 8 + tiles[None, :8]).reshape(32)
+    k_tiles = ((x_at ^ away)[:, None] * 16 + y1_at * 8 + tiles[None, :8]).reshape(32)
     slots = key_tiles.shape[2]
     lists = lax.dynamic_slice(key_tiles, (head_at, x_at * 16, 0), (1, 16, slots))[0]
     counts = lax.dynamic_slice(tile_count, (head_at, x_at * 16), (1, 16))[0]
@@ -235,7 +235,7 @@
     got = lax.all_to_all(packed, HEADS, split_axis=0, concat_axis=0, tiled=True)
     got, bias = lax.optimization_barrier((got, bias))
     qg_own, kv_own = got[:, 0:2], got[:, 2:4]
-    kv = [kv_own] + [lax.ppermute(kv_own, "x", ring(4, k)) for k in SHIFTS]
+    kv = [kv_own] + [swap(kv_own, j) for j in AWAY[1:]]
     qg_far = lax.ppermute(qg_own, "y1", SWAP)
     qg = [
         qg_own,
@@ -255,14 +255,14 @@
         lax.ppermute(stat, "y1", SWAP),
         lax.ppermute(stat, ("core", "y1"), [(i, 3 - i) for i in range(4)]),
     ]
-    keep, away, dk, dv = run_grads(place, full, kv, (e_near, e_far), part, acc, stats)
+    keep, leave, dk, dv = run_grads(place, full, kv, (e_near, e_far), part, acc, stats)
 
     def pair(a, b, j):
         rows = slice(512 * j, 512 * (j + 1))
         return jnp.stack([a[rows], b[rows]])
 
-    came = [lax.ppermute(pair(dk, dv, j), "x", ring(4, -BACK[j])) for j in (3, 1, 2)]
-    near, far = add_core(keep, lax.ppermute(away, "core", SWAP))
+    came = [swap(pair(dk, dv, j), AWAY[j]) for j in (3, 2, 1)]
+    near, far = add_core(keep, lax.ppermute(leave, "core", SWAP))
     send = add_up(dk, dv, came, near, lax.ppermute(far, "y1", SWAP))
     back_home = lax.all_to_all(send, HEADS, split_axis=0, concat_axis=0, tiled=True)
     return unpack(back_home)

time: 103 us -> 102 us (level)
  waiting for transfers between devices: 27.3 us -> 28.6 us
    ppermute x7, waiting for transfers between devices: 14.3 us -> 15.7 us  [the longest x6 15.7 us: swap(): return lax.ppermute(a, 'x', [(i, i ^ j) for i in range(4)])]
    ppermute x7, starting transfers between devices: 9.23 us -> 8.07 us  [the longest x6 7.47 us: swap(): return lax.ppermute(a, 'x', [(i, i ^ j) for i in range(4)])]
where the time goes in v4:
time: 102 us; the launch traced here: 101 us
  starting transfers between devices  31.8 us (31%)
  waiting for transfers between devices  28.6 us (28%)
  Pallas kernels  18.7 us (18%)
  blocking collectives  17.8 us (17%)
  other arithmetic  1.67 us (2%)
  local copies, waits for them, and re-layouts  1.36 us (1%)
    all_to_all x1, blocking collectives, per_device(): lax.all_to_all(send, HEADS, split_axis=0, concat_axis=0, tiled=True)  17.8 us
    ppermute x6, waiting for transfers between devices, swap(): return lax.ppermute(a, 'x', [(i, i ^ j) for i in range(4)])  15.7 us
    all_to_all x1, waiting for transfers between devices, per_device(): got = lax.all_to_all(packed, HEADS, split_axis=0, concat_axis=0, tiled=True)  10.9 us
    all_to_all x1, starting transfers between devices, per_device(): got = lax.all_to_all(packed, HEADS, split_axis=0, concat_axis=0, tiled=True)  10.1 us
    pallas_call x1, Pallas kernels, run_grads(): pl.pallas_call(grad_kernel, out_shape=(side, side, keys, keys), in_specs=...  8.83 us
    ppermute x6, starting transfers between devices, swap(): return lax.ppermute(a, 'x', [(i, i ^ j) for i in range(4)])  7.47 us
    pallas_call x2, Pallas kernels, run_stats(): pl.pallas_call(stats_kernel, out_shape=out_shape, in_specs=[VM] * 7 if be...  6.7 us
    ppermute x1, starting transfers between devices, per_device(): lax.ppermute(qg_own, 'core', SWAP)  3.2 us
  transfers between devices with their start and end apart: 15, of which 9 were waited for; matrix products, arithmetic and copies ran while one was open for 3% of the time, Pallas kernels for 4%

profile of v4, /device:TPU:1, one launch (start us, length us, event | category | flops | bytes accessed | tf_op | source)
XLA Modules:
  0.0 100.6 jit_solution(5964340082472953946)
XLA Ops:
  0.6 0.0 copy-start
  0.6 2.0 %pack.1 = bf16[16,4,32,128]{3,2,1,0:T(8,128)(2,1)} custom-call(bf16[32,2048]{1,0:T(8,128)(2,1)} %refs_0_.1, bf16[32,2048]{1,0:T(8,128)(2,1)} %refs_1_.1, bf16[32,2048]{1,0:T(8,128)(2,1)} %refs_2_.1, bf16[32,2048]{1,0:T(8,128)(2,1)} %refs_3_.1), custom_call_target="tpu_custom_call" | custom-call | tf_op jit(solution)/shard_map/pack/pallas_call | solution.py:327
  2.7 10.1 %all-to-all-start = ((bf16[16,4,32,128]{3,2,1,0:T(8,128)(2,1)}), bf16[16,4,32,128]{3,2,1,0:T(8,128)(2,1)S(1)}, u32[]{:S(2)}, u32[]{:S(2)}) async-start(bf16[16,4,32,128]{3,2,1,0:T(8,128)(2,1)} %pack.1), calls=%async_computation | async-start | bytes 1048576 | tf_op jit(solution)/shard_map/all_to_all | solution.py:235
  12.8 0.7 multiply_add_fusion
  13.5 0.1 broadcast_add_fusion
  13.6 0.1 add.46
  13.6 0.1 constant_dynamic-slice_fusion
  13.8 0.1 copy.14
  13.8 0.8 dynamic-slice_bitcast_fusion
  14.6 0.1 select_bitcast_fusion
  14.7 0.7 compare_reduce_fusion
  15.4 0.1 broadcast_in_dim.22
  15.5 0.1 copy.17
  15.6 10.9 %all-to-all-done = bf16[16,4,32,128]{3,2,1,0:T(8,128)(2,1)S(1)} async-done(((bf16[16,4,32,128]{3,2,1,0:T(8,128)(2,1)}), bf16[16,4,32,128]{3,2,1,0:T(8,128)(2,1)S(1)}, u32[]{:S(2)}, u32[]{:S(2)}) %all-to-all-start) | async-done | bytes 524320 | tf_op jit(solution)/shard_map/all_to_all | solution.py:235
  26.6 2.7 %collective-permute-start.4 = (bf16[16,2,32,128]{3,2,1,0:T(8,128)(2,1)S(1)}, bf16[16,2,32,128]{3,2,1,0:T(8,128)(2,1)S(1)}, u32[]{:S(2)}, u32[]{:S(2)}) collective-permute-start(bf16[16,2,32,128]{3,2,1,0:T(8,128)(2,1)S(1)} %get-tuple-element.44.refs_1_), channel_id=1, source_target_pairs={{0,2},{2,0},{1,3},{3,1},{4,6},{6,4},{5,7},{7,5},{8,10},{10,8},{9,1... | collective-permute-start | bytes 786440 | tf_op jit(solution)/shard_map/ppermute | solution.py:239
  29.3 0.1 pad_add_fusion.refs_0_
  29.4 3.2 %collective-permute-start.3 = (bf16[16,2,32,128]{3,2,1,0:T(8,128)(2,1)S(1)}, bf16[16,2,32,128]{3,2,1,0:T(8,128)(2,1)S(1)}, u32[]{:S(2)}, u32[]{:S(2)}) collective-permute-start(bf16[16,2,32,128]{3,2,1,0:T(8,128)(2,1)S(1)} %get-tuple-element.44.refs_1_), channel_id=1, source_target_pairs={{0,16},{16,0},{1,17},{17,1},{2,18},{18,2},{3,19},{19,3},{4,20},{20... | collective-permute-start | bytes 786440 | tf_op jit(solution)/shard_map/ppermute | solution.py:242
  32.6 2.8 %collective-permute-start.2 = (bf16[16,2,32,128]{3,2,1,0:T(8,128)(2,1)S(1)}, bf16[16,2,32,128]{3,2,1,0:T(8,128)(2,1)S(1)}, u32[]{:S(2)}, u32[]{:S(2)}) collective-permute-start(bf16[16,2,32,128]{3,2,1,0:T(8,128)(2,1)S(1)} %get-tuple-element.45.refs_5_.refs_1_), channel_id=1, source_target_pairs={{0,8},{4,12},{8,0},{12,4},{1,9},{5,13},{9,1},{13,5},{2,10},{6,14},... | collective-permute-start | bytes 786440 | tf_op jit(solution)/shard_map/ppermute | solution.py:211
  35.3 0.3 collective-permute-start.1
  35.7 0.6 collective-permute-start
  36.2 1.3 %collective-permute-start.5 = (bf16[16,2,32,128]{3,2,1,0:T(8,128)(2,1)S(1)}, bf16[16,2,32,128]{3,2,1,0:T(8,128)(2,1)S(1)}, u32[]{:S(2)}, u32[]{:S(2)}) collective-permute-start(bf16[16,2,32,128]{3,2,1,0:T(8,128)(2,1)S(1)} %collective-permute-done.4.refs_3_), channel_id=1, source_target_pairs={{0,16},{16,0},{1,17},{17,1},{2,18},{18,2},{3,19},{19,3},{4,20},{20... | collective-permute-start | bytes 786440 | tf_op jit(solution)/shard_map/ppermute | solution.py:244
  37.5 4.5 %collective-permute-done.2.refs_6_.refs_4_ = bf16[16,2,32,128]{3,2,1,0:T(8,128)(2,1)S(1)} collective-permute-done((bf16[16,2,32,128]{3,2,1,0:T(8,128)(2,1)S(1)}, bf16[16,2,32,128]{3,2,1,0:T(8,128)(2,1)S(1)}, u32[]{:S(2)}, u32[]{:S(2)}) %collective-permute-start.2) | collective-permute-done | bytes 262176 | tf_op jit(solution)/shard_map/ppermute | solution.py:211
  42.0 0.0 collective-permute-done.5.refs_4_
  42.0 3.5 %stats_near.1 = (f32[3,8,256]{2,1,0:T(8,128)S(1)}, f32[128,2048]{1,0:T(8,128)S(1)}, bf16[1024,2048]{1,0:T(8,128)(2,1)S(1)}, bf16[2,16,2,32,128]{4,3,2,1,0:T(8,128)(2,1)S(1)}, bf16[2,16,2,32,128]{4,3,2,1,0:T(8,128)(2,1)S(1)}) custom-call(s32[2]{0:T(128)S(1)} %pad_add_fusion.refs_0_, bf16[16,2,32,128]{3,2,1,0:T(8,128)(2,1)S(1)} %get-tuple-element.44.refs_1_, ...), custom_call_target="tpu_custom_call" | custom-call | flops 1073741824 | bytes 4194304 | tf_op jit(solution)/shard_map/stats_near/pallas_call | solution.py:175
  45.5 2.2 %collective-permute-done.1.refs_3_ = bf16[16,2,32,128]{3,2,1,0:T(8,128)(2,1)S(1)} collective-permute-done((bf16[16,2,32,128]{3,2,1,0:T(8,128)(2,1)S(1)}, bf16[16,2,32,128]{3,2,1,0:T(8,128)(2,1)S(1)}, u32[]{:S(2)}, u32[]{:S(2)}) %collective-permute-start.1) | collective-permute-done | bytes 262176 | tf_op jit(solution)/shard_map/ppermute | solution.py:211
  47.7 0.2 collective-permute-done.refs_2_
  47.9 3.2 %stats_far.1 = (f32[3,8,256]{2,1,0:T(8,128)S(1)}, f32[128,2048]{1,0:T(8,128)S(1)}, bf16[1024,2048]{1,0:T(8,128)(2,1)S(1)}, f32[2,8,256]{2,1,0:T(8,128)S(1)}) custom-call(bf16[2,16,2,32,128]{4,3,2,1,0:T(8,128)(2,1)S(1)} %get-tuple-element.23.refs_0_.refs_5_, bf16[2,16,2,32,128]{4,3,2,1,0:T(8,128)(2,1)S(1)} %get-tuple-element.24.refs_1_.refs_6_, ...), custom_call_target="tpu_custom_call" | custom-call | flops 1073741824 | bytes 4194304 | tf_op jit(solution)/shard_map/stats_far/pallas_call | solution.py:175
  51.1 0.9 collective-permute-start.8
  52.0 2.6 %collective-permute-start.7 = (f32[3,8,256]{2,1,0:T(8,128)S(1)}, f32[3,8,256]{2,1,0:T(8,128)S(1)}, u32[]{:S(2)}, u32[]{:S(2)}) collective-permute-start(f32[3,8,256]{2,1,0:T(8,128)S(1)} %get-tuple-element.31.refs_11_), channel_id=1, source_target_pairs={{0,2},{2,0},{1,3},{3,1},{4,6},{6,4},{5,7},{7,5},{8,10},{10,8},{9,1... | collective-permute-start | bytes 73736 | tf_op jit(solution)/shard_map/ppermute | solution.py:255
  54.7 0.2 collective-permute-start.6
  54.8 1.5 %collective-permute-done.8.refs_14_ = f32[3,8,256]{2,1,0:T(8,128)S(1)} collective-permute-done((f32[3,8,256]{2,1,0:T(8,128)S(1)}, f32[3,8,256]{2,1,0:T(8,128)S(1)}, u32[]{:S(2)}, u32[]{:S(2)}) %collective-permute-start.8) | collective-permute-done | bytes 24608 | tf_op jit(solution)/shard_map/ppermute | solution.py:256
  56.3 0.5 collective-permute-done.7.refs_13_
  56.8 0.0 collective-permute-done.6.refs_12_
  56.8 8.8 %grads.1 = (bf16[2,2,16,32,128]{4,3,2,1,0:T(8,128)(2,1)S(1)}, bf16[2,2,16,32,128]{4,3,2,1,0:T(8,128)(2,1)S(1)}, bf16[2048,128]{1,0:T(8,128)(2,1)S(1)}, bf16[2048,128]{1,0:T(8,128)(2,1)S(1)}) custom-call(s32[2]{0:T(128)S(1)} %pad_add_fusion.refs_0_, bf16[16,2,32,128]{3,2,1,0:T(8,128)(2,1)S(1)} %get-tuple-element.45.refs_5_.refs_1_, ...), custom_call_target="tpu_custom_call" | custom-call | flops 4294967296 | bytes 4194304 | tf_op jit(solution)/shard_map/grads/pallas_call | solution.py:195
  65.7 0.6 collective-permute-start.12
  66.3 0.1 slice_bitcast_fusion
  66.4 2.8 %collective-permute-start.9 = (bf16[2,512,128]{2,1,0:T(8,128)(2,1)S(1)}, bf16[2,512,128]{2,1,0:T(8,128)(2,1)S(1)}, u32[]{:S(2)}, u32[]{:S(2)}) collective-permute-start(bf16[2,512,128]{2,1,0:T(8,128)(2,1)S(1)} %pad_maximum_fusion), channel_id=1, source_target_pairs={{0,8},{4,12},{8,0},{12,4},{1,9},{5,13},{9,1},{13,5},{2,10},{6,14},... | collective-permute-start | bytes 786440 | tf_op jit(solution)/shard_map/ppermute | solution.py:211
  69.2 0.4 collective-permute-start.10
  69.6 0.7 collective-permute-start.11
  70.3 0.1 add_core.1
  70.4 2.7 %collective-permute-start.13 = (bf16[2,16,32,128]{3,2,1,0:T(8,128)(2,1)S(1)}, bf16[2,16,32,128]{3,2,1,0:T(8,128)(2,1)S(1)}, u32[]{:S(2)}, u32[]{:S(2)}) collective-permute-start(bf16[2,16,32,128]{3,2,1,0:T(8,128)(2,1)S(1)} %get-tuple-element.37), channel_id=1, source_target_pairs={{0,2},{2,0},{1,3},{3,1},{4,6},{6,4},{5,7},{7,5},{8,10},{10,8},{9,1... | collective-permute-start | bytes 786440 | tf_op jit(solution)/shard_map/ppermute | solution.py:266
  73.0 2.9 %collective-permute-done.9.refs_0_ = bf16[2,512,128]{2,1,0:T(8,128)(2,1)S(1)} collective-permute-done((bf16[2,512,128]{2,1,0:T(8,128)(2,1)S(1)}, bf16[2,512,128]{2,1,0:T(8,128)(2,1)S(1)}, u32[]{:S(2)}, u32[]{:S(2)}) %collective-permute-start.9) | collective-permute-done | bytes 262176 | tf_op jit(solution)/shard_map/ppermute | solution.py:211
  75.9 5.7 %collective-permute-done.10.refs_1_ = bf16[2,512,128]{2,1,0:T(8,128)(2,1)S(1)} collective-permute-done((bf16[2,512,128]{2,1,0:T(8,128)(2,1)S(1)}, bf16[2,512,128]{2,1,0:T(8,128)(2,1)S(1)}, u32[]{:S(2)}, u32[]{:S(2)}) %collective-permute-start.10) | collective-permute-done | bytes 262176 | tf_op jit(solution)/shard_map/ppermute | solution.py:211
  81.6 0.2 collective-permute-done.11.refs_2_
  81.8 0.0 collective-permute-done.13.refs_4_
  81.8 0.2 add_up.1
  82.0 17.8 %all_to_all.10.src_ref = bf16[16,4,32,128]{3,2,1,0:T(8,128)(2,1)S(1)} all-to-all(bf16[16,4,32,128]{3,2,1,0:T(8,128)(2,1)S(1)} %add_up.1), channel_id=1, replica_groups=mesh['z'=8,'core'=2,'x'=4,'y1'=2,'y0'=2] {'y0','z'}, dimensions={0} | all-to-all | bytes 1048576 | tf_op jit(solution)/shard_map/all_to_all | solution.py:267
  99.7 0.9 unpack.1
  (11 shorter events, 0.2 us)
Async XLA Ops:
  0.6 13.0 %copy-start = (s32[16,64,38]{1,0,2:T(8,128)S(1)}, s32[16,64,38]{1,0,2:T(8,128)}, u32[]{:S(2)}) copy-start(s32[16,64,38]{1,0,2:T(8,128)} %param.11) | copy-start | bytes 466948
  2.7 23.9 %all-to-all-start = ((bf16[16,4,32,128]{3,2,1,0:T(8,128)(2,1)}), bf16[16,4,32,128]{3,2,1,0:T(8,128)(2,1)S(1)}, u32[]{:S(2)}, u32[]{:S(2)}) async-start(bf16[16,4,32,128]{3,2,1,0:T(8,128)(2,1)} %pack.1), calls=%async_computation | async-start | bytes 1048576 | tf_op jit(solution)/shard_map/all_to_all | solution.py:235
  26.6 9.6 %collective-permute-start.4 = (bf16[16,2,32,128]{3,2,1,0:T(8,128)(2,1)S(1)}, bf16[16,2,32,128]{3,2,1,0:T(8,128)(2,1)S(1)}, u32[]{:S(2)}, u32[]{:S(2)}) collective-permute-start(bf16[16,2,32,128]{3,2,1,0:T(8,128)(2,1)S(1)} %get-tuple-element.44.refs_1_), channel_id=1, source_target_pairs={{0,2},{2,0},{1,3},{3,1},{4,6},{6,4},{5,7},{7,5},{8,10},{10,8},{9,1... | collective-permute-start | bytes 786440 | tf_op jit(solution)/shard_map/ppermute | solution.py:239
  29.4 8.1 %collective-permute-start.3 = (bf16[16,2,32,128]{3,2,1,0:T(8,128)(2,1)S(1)}, bf16[16,2,32,128]{3,2,1,0:T(8,128)(2,1)S(1)}, u32[]{:S(2)}, u32[]{:S(2)}) collective-permute-start(bf16[16,2,32,128]{3,2,1,0:T(8,128)(2,1)S(1)} %get-tuple-element.44.refs_1_), channel_id=1, source_target_pairs={{0,16},{16,0},{1,17},{17,1},{2,18},{18,2},{3,19},{19,3},{4,20},{20... | collective-permute-start | bytes 786440 | tf_op jit(solution)/shard_map/ppermute | solution.py:242
  32.6 9.4 %collective-permute-start.2 = (bf16[16,2,32,128]{3,2,1,0:T(8,128)(2,1)S(1)}, bf16[16,2,32,128]{3,2,1,0:T(8,128)(2,1)S(1)}, u32[]{:S(2)}, u32[]{:S(2)}) collective-permute-start(bf16[16,2,32,128]{3,2,1,0:T(8,128)(2,1)S(1)} %get-tuple-element.45.refs_5_.refs_1_), channel_id=1, source_target_pairs={{0,8},{4,12},{8,0},{12,4},{1,9},{5,13},{9,1},{13,5},{2,10},{6,14},... | collective-permute-start | bytes 786440 | tf_op jit(solution)/shard_map/ppermute | solution.py:211
  35.3 12.4 %collective-permute-start.1 = (bf16[16,2,32,128]{3,2,1,0:T(8,128)(2,1)S(1)}, bf16[16,2,32,128]{3,2,1,0:T(8,128)(2,1)S(1)}, u32[]{:S(2)}, u32[]{:S(2)}) collective-permute-start(bf16[16,2,32,128]{3,2,1,0:T(8,128)(2,1)S(1)} %get-tuple-element.45.refs_5_.refs_1_), channel_id=1, source_target_pairs={{0,4},{4,0},{8,12},{12,8},{1,5},{5,1},{9,13},{13,9},{2,6},{6,2},{1... | collective-permute-start | bytes 786440 | tf_op jit(solution)/shard_map/ppermute | solution.py:211
  35.7 12.3 %collective-permute-start = (bf16[16,2,32,128]{3,2,1,0:T(8,128)(2,1)S(1)}, bf16[16,2,32,128]{3,2,1,0:T(8,128)(2,1)S(1)}, u32[]{:S(2)}, u32[]{:S(2)}) collective-permute-start(bf16[16,2,32,128]{3,2,1,0:T(8,128)(2,1)S(1)} %get-tuple-element.45.refs_5_.refs_1_), channel_id=1, source_target_pairs={{0,12},{4,8},{8,4},{12,0},{1,13},{5,9},{9,5},{13,1},{2,14},{6,10},... | collective-permute-start | bytes 786440 | tf_op jit(solution)/shard_map/ppermute | solution.py:211
  36.2 5.8 %collective-permute-start.5 = (bf16[16,2,32,128]{3,2,1,0:T(8,128)(2,1)S(1)}, bf16[16,2,32,128]{3,2,1,0:T(8,128)(2,1)S(1)}, u32[]{:S(2)}, u32[]{:S(2)}) collective-permute-start(bf16[16,2,32,128]{3,2,1,0:T(8,128)(2,1)S(1)} %collective-permute-done.4.refs_3_), channel_id=1, source_target_pairs={{0,16},{16,0},{1,17},{17,1},{2,18},{18,2},{3,19},{19,3},{4,20},{20... | collective-permute-start | bytes 786440 | tf_op jit(solution)/shard_map/ppermute | solution.py:244
  51.1 5.2 %collective-permute-start.8 = (f32[3,8,256]{2,1,0:T(8,128)S(1)}, f32[3,8,256]{2,1,0:T(8,128)S(1)}, u32[]{:S(2)}, u32[]{:S(2)}) collective-permute-start(f32[3,8,256]{2,1,0:T(8,128)S(1)} %get-tuple-element.31.refs_11_), channel_id=1, source_target_pairs={{0,18},{2,16},{16,2},{18,0},{1,19},{3,17},{17,3},{19,1},{4,22},{6,... | collective-permute-start | bytes 73736 | tf_op jit(solution)/shard_map/ppermute | solution.py:256
  52.0 4.8 %collective-permute-start.7 = (f32[3,8,256]{2,1,0:T(8,128)S(1)}, f32[3,8,256]{2,1,0:T(8,128)S(1)}, u32[]{:S(2)}, u32[]{:S(2)}) collective-permute-start(f32[3,8,256]{2,1,0:T(8,128)S(1)} %get-tuple-element.31.refs_11_), channel_id=1, source_target_pairs={{0,2},{2,0},{1,3},{3,1},{4,6},{6,4},{5,7},{7,5},{8,10},{10,8},{9,1... | collective-permute-start | bytes 73736 | tf_op jit(solution)/shard_map/ppermute | solution.py:255
  54.7 2.2 %collective-permute-start.6 = (f32[3,8,256]{2,1,0:T(8,128)S(1)}, f32[3,8,256]{2,1,0:T(8,128)S(1)}, u32[]{:S(2)}, u32[]{:S(2)}) collective-permute-start(f32[3,8,256]{2,1,0:T(8,128)S(1)} %get-tuple-element.31.refs_11_), channel_id=1, source_target_pairs={{0,16},{16,0},{1,17},{17,1},{2,18},{18,2},{3,19},{19,3},{4,20},{20... | collective-permute-start | bytes 73736 | tf_op jit(solution)/shard_map/ppermute | solution.py:254
  65.7 4.6 %collective-permute-start.12 = (bf16[2,2,16,32,128]{4,3,2,1,0:T(8,128)(2,1)S(1)}, bf16[2,2,16,32,128]{4,3,2,1,0:T(8,128)(2,1)S(1)}, u32[]{:S(2)}, u32[]{:S(2)}) collective-permute-start(bf16[2,2,16,32,128]{4,3,2,1,0:T(8,128)(2,1)S(1)} %get-tuple-element.35), channel_id=1, source_target_pairs={{0,16},{16,0},{1,17},{17,1},{2,18},{18,2},{3,19},{19,3},{4,20},{20... | collective-permute-start | bytes 1572872 | tf_op jit(solution)/shard_map/ppermute | solution.py:265
  66.4 9.6 %collective-permute-start.9 = (bf16[2,512,128]{2,1,0:T(8,128)(2,1)S(1)}, bf16[2,512,128]{2,1,0:T(8,128)(2,1)S(1)}, u32[]{:S(2)}, u32[]{:S(2)}) collective-permute-start(bf16[2,512,128]{2,1,0:T(8,128)(2,1)S(1)} %pad_maximum_fusion), channel_id=1, source_target_pairs={{0,8},{4,12},{8,0},{12,4},{1,9},{5,13},{9,1},{13,5},{2,10},{6,14},... | collective-permute-start | bytes 786440 | tf_op jit(solution)/shard_map/ppermute | solution.py:211
  69.2 12.4 %collective-permute-start.10 = (bf16[2,512,128]{2,1,0:T(8,128)(2,1)S(1)}, bf16[2,512,128]{2,1,0:T(8,128)(2,1)S(1)}, u32[]{:S(2)}, u32[]{:S(2)}) collective-permute-start(bf16[2,512,128]{2,1,0:T(8,128)(2,1)S(1)} %pad_maximum_fusion.1), channel_id=1, source_target_pairs={{0,4},{4,0},{8,12},{12,8},{1,5},{5,1},{9,13},{13,9},{2,6},{6,2},{1... | collective-permute-start | bytes 786440 | tf_op jit(solution)/shard_map/ppermute | solution.py:211
  69.6 12.2 %collective-permute-start.11 = (bf16[2,512,128]{2,1,0:T(8,128)(2,1)S(1)}, bf16[2,512,128]{2,1,0:T(8,128)(2,1)S(1)}, u32[]{:S(2)}, u32[]{:S(2)}) collective-permute-start(bf16[2,512,128]{2,1,0:T(8,128)(2,1)S(1)} %pad_maximum_fusion.2), channel_id=1, source_target_pairs={{0,12},{4,8},{8,4},{12,0},{1,13},{5,9},{9,5},{13,1},{2,14},{6,10},... | collective-permute-start | bytes 786440 | tf_op jit(solution)/shard_map/ppermute | solution.py:211
  70.4 11.4 %collective-permute-start.13 = (bf16[2,16,32,128]{3,2,1,0:T(8,128)(2,1)S(1)}, bf16[2,16,32,128]{3,2,1,0:T(8,128)(2,1)S(1)}, u32[]{:S(2)}, u32[]{:S(2)}) collective-permute-start(bf16[2,16,32,128]{3,2,1,0:T(8,128)(2,1)S(1)} %get-tuple-element.37), channel_id=1, source_target_pairs={{0,2},{2,0},{1,3},{3,1},{4,6},{6,4},{5,7},{7,5},{8,10},{10,8},{9,1... | collective-permute-start | bytes 786440 | tf_op jit(solution)/shard_map/ppermute | solution.py:266

commit v5 on v4

--- a/solution.py
+++ b/solution.py
@@ -96,7 +96,7 @@
         finish(2 * i + 1, xb_s, top_b)
         return top_a
 
-    lax.fori_loop(0, 4, pair, score(0, xa_s), unroll=2)
+    lax.fori_loop(0, 4, pair, score(0, xa_s), unroll=4)
 
 
 def grad_kernel(*refs):
@@ -156,12 +156,6 @@
 ROWS5 = pltpu.VMEM((2, 16, 2, 32, DH), jnp.bfloat16)
 
 
-def cost(products):
-    return pl.CostEstimate(
-        flops=products * 2 * 2048 * 2048 * DH, bytes_accessed=1 << 22, transcendentals=1 << 21
-    )
-
-
 def run_stats(rows, kv, bias, *before):
     out_shape = [
         jax.ShapeDtypeStruct((3, 8, QB), jnp.float32),
@@ -184,7 +178,6 @@
             pltpu.VMEM((1024, QB), jnp.float32),
         ],
         compiler_params=PARAMS,
-        cost_estimate=cost(1),
         name="stats_far" if before else "stats_near",
     )(*rows, *kv, bias, *before)
 
@@ -202,7 +195,6 @@
         + [pltpu.VMEM((2048, DH), jnp.float32)] * 2
         + [pltpu.VMEM((8, QB), jnp.float32)] * 2,
         compiler_params=PARAMS,
-        cost_estimate=cost(4),
         name="grads",
     )(place, *kv, *rows, *e, part, acc, *stats)
 

time: 102 us -> 102 us (level)
  transfers between devices with their start and end apart: 15 -> 15, of which waited for: 9 -> 9; matrix products, arithmetic and copies ran while one was open for 3% -> 3% of each run, Pallas kernels for 4% -> 3%
where the time goes in v5:
time: 102 us; the launch traced here: 100 us
  starting transfers between devices  31.8 us (31%)
  waiting for transfers between devices  29 us (28%)
  Pallas kernels  18 us (18%)
  blocking collectives  17.6 us (17%)
  other arithmetic  1.67 us (2%)
  local copies, waits for them, and re-layouts  1.36 us (1%)
    all_to_all x1, blocking collectives, per_device(): lax.all_to_all(send, HEADS, split_axis=0, concat_axis=0, tiled=True)  17.6 us
    ppermute x6, waiting for transfers between devices, swap(): return lax.ppermute(a, 'x', [(i, i ^ j) for i in range(4)])  16 us
    all_to_all x1, waiting for transfers between devices, per_device(): got = lax.all_to_all(packed, HEADS, split_axis=0, concat_axis=0, tiled=True)  10.9 us
    all_to_all x1, starting transfers between devices, per_device(): got = lax.all_to_all(packed, HEADS, split_axis=0, concat_axis=0, tiled=True)  10.1 us
    pallas_call x1, Pallas kernels, run_grads(): pl.pallas_call(grad_kernel, out_shape=(side, side, keys, keys), in_specs=...  8.83 us
    ppermute x6, starting transfers between devices, swap(): return lax.ppermute(a, 'x', [(i, i ^ j) for i in range(4)])  7.45 us
    pallas_call x2, Pallas kernels, run_stats(): pl.pallas_call(stats_kernel, out_shape=out_shape, in_specs=[VM] * 7 if be...  5.98 us
    ppermute x1, starting transfers between devices, per_device(): lax.ppermute(qg_own, 'core', SWAP)  3.2 us
  transfers between devices with their start and end apart: 15, of which 9 were waited for; matrix products, arithmetic and copies ran while one was open for 3% of the time, Pallas kernels for 3%

profile of v5, /device:TPU:1, one launch (start us, length us, event | category | flops | bytes accessed | tf_op | source)
XLA Modules:
  0.0 100.1 jit_solution(16193601356203902947)
XLA Ops:
  0.6 0.0 copy-start
  0.6 2.0 %pack.1 = bf16[16,4,32,128]{3,2,1,0:T(8,128)(2,1)} custom-call(bf16[32,2048]{1,0:T(8,128)(2,1)} %refs_0_.1, bf16[32,2048]{1,0:T(8,128)(2,1)} %refs_1_.1, bf16[32,2048]{1,0:T(8,128)(2,1)} %refs_2_.1, bf16[32,2048]{1,0:T(8,128)(2,1)} %refs_3_.1), custom_call_target="tpu_custom_call" | custom-call | tf_op jit(solution)/shard_map/pack/pallas_call | solution.py:319
  2.7 10.1 %all-to-all-start = ((bf16[16,4,32,128]{3,2,1,0:T(8,128)(2,1)}), bf16[16,4,32,128]{3,2,1,0:T(8,128)(2,1)S(1)}, u32[]{:S(2)}, u32[]{:S(2)}) async-start(bf16[16,4,32,128]{3,2,1,0:T(8,128)(2,1)} %pack.1), calls=%async_computation | async-start | bytes 1048576 | tf_op jit(solution)/shard_map/all_to_all | solution.py:227
  12.8 0.7 multiply_add_fusion
  13.5 0.1 broadcast_add_fusion
  13.6 0.1 add.46
  13.6 0.1 constant_dynamic-slice_fusion
  13.8 0.1 copy.14
  13.8 0.8 dynamic-slice_bitcast_fusion
  14.6 0.1 select_bitcast_fusion
  14.7 0.7 compare_reduce_fusion
  15.4 0.1 broadcast_in_dim.22
  15.5 0.1 copy.17
  15.6 10.9 %all-to-all-done = bf16[16,4,32,128]{3,2,1,0:T(8,128)(2,1)S(1)} async-done(((bf16[16,4,32,128]{3,2,1,0:T(8,128)(2,1)}), bf16[16,4,32,128]{3,2,1,0:T(8,128)(2,1)S(1)}, u32[]{:S(2)}, u32[]{:S(2)}) %all-to-all-start) | async-done | bytes 524320 | tf_op jit(solution)/shard_map/all_to_all | solution.py:227
  26.6 2.7 %collective-permute-start.4 = (bf16[16,2,32,128]{3,2,1,0:T(8,128)(2,1)S(1)}, bf16[16,2,32,128]{3,2,1,0:T(8,128)(2,1)S(1)}, u32[]{:S(2)}, u32[]{:S(2)}) collective-permute-start(bf16[16,2,32,128]{3,2,1,0:T(8,128)(2,1)S(1)} %get-tuple-element.44.refs_1_), channel_id=1, source_target_pairs={{0,2},{2,0},{1,3},{3,1},{4,6},{6,4},{5,7},{7,5},{8,10},{10,8},{9,1... | collective-permute-start | bytes 786440 | tf_op jit(solution)/shard_map/ppermute | solution.py:231
  29.3 0.1 pad_add_fusion.refs_0_
  29.4 3.2 %collective-permute-start.3 = (bf16[16,2,32,128]{3,2,1,0:T(8,128)(2,1)S(1)}, bf16[16,2,32,128]{3,2,1,0:T(8,128)(2,1)S(1)}, u32[]{:S(2)}, u32[]{:S(2)}) collective-permute-start(bf16[16,2,32,128]{3,2,1,0:T(8,128)(2,1)S(1)} %get-tuple-element.44.refs_1_), channel_id=1, source_target_pairs={{0,16},{16,0},{1,17},{17,1},{2,18},{18,2},{3,19},{19,3},{4,20},{20... | collective-permute-start | bytes 786440 | tf_op jit(solution)/shard_map/ppermute | solution.py:234
  32.6 2.8 %collective-permute-start.2 = (bf16[16,2,32,128]{3,2,1,0:T(8,128)(2,1)S(1)}, bf16[16,2,32,128]{3,2,1,0:T(8,128)(2,1)S(1)}, u32[]{:S(2)}, u32[]{:S(2)}) collective-permute-start(bf16[16,2,32,128]{3,2,1,0:T(8,128)(2,1)S(1)} %get-tuple-element.45.refs_5_.refs_1_), channel_id=1, source_target_pairs={{0,8},{4,12},{8,0},{12,4},{1,9},{5,13},{9,1},{13,5},{2,10},{6,14},... | collective-permute-start | bytes 786440 | tf_op jit(solution)/shard_map/ppermute | solution.py:203
  35.3 0.3 collective-permute-start.1
  35.7 0.6 collective-permute-start
  36.2 0.0 collective-permute-done.4.refs_3_
  36.2 1.3 %collective-permute-start.5 = (bf16[16,2,32,128]{3,2,1,0:T(8,128)(2,1)S(1)}, bf16[16,2,32,128]{3,2,1,0:T(8,128)(2,1)S(1)}, u32[]{:S(2)}, u32[]{:S(2)}) collective-permute-start(bf16[16,2,32,128]{3,2,1,0:T(8,128)(2,1)S(1)} %collective-permute-done.4.refs_3_), channel_id=1, source_target_pairs={{0,16},{16,0},{1,17},{17,1},{2,18},{18,2},{3,19},{19,3},{4,20},{20... | collective-permute-start | bytes 786440 | tf_op jit(solution)/shard_map/ppermute | solution.py:236
  37.5 0.0 collective-permute-done.3.refs_2_
  37.5 4.5 %collective-permute-done.2.refs_6_.refs_4_ = bf16[16,2,32,128]{3,2,1,0:T(8,128)(2,1)S(1)} collective-permute-done((bf16[16,2,32,128]{3,2,1,0:T(8,128)(2,1)S(1)}, bf16[16,2,32,128]{3,2,1,0:T(8,128)(2,1)S(1)}, u32[]{:S(2)}, u32[]{:S(2)}) %collective-permute-start.2) | collective-permute-done | bytes 262176 | tf_op jit(solution)/shard_map/ppermute | solution.py:203
  42.0 0.0 collective-permute-done.5.refs_4_
  42.0 3.2 %stats_near.1 = (f32[3,8,256]{2,1,0:T(8,128)S(1)}, f32[128,2048]{1,0:T(8,128)S(1)}, bf16[1024,2048]{1,0:T(8,128)(2,1)S(1)}, bf16[2,16,2,32,128]{4,3,2,1,0:T(8,128)(2,1)S(1)}, bf16[2,16,2,32,128]{4,3,2,1,0:T(8,128)(2,1)S(1)}) custom-call(s32[2]{0:T(128)S(1)} %pad_add_fusion.refs_0_, bf16[16,2,32,128]{3,2,1,0:T(8,128)(2,1)S(1)} %get-tuple-element.44.refs_1_, ...), custom_call_target="tpu_custom_call" | custom-call | tf_op jit(solution)/shard_map/stats_near/pallas_call | solution.py:169
  45.2 2.5 %collective-permute-done.1.refs_3_ = bf16[16,2,32,128]{3,2,1,0:T(8,128)(2,1)S(1)} collective-permute-done((bf16[16,2,32,128]{3,2,1,0:T(8,128)(2,1)S(1)}, bf16[16,2,32,128]{3,2,1,0:T(8,128)(2,1)S(1)}, u32[]{:S(2)}, u32[]{:S(2)}) %collective-permute-start.1) | collective-permute-done | bytes 262176 | tf_op jit(solution)/shard_map/ppermute | solution.py:203
  47.7 0.2 collective-permute-done.refs_2_
  47.9 2.8 %stats_far.1 = (f32[3,8,256]{2,1,0:T(8,128)S(1)}, f32[128,2048]{1,0:T(8,128)S(1)}, bf16[1024,2048]{1,0:T(8,128)(2,1)S(1)}, f32[2,8,256]{2,1,0:T(8,128)S(1)}) custom-call(bf16[2,16,2,32,128]{4,3,2,1,0:T(8,128)(2,1)S(1)} %get-tuple-element.23.refs_0_.refs_5_, bf16[2,16,2,32,128]{4,3,2,1,0:T(8,128)(2,1)S(1)} %get-tuple-element.24.refs_1_.refs_6_, ...), custom_call_target="tpu_custom_call" | custom-call | tf_op jit(solution)/shard_map/stats_far/pallas_call | solution.py:169
  50.8 0.9 collective-permute-start.8
  51.7 2.6 %collective-permute-start.7 = (f32[3,8,256]{2,1,0:T(8,128)S(1)}, f32[3,8,256]{2,1,0:T(8,128)S(1)}, u32[]{:S(2)}, u32[]{:S(2)}) collective-permute-start(f32[3,8,256]{2,1,0:T(8,128)S(1)} %get-tuple-element.31.refs_11_), channel_id=1, source_target_pairs={{0,2},{2,0},{1,3},{3,1},{4,6},{6,4},{5,7},{7,5},{8,10},{10,8},{9,1... | collective-permute-start | bytes 73736 | tf_op jit(solution)/shard_map/ppermute | solution.py:247
  54.3 0.2 collective-permute-start.6
  54.5 1.5 %collective-permute-done.8.refs_14_ = f32[3,8,256]{2,1,0:T(8,128)S(1)} collective-permute-done((f32[3,8,256]{2,1,0:T(8,128)S(1)}, f32[3,8,256]{2,1,0:T(8,128)S(1)}, u32[]{:S(2)}, u32[]{:S(2)}) %collective-permute-start.8) | collective-permute-done | bytes 24608 | tf_op jit(solution)/shard_map/ppermute | solution.py:248
  56.0 0.5 collective-permute-done.7.refs_13_
  56.5 8.8 %grads.1 = (bf16[2,2,16,32,128]{4,3,2,1,0:T(8,128)(2,1)S(1)}, bf16[2,2,16,32,128]{4,3,2,1,0:T(8,128)(2,1)S(1)}, bf16[2048,128]{1,0:T(8,128)(2,1)S(1)}, bf16[2048,128]{1,0:T(8,128)(2,1)S(1)}) custom-call(s32[2]{0:T(128)S(1)} %pad_add_fusion.refs_0_, bf16[16,2,32,128]{3,2,1,0:T(8,128)(2,1)S(1)} %get-tuple-element.45.refs_5_.refs_1_, ...), custom_call_target="tpu_custom_call" | custom-call | tf_op jit(solution)/shard_map/grads/pallas_call | solution.py:188
  65.3 0.6 collective-permute-start.12
  65.9 0.1 slice_bitcast_fusion
  66.0 2.7 %collective-permute-start.9 = (bf16[2,512,128]{2,1,0:T(8,128)(2,1)S(1)}, bf16[2,512,128]{2,1,0:T(8,128)(2,1)S(1)}, u32[]{:S(2)}, u32[]{:S(2)}) collective-permute-start(bf16[2,512,128]{2,1,0:T(8,128)(2,1)S(1)} %pad_maximum_fusion), channel_id=1, source_target_pairs={{0,8},{4,12},{8,0},{12,4},{1,9},{5,13},{9,1},{13,5},{2,10},{6,14},... | collective-permute-start | bytes 786440 | tf_op jit(solution)/shard_map/ppermute | solution.py:203
  68.8 0.4 collective-permute-start.10
  69.2 0.7 collective-permute-start.11
  69.9 0.1 add_core.1
  70.0 2.7 %collective-permute-start.13 = (bf16[2,16,32,128]{3,2,1,0:T(8,128)(2,1)S(1)}, bf16[2,16,32,128]{3,2,1,0:T(8,128)(2,1)S(1)}, u32[]{:S(2)}, u32[]{:S(2)}) collective-permute-start(bf16[2,16,32,128]{3,2,1,0:T(8,128)(2,1)S(1)} %get-tuple-element.37), channel_id=1, source_target_pairs={{0,2},{2,0},{1,3},{3,1},{4,6},{6,4},{5,7},{7,5},{8,10},{10,8},{9,1... | collective-permute-start | bytes 786440 | tf_op jit(solution)/shard_map/ppermute | solution.py:258
  72.7 2.9 %collective-permute-done.9.refs_0_ = bf16[2,512,128]{2,1,0:T(8,128)(2,1)S(1)} collective-permute-done((bf16[2,512,128]{2,1,0:T(8,128)(2,1)S(1)}, bf16[2,512,128]{2,1,0:T(8,128)(2,1)S(1)}, u32[]{:S(2)}, u32[]{:S(2)}) %collective-permute-start.9) | collective-permute-done | bytes 262176 | tf_op jit(solution)/shard_map/ppermute | solution.py:203
  75.6 5.6 %collective-permute-done.10.refs_1_ = bf16[2,512,128]{2,1,0:T(8,128)(2,1)S(1)} collective-permute-done((bf16[2,512,128]{2,1,0:T(8,128)(2,1)S(1)}, bf16[2,512,128]{2,1,0:T(8,128)(2,1)S(1)}, u32[]{:S(2)}, u32[]{:S(2)}) %collective-permute-start.10) | collective-permute-done | bytes 262176 | tf_op jit(solution)/shard_map/ppermute | solution.py:203
  81.2 0.3 collective-permute-done.11.refs_2_
  81.5 0.2 add_up.1
  81.6 17.6 %all_to_all.10.src_ref = bf16[16,4,32,128]{3,2,1,0:T(8,128)(2,1)S(1)} all-to-all(bf16[16,4,32,128]{3,2,1,0:T(8,128)(2,1)S(1)} %add_up.1), channel_id=1, replica_groups=mesh['z'=8,'core'=2,'x'=4,'y1'=2,'y0'=2] {'y0','z'}, dimensions={0} | all-to-all | bytes 1048576 | tf_op jit(solution)/shard_map/all_to_all | solution.py:259
  99.2 0.9 unpack.1
  (11 shorter events, 0.2 us)
Async XLA Ops:
  0.6 13.0 %copy-start = (s32[16,64,38]{1,0,2:T(8,128)S(1)}, s32[16,64,38]{1,0,2:T(8,128)}, u32[]{:S(2)}) copy-start(s32[16,64,38]{1,0,2:T(8,128)} %param.11) | copy-start | bytes 466948
  2.7 23.9 %all-to-all-start = ((bf16[16,4,32,128]{3,2,1,0:T(8,128)(2,1)}), bf16[16,4,32,128]{3,2,1,0:T(8,128)(2,1)S(1)}, u32[]{:S(2)}, u32[]{:S(2)}) async-start(bf16[16,4,32,128]{3,2,1,0:T(8,128)(2,1)} %pack.1), calls=%async_computation | async-start | bytes 1048576 | tf_op jit(solution)/shard_map/all_to_all | solution.py:227
  26.6 9.6 %collective-permute-start.4 = (bf16[16,2,32,128]{3,2,1,0:T(8,128)(2,1)S(1)}, bf16[16,2,32,128]{3,2,1,0:T(8,128)(2,1)S(1)}, u32[]{:S(2)}, u32[]{:S(2)}) collective-permute-start(bf16[16,2,32,128]{3,2,1,0:T(8,128)(2,1)S(1)} %get-tuple-element.44.refs_1_), channel_id=1, source_target_pairs={{0,2},{2,0},{1,3},{3,1},{4,6},{6,4},{5,7},{7,5},{8,10},{10,8},{9,1... | collective-permute-start | bytes 786440 | tf_op jit(solution)/shard_map/ppermute | solution.py:231
  29.4 8.1 %collective-permute-start.3 = (bf16[16,2,32,128]{3,2,1,0:T(8,128)(2,1)S(1)}, bf16[16,2,32,128]{3,2,1,0:T(8,128)(2,1)S(1)}, u32[]{:S(2)}, u32[]{:S(2)}) collective-permute-start(bf16[16,2,32,128]{3,2,1,0:T(8,128)(2,1)S(1)} %get-tuple-element.44.refs_1_), channel_id=1, source_target_pairs={{0,16},{16,0},{1,17},{17,1},{2,18},{18,2},{3,19},{19,3},{4,20},{20... | collective-permute-start | bytes 786440 | tf_op jit(solution)/shard_map/ppermute | solution.py:234
  32.6 9.4 %collective-permute-start.2 = (bf16[16,2,32,128]{3,2,1,0:T(8,128)(2,1)S(1)}, bf16[16,2,32,128]{3,2,1,0:T(8,128)(2,1)S(1)}, u32[]{:S(2)}, u32[]{:S(2)}) collective-permute-start(bf16[16,2,32,128]{3,2,1,0:T(8,128)(2,1)S(1)} %get-tuple-element.45.refs_5_.refs_1_), channel_id=1, source_target_pairs={{0,8},{4,12},{8,0},{12,4},{1,9},{5,13},{9,1},{13,5},{2,10},{6,14},... | collective-permute-start | bytes 786440 | tf_op jit(solution)/shard_map/ppermute | solution.py:203
  35.3 12.4 %collective-permute-start.1 = (bf16[16,2,32,128]{3,2,1,0:T(8,128)(2,1)S(1)}, bf16[16,2,32,128]{3,2,1,0:T(8,128)(2,1)S(1)}, u32[]{:S(2)}, u32[]{:S(2)}) collective-permute-start(bf16[16,2,32,128]{3,2,1,0:T(8,128)(2,1)S(1)} %get-tuple-element.45.refs_5_.refs_1_), channel_id=1, source_target_pairs={{0,4},{4,0},{8,12},{12,8},{1,5},{5,1},{9,13},{13,9},{2,6},{6,2},{1... | collective-permute-start | bytes 786440 | tf_op jit(solution)/shard_map/ppermute | solution.py:203
  35.7 12.3 %collective-permute-start = (bf16[16,2,32,128]{3,2,1,0:T(8,128)(2,1)S(1)}, bf16[16,2,32,128]{3,2,1,0:T(8,128)(2,1)S(1)}, u32[]{:S(2)}, u32[]{:S(2)}) collective-permute-start(bf16[16,2,32,128]{3,2,1,0:T(8,128)(2,1)S(1)} %get-tuple-element.45.refs_5_.refs_1_), channel_id=1, source_target_pairs={{0,12},{4,8},{8,4},{12,0},{1,13},{5,9},{9,5},{13,1},{2,14},{6,10},... | collective-permute-start | bytes 786440 | tf_op jit(solution)/shard_map/ppermute | solution.py:203
  36.2 5.8 %collective-permute-start.5 = (bf16[16,2,32,128]{3,2,1,0:T(8,128)(2,1)S(1)}, bf16[16,2,32,128]{3,2,1,0:T(8,128)(2,1)S(1)}, u32[]{:S(2)}, u32[]{:S(2)}) collective-permute-start(bf16[16,2,32,128]{3,2,1,0:T(8,128)(2,1)S(1)} %collective-permute-done.4.refs_3_), channel_id=1, source_target_pairs={{0,16},{16,0},{1,17},{17,1},{2,18},{18,2},{3,19},{19,3},{4,20},{20... | collective-permute-start | bytes 786440 | tf_op jit(solution)/shard_map/ppermute | solution.py:236
  50.8 5.3 %collective-permute-start.8 = (f32[3,8,256]{2,1,0:T(8,128)S(1)}, f32[3,8,256]{2,1,0:T(8,128)S(1)}, u32[]{:S(2)}, u32[]{:S(2)}) collective-permute-start(f32[3,8,256]{2,1,0:T(8,128)S(1)} %get-tuple-element.31.refs_11_), channel_id=1, source_target_pairs={{0,18},{2,16},{16,2},{18,0},{1,19},{3,17},{17,3},{19,1},{4,22},{6,... | collective-permute-start | bytes 73736 | tf_op jit(solution)/shard_map/ppermute | solution.py:248
  51.7 4.8 %collective-permute-start.7 = (f32[3,8,256]{2,1,0:T(8,128)S(1)}, f32[3,8,256]{2,1,0:T(8,128)S(1)}, u32[]{:S(2)}, u32[]{:S(2)}) collective-permute-start(f32[3,8,256]{2,1,0:T(8,128)S(1)} %get-tuple-element.31.refs_11_), channel_id=1, source_target_pairs={{0,2},{2,0},{1,3},{3,1},{4,6},{6,4},{5,7},{7,5},{8,10},{10,8},{9,1... | collective-permute-start | bytes 73736 | tf_op jit(solution)/shard_map/ppermute | solution.py:247
  54.3 2.2 %collective-permute-start.6 = (f32[3,8,256]{2,1,0:T(8,128)S(1)}, f32[3,8,256]{2,1,0:T(8,128)S(1)}, u32[]{:S(2)}, u32[]{:S(2)}) collective-permute-start(f32[3,8,256]{2,1,0:T(8,128)S(1)} %get-tuple-element.31.refs_11_), channel_id=1, source_target_pairs={{0,16},{16,0},{1,17},{17,1},{2,18},{18,2},{3,19},{19,3},{4,20},{20... | collective-permute-start | bytes 73736 | tf_op jit(solution)/shard_map/ppermute | solution.py:246
  65.3 4.6 %collective-permute-start.12 = (bf16[2,2,16,32,128]{4,3,2,1,0:T(8,128)(2,1)S(1)}, bf16[2,2,16,32,128]{4,3,2,1,0:T(8,128)(2,1)S(1)}, u32[]{:S(2)}, u32[]{:S(2)}) collective-permute-start(bf16[2,2,16,32,128]{4,3,2,1,0:T(8,128)(2,1)S(1)} %get-tuple-element.35), channel_id=1, source_target_pairs={{0,16},{16,0},{1,17},{17,1},{2,18},{18,2},{3,19},{19,3},{4,20},{20... | collective-permute-start | bytes 1572872 | tf_op jit(solution)/shard_map/ppermute | solution.py:257
  66.0 9.6 %collective-permute-start.9 = (bf16[2,512,128]{2,1,0:T(8,128)(2,1)S(1)}, bf16[2,512,128]{2,1,0:T(8,128)(2,1)S(1)}, u32[]{:S(2)}, u32[]{:S(2)}) collective-permute-start(bf16[2,512,128]{2,1,0:T(8,128)(2,1)S(1)} %pad_maximum_fusion), channel_id=1, source_target_pairs={{0,8},{4,12},{8,0},{12,4},{1,9},{5,13},{9,1},{13,5},{2,10},{6,14},... | collective-permute-start | bytes 786440 | tf_op jit(solution)/shard_map/ppermute | solution.py:203
  68.8 12.4 %collective-permute-start.10 = (bf16[2,512,128]{2,1,0:T(8,128)(2,1)S(1)}, bf16[2,512,128]{2,1,0:T(8,128)(2,1)S(1)}, u32[]{:S(2)}, u32[]{:S(2)}) collective-permute-start(bf16[2,512,128]{2,1,0:T(8,128)(2,1)S(1)} %pad_maximum_fusion.1), channel_id=1, source_target_pairs={{0,4},{4,0},{8,12},{12,8},{1,5},{5,1},{9,13},{13,9},{2,6},{6,2},{1... | collective-permute-start | bytes 786440 | tf_op jit(solution)/shard_map/ppermute | solution.py:203
  69.2 12.2 %collective-permute-start.11 = (bf16[2,512,128]{2,1,0:T(8,128)(2,1)S(1)}, bf16[2,512,128]{2,1,0:T(8,128)(2,1)S(1)}, u32[]{:S(2)}, u32[]{:S(2)}) collective-permute-start(bf16[2,512,128]{2,1,0:T(8,128)(2,1)S(1)} %pad_maximum_fusion.2), channel_id=1, source_target_pairs={{0,12},{4,8},{8,4},{12,0},{1,13},{5,9},{9,5},{13,1},{2,14},{6,10},... | collective-permute-start | bytes 786440 | tf_op jit(solution)/shard_map/ppermute | solution.py:203
  70.0 11.4 %collective-permute-start.13 = (bf16[2,16,32,128]{3,2,1,0:T(8,128)(2,1)S(1)}, bf16[2,16,32,128]{3,2,1,0:T(8,128)(2,1)S(1)}, u32[]{:S(2)}, u32[]{:S(2)}) collective-permute-start(bf16[2,16,32,128]{3,2,1,0:T(8,128)(2,1)S(1)} %get-tuple-element.37), channel_id=1, source_target_pairs={{0,2},{2,0},{1,3},{3,1},{4,6},{6,4},{5,7},{7,5},{8,10},{10,8},{9,1... | collective-permute-start | bytes 786440 | tf_op jit(solution)/shard_map/ppermute | solution.py:258

commit v6 on v5

--- a/solution.py
+++ b/solution.py
@@ -330,10 +330,15 @@
     )(*arrays)
 
 
-def unpack_kernel(src_ref, *outs):
-    for n, out in enumerate(outs):
+def unpack_kernel(src_ref, *refs):
+    outs, held, sems = refs[0:4], refs[4], refs[5]
+    copies = [pltpu.make_async_copy(held.at[n], outs[n], sems.at[n]) for n in range(4)]
+    for n, copy in enumerate(copies):
         for h in range(16):
-            out[:, h * DH:(h + 1) * DH] = src_ref[h, n]
+            held[n, :, h * DH:(h + 1) * DH] = src_ref[h, n]
+        copy.start()
+    for copy in copies:
+        copy.wait()
 
 
 def unpack(a):
@@ -342,7 +347,11 @@
         unpack_kernel,
         out_shape=(rows,) * 4,
         in_specs=[VM],
-        out_specs=(VM,) * 4,
+        out_specs=(pl.BlockSpec(memory_space=pl.ANY),) * 4,
+        scratch_shapes=[
+            pltpu.VMEM((4, 32, 16 * DH), jnp.bfloat16),
+            pltpu.SemaphoreType.DMA((4,)),
+        ],
         compiler_params=PARAMS,
         name="unpack",
     )(a)

time: 102 us -> 102 us (level)
  no operation moved by 1% of the time
where the time goes in v6:
time: 102 us; the launch traced here: 100 us
  starting transfers between devices  31.8 us (31%)
  waiting for transfers between devices  29 us (28%)
  Pallas kernels  17.9 us (18%)
  blocking collectives  17.6 us (17%)
  other arithmetic  1.67 us (2%)
  local copies, waits for them, and re-layouts  1.36 us (1%)
    all_to_all x1, blocking collectives, per_device(): lax.all_to_all(send, HEADS, split_axis=0, concat_axis=0, tiled=True)  17.6 us
    ppermute x6, waiting for transfers between devices, swap(): return lax.ppermute(a, 'x', [(i, i ^ j) for i in range(4)])  16 us
    all_to_all x1, waiting for transfers between devices, per_device(): got = lax.all_to_all(packed, HEADS, split_axis=0, concat_axis=0, tiled=True)  10.9 us
    all_to_all x1, starting transfers between devices, per_device(): got = lax.all_to_all(packed, HEADS, split_axis=0, concat_axis=0, tiled=True)  10.1 us
    pallas_call x1, Pallas kernels, run_grads(): pl.pallas_call(grad_kernel, out_shape=(side, side, keys, keys), in_specs=...  8.83 us
    ppermute x6, starting transfers between devices, swap(): return lax.ppermute(a, 'x', [(i, i ^ j) for i in range(4)])  7.45 us
    pallas_call x2, Pallas kernels, run_stats(): pl.pallas_call(stats_kernel, out_shape=out_shape, in_specs=[VM] * 7 if be...  5.98 us
    ppermute x1, starting transfers between devices, per_device(): lax.ppermute(qg_own, 'core', SWAP)  3.2 us
  transfers between devices with their start and end apart: 15, of which 9 were waited for; matrix products, arithmetic and copies ran while one was open for 3% of the time, Pallas kernels for 3%

profile of v6, /device:TPU:1, one launch (start us, length us, event | category | flops | bytes accessed | tf_op | source)
XLA Modules:
  0.0 100.2 jit_solution(5557099880914580708)
XLA Ops:
  0.6 0.0 copy-start
  0.6 2.0 %pack.1 = bf16[16,4,32,128]{3,2,1,0:T(8,128)(2,1)} custom-call(bf16[32,2048]{1,0:T(8,128)(2,1)} %refs_0_.1, bf16[32,2048]{1,0:T(8,128)(2,1)} %refs_1_.1, bf16[32,2048]{1,0:T(8,128)(2,1)} %refs_2_.1, bf16[32,2048]{1,0:T(8,128)(2,1)} %refs_3_.1), custom_call_target="tpu_custom_call" | custom-call | tf_op jit(solution)/shard_map/pack/pallas_call | solution.py:319
  2.7 10.1 %all-to-all-start = ((bf16[16,4,32,128]{3,2,1,0:T(8,128)(2,1)}), bf16[16,4,32,128]{3,2,1,0:T(8,128)(2,1)S(1)}, u32[]{:S(2)}, u32[]{:S(2)}) async-start(bf16[16,4,32,128]{3,2,1,0:T(8,128)(2,1)} %pack.1), calls=%async_computation | async-start | bytes 1048576 | tf_op jit(solution)/shard_map/all_to_all | solution.py:227
  12.8 0.7 multiply_add_fusion
  13.5 0.1 broadcast_add_fusion
  13.6 0.1 add.46
  13.6 0.1 constant_dynamic-slice_fusion
  13.8 0.1 copy.14
  13.8 0.8 dynamic-slice_bitcast_fusion
  14.6 0.1 select_bitcast_fusion
  14.7 0.7 compare_reduce_fusion
  15.4 0.1 broadcast_in_dim.22
  15.5 0.1 copy.17
  15.6 10.9 %all-to-all-done = bf16[16,4,32,128]{3,2,1,0:T(8,128)(2,1)S(1)} async-done(((bf16[16,4,32,128]{3,2,1,0:T(8,128)(2,1)}), bf16[16,4,32,128]{3,2,1,0:T(8,128)(2,1)S(1)}, u32[]{:S(2)}, u32[]{:S(2)}) %all-to-all-start) | async-done | bytes 524320 | tf_op jit(solution)/shard_map/all_to_all | solution.py:227
  26.6 2.7 %collective-permute-start.4 = (bf16[16,2,32,128]{3,2,1,0:T(8,128)(2,1)S(1)}, bf16[16,2,32,128]{3,2,1,0:T(8,128)(2,1)S(1)}, u32[]{:S(2)}, u32[]{:S(2)}) collective-permute-start(bf16[16,2,32,128]{3,2,1,0:T(8,128)(2,1)S(1)} %get-tuple-element.44.refs_1_), channel_id=1, source_target_pairs={{0,2},{2,0},{1,3},{3,1},{4,6},{6,4},{5,7},{7,5},{8,10},{10,8},{9,1... | collective-permute-start | bytes 786440 | tf_op jit(solution)/shard_map/ppermute | solution.py:231
  29.3 0.1 pad_add_fusion.refs_0_
  29.4 3.2 %collective-permute-start.3 = (bf16[16,2,32,128]{3,2,1,0:T(8,128)(2,1)S(1)}, bf16[16,2,32,128]{3,2,1,0:T(8,128)(2,1)S(1)}, u32[]{:S(2)}, u32[]{:S(2)}) collective-permute-start(bf16[16,2,32,128]{3,2,1,0:T(8,128)(2,1)S(1)} %get-tuple-element.44.refs_1_), channel_id=1, source_target_pairs={{0,16},{16,0},{1,17},{17,1},{2,18},{18,2},{3,19},{19,3},{4,20},{20... | collective-permute-start | bytes 786440 | tf_op jit(solution)/shard_map/ppermute | solution.py:234
  32.6 2.8 %collective-permute-start.2 = (bf16[16,2,32,128]{3,2,1,0:T(8,128)(2,1)S(1)}, bf16[16,2,32,128]{3,2,1,0:T(8,128)(2,1)S(1)}, u32[]{:S(2)}, u32[]{:S(2)}) collective-permute-start(bf16[16,2,32,128]{3,2,1,0:T(8,128)(2,1)S(1)} %get-tuple-element.45.refs_5_.refs_1_), channel_id=1, source_target_pairs={{0,8},{4,12},{8,0},{12,4},{1,9},{5,13},{9,1},{13,5},{2,10},{6,14},... | collective-permute-start | bytes 786440 | tf_op jit(solution)/shard_map/ppermute | solution.py:203
  35.3 0.3 collective-permute-start.1
  35.7 0.6 collective-permute-start
  36.2 1.3 %collective-permute-start.5 = (bf16[16,2,32,128]{3,2,1,0:T(8,128)(2,1)S(1)}, bf16[16,2,32,128]{3,2,1,0:T(8,128)(2,1)S(1)}, u32[]{:S(2)}, u32[]{:S(2)}) collective-permute-start(bf16[16,2,32,128]{3,2,1,0:T(8,128)(2,1)S(1)} %collective-permute-done.4.refs_3_), channel_id=1, source_target_pairs={{0,16},{16,0},{1,17},{17,1},{2,18},{18,2},{3,19},{19,3},{4,20},{20... | collective-permute-start | bytes 786440 | tf_op jit(solution)/shard_map/ppermute | solution.py:236
  37.5 4.5 %collective-permute-done.2.refs_6_.refs_4_ = bf16[16,2,32,128]{3,2,1,0:T(8,128)(2,1)S(1)} collective-permute-done((bf16[16,2,32,128]{3,2,1,0:T(8,128)(2,1)S(1)}, bf16[16,2,32,128]{3,2,1,0:T(8,128)(2,1)S(1)}, u32[]{:S(2)}, u32[]{:S(2)}) %collective-permute-start.2) | collective-permute-done | bytes 262176 | tf_op jit(solution)/shard_map/ppermute | solution.py:203
  42.0 0.0 collective-permute-done.5.refs_4_
  42.0 3.2 %stats_near.1 = (f32[3,8,256]{2,1,0:T(8,128)S(1)}, f32[128,2048]{1,0:T(8,128)S(1)}, bf16[1024,2048]{1,0:T(8,128)(2,1)S(1)}, bf16[2,16,2,32,128]{4,3,2,1,0:T(8,128)(2,1)S(1)}, bf16[2,16,2,32,128]{4,3,2,1,0:T(8,128)(2,1)S(1)}) custom-call(s32[2]{0:T(128)S(1)} %pad_add_fusion.refs_0_, bf16[16,2,32,128]{3,2,1,0:T(8,128)(2,1)S(1)} %get-tuple-element.44.refs_1_, ...), custom_call_target="tpu_custom_call" | custom-call | tf_op jit(solution)/shard_map/stats_near/pallas_call | solution.py:169
  45.2 2.5 %collective-permute-done.1.refs_3_ = bf16[16,2,32,128]{3,2,1,0:T(8,128)(2,1)S(1)} collective-permute-done((bf16[16,2,32,128]{3,2,1,0:T(8,128)(2,1)S(1)}, bf16[16,2,32,128]{3,2,1,0:T(8,128)(2,1)S(1)}, u32[]{:S(2)}, u32[]{:S(2)}) %collective-permute-start.1) | collective-permute-done | bytes 262176 | tf_op jit(solution)/shard_map/ppermute | solution.py:203
  47.7 0.2 collective-permute-done.refs_2_
  47.9 2.8 %stats_far.1 = (f32[3,8,256]{2,1,0:T(8,128)S(1)}, f32[128,2048]{1,0:T(8,128)S(1)}, bf16[1024,2048]{1,0:T(8,128)(2,1)S(1)}, f32[2,8,256]{2,1,0:T(8,128)S(1)}) custom-call(bf16[2,16,2,32,128]{4,3,2,1,0:T(8,128)(2,1)S(1)} %get-tuple-element.23.refs_0_.refs_5_, bf16[2,16,2,32,128]{4,3,2,1,0:T(8,128)(2,1)S(1)} %get-tuple-element.24.refs_1_.refs_6_, ...), custom_call_target="tpu_custom_call" | custom-call | tf_op jit(solution)/shard_map/stats_far/pallas_call | solution.py:169
  50.8 0.9 collective-permute-start.8
  51.7 2.6 %collective-permute-start.7 = (f32[3,8,256]{2,1,0:T(8,128)S(1)}, f32[3,8,256]{2,1,0:T(8,128)S(1)}, u32[]{:S(2)}, u32[]{:S(2)}) collective-permute-start(f32[3,8,256]{2,1,0:T(8,128)S(1)} %get-tuple-element.31.refs_11_), channel_id=1, source_target_pairs={{0,2},{2,0},{1,3},{3,1},{4,6},{6,4},{5,7},{7,5},{8,10},{10,8},{9,1... | collective-permute-start | bytes 73736 | tf_op jit(solution)/shard_map/ppermute | solution.py:247
  54.3 0.2 collective-permute-start.6
  54.5 1.5 %collective-permute-done.8.refs_14_ = f32[3,8,256]{2,1,0:T(8,128)S(1)} collective-permute-done((f32[3,8,256]{2,1,0:T(8,128)S(1)}, f32[3,8,256]{2,1,0:T(8,128)S(1)}, u32[]{:S(2)}, u32[]{:S(2)}) %collective-permute-start.8) | collective-permute-done | bytes 24608 | tf_op jit(solution)/shard_map/ppermute | solution.py:248
  56.0 0.5 collective-permute-done.7.refs_13_
  56.5 0.0 collective-permute-done.6.refs_12_
  56.5 8.8 %grads.1 = (bf16[2,2,16,32,128]{4,3,2,1,0:T(8,128)(2,1)S(1)}, bf16[2,2,16,32,128]{4,3,2,1,0:T(8,128)(2,1)S(1)}, bf16[2048,128]{1,0:T(8,128)(2,1)S(1)}, bf16[2048,128]{1,0:T(8,128)(2,1)S(1)}) custom-call(s32[2]{0:T(128)S(1)} %pad_add_fusion.refs_0_, bf16[16,2,32,128]{3,2,1,0:T(8,128)(2,1)S(1)} %get-tuple-element.45.refs_5_.refs_1_, ...), custom_call_target="tpu_custom_call" | custom-call | tf_op jit(solution)/shard_map/grads/pallas_call | solution.py:188
  65.3 0.6 collective-permute-start.12
  65.9 0.1 slice_bitcast_fusion
  66.0 2.7 %collective-permute-start.9 = (bf16[2,512,128]{2,1,0:T(8,128)(2,1)S(1)}, bf16[2,512,128]{2,1,0:T(8,128)(2,1)S(1)}, u32[]{:S(2)}, u32[]{:S(2)}) collective-permute-start(bf16[2,512,128]{2,1,0:T(8,128)(2,1)S(1)} %pad_maximum_fusion), channel_id=1, source_target_pairs={{0,8},{4,12},{8,0},{12,4},{1,9},{5,13},{9,1},{13,5},{2,10},{6,14},... | collective-permute-start | bytes 786440 | tf_op jit(solution)/shard_map/ppermute | solution.py:203
  68.8 0.4 collective-permute-start.10
  69.2 0.7 collective-permute-start.11
  69.9 0.1 add_core.1
  70.0 2.7 %collective-permute-start.13 = (bf16[2,16,32,128]{3,2,1,0:T(8,128)(2,1)S(1)}, bf16[2,16,32,128]{3,2,1,0:T(8,128)(2,1)S(1)}, u32[]{:S(2)}, u32[]{:S(2)}) collective-permute-start(bf16[2,16,32,128]{3,2,1,0:T(8,128)(2,1)S(1)} %get-tuple-element.37), channel_id=1, source_target_pairs={{0,2},{2,0},{1,3},{3,1},{4,6},{6,4},{5,7},{7,5},{8,10},{10,8},{9,1... | collective-permute-start | bytes 786440 | tf_op jit(solution)/shard_map/ppermute | solution.py:258
  72.7 2.9 %collective-permute-done.9.refs_0_ = bf16[2,512,128]{2,1,0:T(8,128)(2,1)S(1)} collective-permute-done((bf16[2,512,128]{2,1,0:T(8,128)(2,1)S(1)}, bf16[2,512,128]{2,1,0:T(8,128)(2,1)S(1)}, u32[]{:S(2)}, u32[]{:S(2)}) %collective-permute-start.9) | collective-permute-done | bytes 262176 | tf_op jit(solution)/shard_map/ppermute | solution.py:203
  75.6 5.6 %collective-permute-done.10.refs_1_ = bf16[2,512,128]{2,1,0:T(8,128)(2,1)S(1)} collective-permute-done((bf16[2,512,128]{2,1,0:T(8,128)(2,1)S(1)}, bf16[2,512,128]{2,1,0:T(8,128)(2,1)S(1)}, u32[]{:S(2)}, u32[]{:S(2)}) %collective-permute-start.10) | collective-permute-done | bytes 262176 | tf_op jit(solution)/shard_map/ppermute | solution.py:203
  81.2 0.3 collective-permute-done.11.refs_2_
  81.5 0.0 collective-permute-done.13.refs_4_
  81.5 0.2 add_up.1
  81.6 17.6 %all_to_all.10.src_ref = bf16[16,4,32,128]{3,2,1,0:T(8,128)(2,1)S(1)} all-to-all(bf16[16,4,32,128]{3,2,1,0:T(8,128)(2,1)S(1)} %add_up.1), channel_id=1, replica_groups=mesh['z'=8,'core'=2,'x'=4,'y1'=2,'y0'=2] {'y0','z'}, dimensions={0} | all-to-all | bytes 1048576 | tf_op jit(solution)/shard_map/all_to_all | solution.py:259
  99.2 0.8 unpack.1
  (11 shorter events, 0.2 us)
Async XLA Ops:
  0.6 13.0 %copy-start = (s32[16,64,38]{1,0,2:T(8,128)S(1)}, s32[16,64,38]{1,0,2:T(8,128)}, u32[]{:S(2)}) copy-start(s32[16,64,38]{1,0,2:T(8,128)} %param.11) | copy-start | bytes 466948
  2.7 23.9 %all-to-all-start = ((bf16[16,4,32,128]{3,2,1,0:T(8,128)(2,1)}), bf16[16,4,32,128]{3,2,1,0:T(8,128)(2,1)S(1)}, u32[]{:S(2)}, u32[]{:S(2)}) async-start(bf16[16,4,32,128]{3,2,1,0:T(8,128)(2,1)} %pack.1), calls=%async_computation | async-start | bytes 1048576 | tf_op jit(solution)/shard_map/all_to_all | solution.py:227
  26.6 9.6 %collective-permute-start.4 = (bf16[16,2,32,128]{3,2,1,0:T(8,128)(2,1)S(1)}, bf16[16,2,32,128]{3,2,1,0:T(8,128)(2,1)S(1)}, u32[]{:S(2)}, u32[]{:S(2)}) collective-permute-start(bf16[16,2,32,128]{3,2,1,0:T(8,128)(2,1)S(1)} %get-tuple-element.44.refs_1_), channel_id=1, source_target_pairs={{0,2},{2,0},{1,3},{3,1},{4,6},{6,4},{5,7},{7,5},{8,10},{10,8},{9,1... | collective-permute-start | bytes 786440 | tf_op jit(solution)/shard_map/ppermute | solution.py:231
  29.4 8.1 %collective-permute-start.3 = (bf16[16,2,32,128]{3,2,1,0:T(8,128)(2,1)S(1)}, bf16[16,2,32,128]{3,2,1,0:T(8,128)(2,1)S(1)}, u32[]{:S(2)}, u32[]{:S(2)}) collective-permute-start(bf16[16,2,32,128]{3,2,1,0:T(8,128)(2,1)S(1)} %get-tuple-element.44.refs_1_), channel_id=1, source_target_pairs={{0,16},{16,0},{1,17},{17,1},{2,18},{18,2},{3,19},{19,3},{4,20},{20... | collective-permute-start | bytes 786440 | tf_op jit(solution)/shard_map/ppermute | solution.py:234
  32.6 9.4 %collective-permute-start.2 = (bf16[16,2,32,128]{3,2,1,0:T(8,128)(2,1)S(1)}, bf16[16,2,32,128]{3,2,1,0:T(8,128)(2,1)S(1)}, u32[]{:S(2)}, u32[]{:S(2)}) collective-permute-start(bf16[16,2,32,128]{3,2,1,0:T(8,128)(2,1)S(1)} %get-tuple-element.45.refs_5_.refs_1_), channel_id=1, source_target_pairs={{0,8},{4,12},{8,0},{12,4},{1,9},{5,13},{9,1},{13,5},{2,10},{6,14},... | collective-permute-start | bytes 786440 | tf_op jit(solution)/shard_map/ppermute | solution.py:203
  35.3 12.4 %collective-permute-start.1 = (bf16[16,2,32,128]{3,2,1,0:T(8,128)(2,1)S(1)}, bf16[16,2,32,128]{3,2,1,0:T(8,128)(2,1)S(1)}, u32[]{:S(2)}, u32[]{:S(2)}) collective-permute-start(bf16[16,2,32,128]{3,2,1,0:T(8,128)(2,1)S(1)} %get-tuple-element.45.refs_5_.refs_1_), channel_id=1, source_target_pairs={{0,4},{4,0},{8,12},{12,8},{1,5},{5,1},{9,13},{13,9},{2,6},{6,2},{1... | collective-permute-start | bytes 786440 | tf_op jit(solution)/shard_map/ppermute | solution.py:203
  35.7 12.3 %collective-permute-start = (bf16[16,2,32,128]{3,2,1,0:T(8,128)(2,1)S(1)}, bf16[16,2,32,128]{3,2,1,0:T(8,128)(2,1)S(1)}, u32[]{:S(2)}, u32[]{:S(2)}) collective-permute-start(bf16[16,2,32,128]{3,2,1,0:T(8,128)(2,1)S(1)} %get-tuple-element.45.refs_5_.refs_1_), channel_id=1, source_target_pairs={{0,12},{4,8},{8,4},{12,0},{1,13},{5,9},{9,5},{13,1},{2,14},{6,10},... | collective-permute-start | bytes 786440 | tf_op jit(solution)/shard_map/ppermute | solution.py:203
  36.2 5.8 %collective-permute-start.5 = (bf16[16,2,32,128]{3,2,1,0:T(8,128)(2,1)S(1)}, bf16[16,2,32,128]{3,2,1,0:T(8,128)(2,1)S(1)}, u32[]{:S(2)}, u32[]{:S(2)}) collective-permute-start(bf16[16,2,32,128]{3,2,1,0:T(8,128)(2,1)S(1)} %collective-permute-done.4.refs_3_), channel_id=1, source_target_pairs={{0,16},{16,0},{1,17},{17,1},{2,18},{18,2},{3,19},{19,3},{4,20},{20... | collective-permute-start | bytes 786440 | tf_op jit(solution)/shard_map/ppermute | solution.py:236
  50.8 5.3 %collective-permute-start.8 = (f32[3,8,256]{2,1,0:T(8,128)S(1)}, f32[3,8,256]{2,1,0:T(8,128)S(1)}, u32[]{:S(2)}, u32[]{:S(2)}) collective-permute-start(f32[3,8,256]{2,1,0:T(8,128)S(1)} %get-tuple-element.31.refs_11_), channel_id=1, source_target_pairs={{0,18},{2,16},{16,2},{18,0},{1,19},{3,17},{17,3},{19,1},{4,22},{6,... | collective-permute-start | bytes 73736 | tf_op jit(solution)/shard_map/ppermute | solution.py:248
  51.7 4.8 %collective-permute-start.7 = (f32[3,8,256]{2,1,0:T(8,128)S(1)}, f32[3,8,256]{2,1,0:T(8,128)S(1)}, u32[]{:S(2)}, u32[]{:S(2)}) collective-permute-start(f32[3,8,256]{2,1,0:T(8,128)S(1)} %get-tuple-element.31.refs_11_), channel_id=1, source_target_pairs={{0,2},{2,0},{1,3},{3,1},{4,6},{6,4},{5,7},{7,5},{8,10},{10,8},{9,1... | collective-permute-start | bytes 73736 | tf_op jit(solution)/shard_map/ppermute | solution.py:247
  54.3 2.2 %collective-permute-start.6 = (f32[3,8,256]{2,1,0:T(8,128)S(1)}, f32[3,8,256]{2,1,0:T(8,128)S(1)}, u32[]{:S(2)}, u32[]{:S(2)}) collective-permute-start(f32[3,8,256]{2,1,0:T(8,128)S(1)} %get-tuple-element.31.refs_11_), channel_id=1, source_target_pairs={{0,16},{16,0},{1,17},{17,1},{2,18},{18,2},{3,19},{19,3},{4,20},{20... | collective-permute-start | bytes 73736 | tf_op jit(solution)/shard_map/ppermute | solution.py:246
  65.3 4.6 %collective-permute-start.12 = (bf16[2,2,16,32,128]{4,3,2,1,0:T(8,128)(2,1)S(1)}, bf16[2,2,16,32,128]{4,3,2,1,0:T(8,128)(2,1)S(1)}, u32[]{:S(2)}, u32[]{:S(2)}) collective-permute-start(bf16[2,2,16,32,128]{4,3,2,1,0:T(8,128)(2,1)S(1)} %get-tuple-element.35), channel_id=1, source_target_pairs={{0,16},{16,0},{1,17},{17,1},{2,18},{18,2},{3,19},{19,3},{4,20},{20... | collective-permute-start | bytes 1572872 | tf_op jit(solution)/shard_map/ppermute | solution.py:257
  66.0 9.6 %collective-permute-start.9 = (bf16[2,512,128]{2,1,0:T(8,128)(2,1)S(1)}, bf16[2,512,128]{2,1,0:T(8,128)(2,1)S(1)}, u32[]{:S(2)}, u32[]{:S(2)}) collective-permute-start(bf16[2,512,128]{2,1,0:T(8,128)(2,1)S(1)} %pad_maximum_fusion), channel_id=1, source_target_pairs={{0,8},{4,12},{8,0},{12,4},{1,9},{5,13},{9,1},{13,5},{2,10},{6,14},... | collective-permute-start | bytes 786440 | tf_op jit(solution)/shard_map/ppermute | solution.py:203
  68.8 12.4 %collective-permute-start.10 = (bf16[2,512,128]{2,1,0:T(8,128)(2,1)S(1)}, bf16[2,512,128]{2,1,0:T(8,128)(2,1)S(1)}, u32[]{:S(2)}, u32[]{:S(2)}) collective-permute-start(bf16[2,512,128]{2,1,0:T(8,128)(2,1)S(1)} %pad_maximum_fusion.1), channel_id=1, source_target_pairs={{0,4},{4,0},{8,12},{12,8},{1,5},{5,1},{9,13},{13,9},{2,6},{6,2},{1... | collective-permute-start | bytes 786440 | tf_op jit(solution)/shard_map/ppermute | solution.py:203
  69.2 12.2 %collective-permute-start.11 = (bf16[2,512,128]{2,1,0:T(8,128)(2,1)S(1)}, bf16[2,512,128]{2,1,0:T(8,128)(2,1)S(1)}, u32[]{:S(2)}, u32[]{:S(2)}) collective-permute-start(bf16[2,512,128]{2,1,0:T(8,128)(2,1)S(1)} %pad_maximum_fusion.2), channel_id=1, source_target_pairs={{0,12},{4,8},{8,4},{12,0},{1,13},{5,9},{9,5},{13,1},{2,14},{6,10},... | collective-permute-start | bytes 786440 | tf_op jit(solution)/shard_map/ppermute | solution.py:203
  70.0 11.4 %collective-permute-start.13 = (bf16[2,16,32,128]{3,2,1,0:T(8,128)(2,1)S(1)}, bf16[2,16,32,128]{3,2,1,0:T(8,128)(2,1)S(1)}, u32[]{:S(2)}, u32[]{:S(2)}) collective-permute-start(bf16[2,16,32,128]{3,2,1,0:T(8,128)(2,1)S(1)} %get-tuple-element.37), channel_id=1, source_target_pairs={{0,2},{2,0},{1,3},{3,1},{4,6},{6,4},{5,7},{7,5},{8,10},{10,8},{9,1... | collective-permute-start | bytes 786440 | tf_op jit(solution)/shard_map/ppermute | solution.py:258
